TPU v7x, 128 devices: a whole 4x4x4 slice. The times are simulated.
128 devices in a mesh: gx: 16 (over y, z), gy: 8 (over x, core).
Axes of the slice: x: 4, y: 4, z: 4, core: 2. Of those that a mesh axis runs over, the one named last changes fastest.
Arguments:
- starting_wetness: float32 [32, 1024, 1024], P(None, 'gx', 'gy'), may hold values from 0.05 to 0.95
- surface_inflow: float32 [1024, 1024], P('gx', 'gy'), may hold values from 0 to 0.2
- category_permeability: float32 [12], replicated, may hold values from 0.01 to 0.09
- earth_category: int32 [1024, 1024], P('gx', 'gy'), may hold values from 0 to 11
- thermal_state: float32 [1024, 1024], P('gx', 'gy'), may hold values from 0.8 to 1.2
- sensor_patch_coefficients: bfloat16 [4096, 4, 128, 128], P(('gx', 'gy')), may hold values from -0.25 to 0.25
- patch_device_slot: int32 [4096, 4], P(('gx', 'gy')), may hold values from 0 to 127, all different within a row; in each aligned block of 32 rows (0 to 31, 32 to 63, ...) at most 4 rows name the same one
- patch_strip_number: int32 [4096, 4], P(('gx', 'gy')), may hold values from 0 to 63
- measured_radiance: float32 [4096, 128], P(('gx', 'gy')), may hold values from -6 to 6
Outputs:
- moisture: float32 [32, 1024, 1024], P(None, 'gx', 'gy')
- brightness: float32 [4096, 128], P(('gx', 'gy'))
- grad_top: float32 [2, 1024, 1024], P(None, 'gx', 'gy')
Inputs may be any that keep to these rules, and one draw needn't show every extreme that they name: `patch_device_slot`: each footprint block names 4 different tiles; the footprint blocks of one device name one tile at most 4 times, and exactly 4 times on some device.
All inputs are finite; a program needn't handle non-finite values.
Results may differ from a plain program's by a relative error of at most 0.0032.
Values may be sent and summed in bfloat16 or wider, within the bound.
No kernel may reach another device: no remote copies, remote signals or barrier semaphores. Data moves between devices by JAX's collectives and lax.ppermute only.
A program may use at most 64 MiB of HBM per device.

v0:
```python
import jax
import jax.numpy as jnp
from jax import lax
from jax.sharding import PartitionSpec as P

CAP = 4
STEPS = 4


def with_halo(cells, sides, width):
    for axis, dim in sides:
        count = lax.axis_size(axis)
        ends = count - 1
        head = lax.slice_in_dim(cells, 0, width, axis=dim)
        tail = lax.slice_in_dim(cells, cells.shape[dim] - width, cells.shape[dim], axis=dim)
        cells = jnp.concatenate(
            [
                lax.ppermute(tail, axis, [(i, (i + 1) % count) for i in range(ends)]),
                cells,
                lax.ppermute(head, axis, [((i + 1) % count, i) for i in range(ends)]),
            ],
            axis=dim,
        )
    return cells


def trimmed_step(state, conduct_col, inside):
    conduct = conduct_col[None] * (0.5 + state)
    middle = state[:, 1:-1, 1:-1]
    conduct_mid = conduct[:, 1:-1, 1:-1]
    change = jnp.zeros_like(middle)
    for near_s, near_k in (
        (state[:, 2:, 1:-1], conduct[:, 2:, 1:-1]),
        (state[:, :-2, 1:-1], conduct[:, :-2, 1:-1]),
        (state[:, 1:-1, 2:], conduct[:, 1:-1, 2:]),
        (state[:, 1:-1, :-2], conduct[:, 1:-1, :-2]),
    ):
        change = change + 0.5 * (conduct_mid + near_k) * (near_s - middle)
    flux_down = 0.5 * (conduct_mid[:-1] + conduct_mid[1:]) * (middle[:-1] - middle[1:] + 0.3)
    change = (
        change
        + jnp.pad(-flux_down, ((0, 1), (0, 0), (0, 0)))
        + jnp.pad(flux_down, ((1, 0), (0, 0), (0, 0)))
    )
    inner = inside[1:-1, 1:-1]
    return ((middle + change) * inner[None], conduct_col[1:-1, 1:-1], inner)


def on_device(
    starting_wetness,
    surface_inflow,
    category_permeability,
    earth_category,
    thermal_state,
    sensor_patch_coefficients,
    patch_device_slot,
    patch_strip_number,
    measured_radiance,
):
    classes = jnp.arange(category_permeability.shape[0], dtype=jnp.int32)
    conduct_col = jnp.sum(
        jnp.where(
            earth_category[None] == classes[:, None, None],
            category_permeability[:, None, None],
            jnp.float32(0.0),
        ),
        axis=0,
    )
    state = starting_wetness.at[0].add(surface_inflow)
    tile_rows = state.shape[1]
    block_len = state.shape[2]
    rows_x = lax.axis_size("gx")
    rows_y = lax.axis_size("gy")
    stacked = jnp.concatenate([state, conduct_col[None]], axis=0)
    padded = with_halo(stacked, (("gx", 1), ("gy", 2)), STEPS)
    grid_rows = (
        lax.axis_index("gx") * tile_rows
        + jnp.arange(tile_rows + 2 * STEPS, dtype=jnp.int32)
        - STEPS
    )
    grid_cols = (
        lax.axis_index("gy") * block_len
        + jnp.arange(block_len + 2 * STEPS, dtype=jnp.int32)
        - STEPS
    )
    row_ok = (grid_rows >= 0) & (grid_rows < tile_rows * rows_x)
    col_ok = (grid_cols >= 0) & (grid_cols < block_len * rows_y)
    inside = (row_ok[:, None] & col_ok[None]).astype(jnp.float32)
    state = padded[:-1]
    wide_conduct = padded[-1]
    for step in range(STEPS):
        state, wide_conduct, inside = trimmed_step(state, wide_conduct, inside)
    combined_average = 0.6 * state[0] + 0.4 * state[1]
    radiance_map = (thermal_state * (1.0 - 0.4 * combined_average * combined_average)).astype(
        jnp.bfloat16
    )
    ndev = rows_x * rows_y
    blocks_own = sensor_patch_coefficients.shape[0]
    touches = sensor_patch_coefficients.shape[1]
    tile_ids = patch_device_slot.reshape(-1)
    row_ids = patch_strip_number.reshape(-1)
    refs = tile_ids.shape[0]
    dest_onehot = (tile_ids[:, None] == jnp.arange(ndev, dtype=jnp.int32)[None]).astype(jnp.float32)
    earlier_mask = (jnp.arange(refs)[:, None] > jnp.arange(refs)[None]).astype(jnp.float32)
    earlier = jnp.dot(earlier_mask, dest_onehot, precision=lax.Precision.HIGHEST)
    slot_ids = jnp.sum(earlier * dest_onehot, axis=1).astype(jnp.int32)
    position = tile_ids * CAP + slot_ids
    placing = position[:, None] == jnp.arange(ndev * CAP, dtype=jnp.int32)[None]
    request = jnp.sum(jnp.where(placing, row_ids[:, None] + 1, 0), axis=0) - 1
    incoming = lax.all_to_all(
        request.reshape(ndev, CAP), ("gx", "gy"), split_axis=0, concat_axis=0, tiled=True
    )
    picker = incoming.reshape(-1)[:, None] == jnp.arange(tile_rows, dtype=jnp.int32)[None]
    served = jnp.dot(
        picker.astype(jnp.bfloat16), radiance_map, preferred_element_type=jnp.float32
    ).astype(jnp.bfloat16)
    returned = lax.all_to_all(
        served.reshape(ndev, CAP, block_len), ("gx", "gy"), split_axis=0, concat_axis=0, tiled=True
    )
    cell_rows = jnp.dot(
        placing.astype(jnp.bfloat16),
        returned.reshape(ndev * CAP, block_len),
        preferred_element_type=jnp.float32,
    ).astype(jnp.bfloat16)
    cell_rows = cell_rows.reshape(blocks_own, touches, block_len)
    brightness = jnp.einsum(
        "bnfc,bnc->bf", sensor_patch_coefficients, cell_rows, preferred_element_type=jnp.float32
    )
    misfit = (brightness - measured_radiance).astype(jnp.bfloat16)
    contrib = jnp.einsum(
        "bnfc,bf->bnc", sensor_patch_coefficients, misfit, preferred_element_type=jnp.float32
    ).reshape(refs, block_len)
    outgoing = jnp.dot(placing.astype(jnp.float32).T, contrib, precision=lax.Precision.HIGHEST)
    returned_grads = lax.all_to_all(
        outgoing.reshape(ndev, CAP, block_len),
        ("gx", "gy"),
        split_axis=0,
        concat_axis=0,
        tiled=True,
    )
    sensitivity_by_location = jnp.dot(
        picker.astype(jnp.float32).T,
        returned_grads.reshape(ndev * CAP, block_len),
        precision=lax.Precision.HIGHEST,
    )
    common_portion = sensitivity_by_location * thermal_state * (-0.8 * combined_average)
    grad_top = jnp.stack([0.6 * common_portion, 0.4 * common_portion])
    return (state, brightness, grad_top)


def solution(mesh):
    placed = (
        P(None, "gx", "gy"),
        P("gx", "gy"),
        P(),
        P("gx", "gy"),
        P("gx", "gy"),
        P(("gx", "gy"), None, None, None),
        P(("gx", "gy"), None),
        P(("gx", "gy"), None),
        P(("gx", "gy"), None),
    )
    return jax.shard_map(
        on_device,
        mesh=mesh,
        in_specs=placed,
        out_specs=(P(None, "gx", "gy"), P(("gx", "gy"), None), P(None, "gx", "gy")),
        check_vma=False,
    )
```

profile of v0, /device:TPU:1, one launch (start us, length us, event | category | flops | bytes accessed | tf_op | source)
XLA Modules:
  0.0 109.1 jit_solution(5741692100837353079)
XLA Ops:
  0.7 1.2 %copy.43 = f32[32,64,128]{2,1,0:T(8,128)S(1)} copy(f32[32,64,128]{2,1,0:T(8,128)} %param.11) | data formatting | bytes 2097152
  1.9 0.8 fusion.89
  2.7 0.9 select_reduce_fusion
  3.6 4.4 %collective-permute-start = (f32[33,4,128]{2,1,0:T(4,128)S(1)}, f32[33,4,128]{2,1,0:T(4,128)S(1)}, u32[]{:S(2)}, u32[]{:S(2)}) collective-permute-start(f32[33,4,128]{2,1,0:T(4,128)S(1)} %get-tuple-element.31), channel_id=1, source_target_pairs={{0,8},{8,16},{16,24},{24,32},{32,40},{40,48},{48,56},{56,64},{64,7... | collective-permute-start | bytes 202760 | tf_op jit(solution)/shard_map/ppermute | solution.py:18
  8.0 1.3 %collective-permute-start.1 = (f32[33,4,128]{2,1,0:T(4,128)S(1)}, f32[33,4,128]{2,1,0:T(4,128)S(1)}, u32[]{:S(2)}, u32[]{:S(2)}) collective-permute-start(f32[33,4,128]{2,1,0:T(4,128)S(1)} %get-tuple-element.32), channel_id=1, source_target_pairs={{8,0},{16,8},{24,16},{32,24},{40,32},{48,40},{56,48},{64,56},{72,6... | collective-permute-start | bytes 202760 | tf_op jit(solution)/shard_map/ppermute | solution.py:20
  9.4 0.1 reshape.143
  9.5 0.2 fusion.55
  9.9 0.1 select_reduce_fusion.1
  10.0 0.7 sub.106
  10.7 12.1 %all-to-all-start = ((s32[128,1,4]{2,1,0:T(1,128)}), s32[128,1,4]{2,1,0:T(1,128)}, u32[]{:S(2)}, u32[]{:S(2)}) async-start(s32[128,1,4]{2,1,0:T(1,128)} %bitcast.3), calls=%async_computation | async-start | bytes 131072 | tf_op jit(solution)/shard_map/all_to_all | solution.py:110
  22.9 0.6 copy-done.2
  23.5 0.6 copy-done.4
  24.2 0.1 pad_maximum_fusion.1
  24.3 0.4 fusion.112
  24.7 1.0 copy.25
  25.7 3.5 %collective-permute-start.2 = (f32[33,72,4]{1,2,0:T(4,128)}, f32[33,72,4]{1,2,0:T(4,128)S(1)}, u32[]{:S(2)}, u32[]{:S(2)}) collective-permute-start(f32[33,72,4]{1,2,0:T(4,128)} %copy.25), channel_id=1, source_target_pairs={{0,1},{1,2},{2,3},{3,4},{4,5},{5,6},{6,7},{8,9},{9,10},{10,11},{11... | collective-permute-start | bytes 114056 | tf_op jit(solution)/shard_map/ppermute | solution.py:18
  29.3 0.4 copy.26
  29.7 1.9 %collective-permute-start.3 = (f32[33,72,4]{1,2,0:T(4,128)S(1)}, f32[33,72,4]{1,2,0:T(4,128)}, u32[]{:S(2)}, u32[]{:S(2)}) collective-permute-start(f32[33,72,4]{1,2,0:T(4,128)S(1)} %copy.26), channel_id=1, source_target_pairs={{1,0},{2,1},{3,2},{4,3},{5,4},{6,5},{7,6},{9,8},{10,9},{11,10},{12... | collective-permute-start | bytes 114056 | tf_op jit(solution)/shard_map/ppermute | solution.py:20
  31.7 0.7 slice.350
  32.4 0.7 slice.366
  33.1 0.7 slice.382
  33.9 0.5 broadcast.206
  34.4 1.6 %reduce.5 = s32[128,4]{1,0:T(8,128)S(1)} reduce(s32[128,1,4]{2,1,0:T(1,128)} %all-to-all-done, s32[]{:T(128)} %broadcast.206), dimensions={1}, to_apply=%all_to_all.10.reduce_sub_computation.3 | reduce | bytes 4100 | tf_op jit(solution)/shard_map/all_to_all | solution.py:110
  36.1 0.1 eq.82
  36.2 0.5 copy.27
  36.7 1.3 %copy.28 = f32[33,72,4]{2,1,0:T(8,128)S(1)} copy(f32[33,72,4]{1,2,0:T(4,128)} %collective-permute-done.3) | data formatting | bytes 76032 | tf_op jit(solution)/shard_map/ppermute | solution.py:20
  38.0 0.8 maximum_bitcast_fusion
  39.1 1.2 %pad_maximum_fusion = f32[33,72,136]{2,1,0:T(8,128)S(1)} fusion(f32[33,72,4]{2,1,0:T(8,128)S(1)} %copy.28, f32[33,4,128]{2,1,0:T(4,128)S(1)} %copy-done.5, f32[1,64,128]{2,1,0:T(8,128)S(1)} %bitcast.47, f32[32,64,128]{2,1,0:T(8,128)S(1)} %fusion.89, f32[33,4,128]{2,1,0:T(4,128)S(1)} %copy-done.3, f32[33,72,4]{2,1,0:T(8,128)S(1)} %copy.27), kind=kLoop, calls=%fused_computation | loop fusion | flops 1615680 | bytes 2585088 | tf_op jit(solution)/shard_map/concatenate | solution.py:16
  40.3 0.2 fusion.45
  40.5 2.4 %fusion.110 = (f32[31,70,134]{2,1,0:T(8,128)S(1)}, f32[31,70,134]{2,1,0:T(8,128)S(1)}) fusion(f32[33,72,136]{2,1,0:T(8,128)S(1)} %pad_maximum_fusion, f32[32,72,136]{2,1,0:T(8,128)S(1)} %fusion.45), kind=kLoop, calls=%fused_computation.177 | loop fusion | flops 1744680 | bytes 6978720 | tf_op jit(solution)/shard_map/neg | solution.py:42
  42.9 5.5 %add_multiply_fusion.2 = (f32[32,70,134]{2,1,0:T(8,128)S(1)}, f32[32,70,134]{2,1,0:T(8,128)S(1)}) fusion(f32[70,134]{1,0:T(8,128)S(1)} %slice.352, f32[70,134]{1,0:T(8,128)S(1)} %copy-done.8, f32[31,70,134]{2,1,0:T(8,128)S(1)} %get-tuple-element.28, f32[31,70,134]{2,1,0:T(8,128)S(1)} %get-tuple-element.27, f32[33,72,136]{2,1,0:T(8,128)S(1)} %pad_maximum_fusion, ...), kind=kLoop, calls=%fused_computation.74 | loop fusion | flops 7504000 | bytes 16808960 | tf_op jit(solution)/shard_map/mul | solution.py:28
  48.4 2.4 %fusion.107 = (f32[31,68,132]{2,1,0:T(8,128)S(1)}, f32[31,68,132]{2,1,0:T(8,128)S(1)}) fusion(f32[32,70,134]{2,1,0:T(8,128)S(1)} %get-tuple-element.26, f32[32,70,134]{2,1,0:T(8,128)S(1)} %get-tuple-element.25), kind=kLoop, calls=%fused_computation.176 | loop fusion | flops 1669536 | bytes 6678144 | tf_op jit(solution)/shard_map/neg | solution.py:42
  50.9 5.1 %add_multiply_fusion.1 = (f32[32,68,132]{2,1,0:T(8,128)S(1)}, f32[32,68,132]{2,1,0:T(8,128)S(1)}) fusion(f32[68,132]{1,0:T(8,128)S(1)} %slice.368, f32[68,132]{1,0:T(8,128)S(1)} %copy-done.7, f32[31,68,132]{2,1,0:T(8,128)S(1)} %get-tuple-element.24, f32[31,68,132]{2,1,0:T(8,128)S(1)} %get-tuple-element.23, f32[32,70,134]{2,1,0:T(8,128)S(1)} %get-tuple-element.26, ...), kind=kLoop, calls=%fused_computation.73 | loop fusion | flops 7180800 | bytes 16084992 | tf_op jit(solution)/shard_map/mul | solution.py:28
  56.0 2.4 %fusion.104 = (f32[31,66,130]{2,1,0:T(8,128)S(1)}, f32[31,66,130]{2,1,0:T(8,128)S(1)}) fusion(f32[32,68,132]{2,1,0:T(8,128)S(1)} %get-tuple-element.22, f32[32,68,132]{2,1,0:T(8,128)S(1)} %get-tuple-element.21), kind=kLoop, calls=%fused_computation.175 | loop fusion | flops 1595880 | bytes 6383520 | tf_op jit(solution)/shard_map/neg | solution.py:42
  58.4 5.3 %add_multiply_fusion = (f32[32,66,130]{2,1,0:T(8,128)S(1)}, f32[32,66,130]{2,1,0:T(8,128)S(1)}) fusion(f32[66,130]{1,0:T(8,128)S(1)} %slice.384, f32[66,130]{1,0:T(8,128)S(1)} %copy-done.6, f32[31,66,130]{2,1,0:T(8,128)S(1)} %get-tuple-element.20, f32[31,66,130]{2,1,0:T(8,128)S(1)} %get-tuple-element.19, f32[32,68,132]{2,1,0:T(8,128)S(1)} %get-tuple-element.22, ...), kind=kLoop, calls=%fused_computation.72 | loop fusion | flops 6864000 | bytes 15375360 | tf_op jit(solution)/shard_map/mul | solution.py:28
  63.8 1.1 %fusion.101 = (f32[31,64,128]{2,1,0:T(8,128)S(1)}, f32[31,64,128]{2,1,0:T(8,128)S(1)}) fusion(f32[32,66,130]{2,1,0:T(8,128)S(1)} %get-tuple-element.18, f32[32,66,130]{2,1,0:T(8,128)S(1)} %get-tuple-element.17), kind=kLoop, calls=%fused_computation.174 | loop fusion | flops 1523712 | bytes 6094848 | tf_op jit(solution)/shard_map/neg | solution.py:42
  64.9 2.3 %fusion.62 = f32[32,64,128]{2,1,0:T(8,128)S(1)} fusion(f32[32,66,130]{2,1,0:T(8,128)S(1)} %get-tuple-element.18, f32[32,66,130]{2,1,0:T(8,128)S(1)} %get-tuple-element.17, f32[31,64,128]{2,1,0:T(8,128)S(1)} %get-tuple-element.16, f32[31,64,128]{2,1,0:T(8,128)S(1)} %get-tuple-element.15, f32[64,128]{1,0:T(8,128)S(1)} %slice.398), kind=kLoop, calls=%fused_computation.103 | loop fusion | flops 6029312 | bytes 13598720 | tf_op jit(solution)/shard_map/mul | solution.py:46
  67.2 1.0 convolution_convert_fusion
  68.2 9.9 %all-to-all-start.1 = ((bf16[128,4,128]{2,1,0:T(4,128)(2,1)}), bf16[128,4,128]{2,1,0:T(4,128)(2,1)S(1)}, u32[]{:S(2)}, u32[]{:S(2)}) async-start(bf16[128,4,128]{2,1,0:T(4,128)(2,1)} %bitcast.5), calls=%async_computation.1 | async-start | bytes 262144 | tf_op jit(solution)/shard_map/all_to_all | solution.py:117
  78.1 10.0 %all-to-all-done.1 = bf16[128,4,128]{2,1,0:T(4,128)(2,1)S(1)} async-done(((bf16[128,4,128]{2,1,0:T(4,128)(2,1)}), bf16[128,4,128]{2,1,0:T(4,128)(2,1)S(1)}, u32[]{:S(2)}, u32[]{:S(2)}) %all-to-all-start.1) | async-done | bytes 131104 | tf_op jit(solution)/shard_map/all_to_all | solution.py:117
  88.0 0.2 convolution_convert_fusion.1
  88.3 3.5 %fusion.82 = f32[32,1,128,1]{2,1,3,0:T(1,128)S(1)} fusion(bf16[32,4,128,128]{3,2,1,0:T(8,128)(2,1)} %param.16, bf16[32,4,128,1]{2,1,0,3:T(4,128)(2,1)S(1)} %bitcast.49), kind=kOutput, calls=%fused_computation.142 | convolution fusion | flops 4194304 | bytes 4243456 | tf_op jit(solution)/shard_map/bnfc,bnc->bf/dot_general | solution.py:126
  91.8 0.7 fusion.92
  92.5 0.3 fusion.75
  92.8 0.2 copy.32
  93.0 15.0 %all_to_all.16 = f32[128,4,128]{2,1,0:T(4,128)S(1)} all-to-all(f32[128,4,128]{2,1,0:T(4,128)S(1)} %copy.32), channel_id=1, replica_groups=mesh['gx'=16,'gy'=8] {'gx','gy'}, dimensions={0} | all-to-all | bytes 524288 | tf_op jit(solution)/shard_map/all_to_all | solution.py:134
  108.0 0.5 multiply_bitcast_fusion.1
  108.5 0.6 pad_maximum_fusion.4
  (47 shorter events, 0.8 us)
Async XLA Ops:
  0.6 8.6 %copy-start.12 = (s32[32,4]{0,1:T(4,128)S(1)}, s32[32,4]{0,1:T(4,128)}, u32[]{:S(2)}) copy-start(s32[32,4]{0,1:T(4,128)} %param.17) | copy-start | bytes 1540
  0.6 9.0 %copy-start.13 = (s32[32,4]{0,1:T(4,128)S(1)}, s32[32,4]{0,1:T(4,128)}, u32[]{:S(2)}) copy-start(s32[32,4]{0,1:T(4,128)} %param.18) | copy-start | bytes 1540
  3.6 19.4 %collective-permute-start = (f32[33,4,128]{2,1,0:T(4,128)S(1)}, f32[33,4,128]{2,1,0:T(4,128)S(1)}, u32[]{:S(2)}, u32[]{:S(2)}) collective-permute-start(f32[33,4,128]{2,1,0:T(4,128)S(1)} %get-tuple-element.31), channel_id=1, source_target_pairs={{0,8},{8,16},{16,24},{24,32},{32,40},{40,48},{48,56},{56,64},{64,7... | collective-permute-start | bytes 202760 | tf_op jit(solution)/shard_map/ppermute | solution.py:18
  8.0 15.0 %collective-permute-start.1 = (f32[33,4,128]{2,1,0:T(4,128)S(1)}, f32[33,4,128]{2,1,0:T(4,128)S(1)}, u32[]{:S(2)}, u32[]{:S(2)}) collective-permute-start(f32[33,4,128]{2,1,0:T(4,128)S(1)} %get-tuple-element.32), channel_id=1, source_target_pairs={{8,0},{16,8},{24,16},{32,24},{40,32},{48,40},{56,48},{64,56},{72,6... | collective-permute-start | bytes 202760 | tf_op jit(solution)/shard_map/ppermute | solution.py:20
  10.7 23.2 %all-to-all-start = ((s32[128,1,4]{2,1,0:T(1,128)}), s32[128,1,4]{2,1,0:T(1,128)}, u32[]{:S(2)}, u32[]{:S(2)}) async-start(s32[128,1,4]{2,1,0:T(1,128)} %bitcast.3), calls=%async_computation | async-start | bytes 131072 | tf_op jit(solution)/shard_map/all_to_all | solution.py:110
  22.9 0.6 copy-start.2
  23.5 0.6 copy-start.4
  25.7 10.5 %collective-permute-start.2 = (f32[33,72,4]{1,2,0:T(4,128)}, f32[33,72,4]{1,2,0:T(4,128)S(1)}, u32[]{:S(2)}, u32[]{:S(2)}) collective-permute-start(f32[33,72,4]{1,2,0:T(4,128)} %copy.25), channel_id=1, source_target_pairs={{0,1},{1,2},{2,3},{3,4},{4,5},{5,6},{6,7},{8,9},{9,10},{10,11},{11... | collective-permute-start | bytes 114056 | tf_op jit(solution)/shard_map/ppermute | solution.py:18
  29.7 7.0 %collective-permute-start.3 = (f32[33,72,4]{1,2,0:T(4,128)S(1)}, f32[33,72,4]{1,2,0:T(4,128)}, u32[]{:S(2)}, u32[]{:S(2)}) collective-permute-start(f32[33,72,4]{1,2,0:T(4,128)S(1)} %copy.26), channel_id=1, source_target_pairs={{1,0},{2,1},{3,2},{4,3},{5,4},{6,5},{7,6},{9,8},{10,9},{11,10},{12... | collective-permute-start | bytes 114056 | tf_op jit(solution)/shard_map/ppermute | solution.py:20
  38.0 1.1 %copy-start.3 = (f32[33,4,128]{2,1,0:T(4,128)S(1)}, f32[33,4,128]{2,1,0:T(4,128)}, u32[]{:S(2)}) copy-start(f32[33,4,128]{2,1,0:T(4,128)} %copy-done.2) | copy-start | bytes 202756
  38.0 1.1 %copy-start.5 = (f32[33,4,128]{2,1,0:T(4,128)S(1)}, f32[33,4,128]{2,1,0:T(4,128)}, u32[]{:S(2)}) copy-start(f32[33,4,128]{2,1,0:T(4,128)} %copy-done.4) | copy-start | bytes 202756
  40.5 2.5 %copy-start.8 = (f32[70,134]{1,0:T(8,128)S(1)}, f32[70,134]{1,0:T(8,128)}, u32[]{:S(2)}) copy-start(f32[70,134]{1,0:T(8,128)} %slice.350) | copy-start | bytes 112564
  48.4 2.4 %copy-start.7 = (f32[68,132]{1,0:T(8,128)S(1)}, f32[68,132]{1,0:T(8,128)}, u32[]{:S(2)}) copy-start(f32[68,132]{1,0:T(8,128)} %slice.366) | copy-start | bytes 107716
  56.0 2.4 %copy-start.6 = (f32[66,130]{1,0:T(8,128)S(1)}, f32[66,130]{1,0:T(8,128)}, u32[]{:S(2)}) copy-start(f32[66,130]{1,0:T(8,128)} %slice.382) | copy-start | bytes 102964
  64.9 2.3 %copy-start.9 = (f32[64,128]{1,0:T(8,128)S(1)}, f32[64,128]{1,0:T(8,128)}, u32[]{:S(2)}) copy-start(f32[64,128]{1,0:T(8,128)} %param.15) | copy-start | bytes 98308
  67.2 40.8 %copy-start.1 = (f32[32,64,128]{2,1,0:T(8,128)}, f32[32,64,128]{2,1,0:T(8,128)S(1)}, u32[]{:S(2)}) copy-start(f32[32,64,128]{2,1,0:T(8,128)S(1)} %fusion.62) | copy-start | bytes 3145732
  68.2 23.6 %copy-start.11 = (f32[32,128]{1,0:T(8,128)S(1)}, f32[32,128]{1,0:T(8,128)}, u32[]{:S(2)}) copy-start(f32[32,128]{1,0:T(8,128)} %param.19) | copy-start | bytes 49156
  68.2 19.8 %all-to-all-start.1 = ((bf16[128,4,128]{2,1,0:T(4,128)(2,1)}), bf16[128,4,128]{2,1,0:T(4,128)(2,1)S(1)}, u32[]{:S(2)}, u32[]{:S(2)}) async-start(bf16[128,4,128]{2,1,0:T(4,128)(2,1)} %bitcast.5), calls=%async_computation.1 | async-start | bytes 262144 | tf_op jit(solution)/shard_map/all_to_all | solution.py:117
  88.0 3.8 %copy-start = (bf16[32,4,128,128]{3,2,1,0:T(8,128)(2,1)S(1)}, bf16[32,4,128,128]{3,2,1,0:T(8,128)(2,1)}, u32[]{:S(2)}) copy-start(bf16[32,4,128,128]{3,2,1,0:T(8,128)(2,1)} %param.16) | copy-start | bytes 12582916
  91.8 1.2 %copy-start.10 = (f32[32,1,128,1]{2,1,3,0:T(1,128)}, f32[32,1,128,1]{2,1,3,0:T(1,128)S(1)}, u32[]{:S(2)}) copy-start(f32[32,1,128,1]{2,1,3,0:T(1,128)S(1)} %fusion.82) | copy-start | bytes 49156
where the time goes:
time: 110 us; the launch traced here: 109 us
  other arithmetic  33.1 us (30%)
  starting transfers between devices  33.1 us (30%)
  blocking collectives  15 us (14%)
  local copies, waits for them, and re-layouts  10.5 us (10%)
  waiting for transfers between devices  9.96 us (9%)
  matrix products  6.37 us (6%)
  between operations  1.1 us (1%)
    mul x5, other arithmetic, trimmed_step(): conduct = conduct_col[None] * (0.5 + state)  16.9 us
    all_to_all x1, blocking collectives, on_device(): lax.all_to_all(outgoing.reshape(ndev, CAP, block_len), ('gx', 'gy'), spli...  15 us
    all_to_all x1, starting transfers between devices, on_device(): lax.all_to_all(request.reshape(ndev, CAP), ('gx', 'gy'), split_axis=0, co...  12.1 us
    all_to_all x1, waiting for transfers between devices, on_device(): lax.all_to_all(served.reshape(ndev, CAP, block_len), ('gx', 'gy'), split_...  9.95 us
    all_to_all x1, starting transfers between devices, on_device(): lax.all_to_all(served.reshape(ndev, CAP, block_len), ('gx', 'gy'), split_...  9.86 us
    neg x4, other arithmetic, trimmed_step(): -flux_down  8.41 us
    ppermute x2, starting transfers between devices, with_halo(): lax.ppermute(tail, axis, [(i, (i + 1) % count) for i in range(ends)])  7.9 us
    dot_general x1, matrix products, on_device(): jnp.einsum('bnfc,bnc->bf', sensor_patch_coefficients, cell_rows, preferre...  3.52 us
  transfers between devices with their start and end apart: 6, of which 1 were waited for; matrix products, arithmetic and copies ran while one was open for 8% of the time, Pallas kernels for 0%

commit v1 on v0

v1 whole, which is shorter than its diff:
```python
import jax
import jax.numpy as jnp
from jax import lax
from jax.experimental import pallas as pl
from jax.experimental.pallas import tpu as pltpu
from jax.sharding import PartitionSpec as P

CAP = 4
STEPS = 4
L = 32
ROWS = 64
COLS = 128
WIDE = ROWS + 8
TILES = 128
SLOTS = TILES * CAP
OWN = 32
TOUCH = 4
REFS = OWN * TOUCH
FOOT = 128
F32 = jnp.float32
BF16 = jnp.bfloat16
VMEM = pl.BlockSpec(memory_space=pltpu.VMEM)
SMEM = pl.BlockSpec(memory_space=pltpu.SMEM)
ANY = pl.BlockSpec(memory_space=pl.ANY)
HBM = pl.BlockSpec(memory_space=pltpu.HBM)
LIMIT = 32 * 1024 * 1024


def call(body, outs, in_specs, name, scratch=(), out_specs=None, aliases=None, flops=0, moved=0):
    return pl.pallas_call(
        body,
        out_shape=outs,
        in_specs=in_specs,
        out_specs=out_specs or jax.tree.map(lambda _: VMEM, outs),
        input_output_aliases=aliases or {},
        scratch_shapes=list(scratch),
        name=name,
        compiler_params=pltpu.CompilerParams(vmem_limit_bytes=LIMIT),
        cost_estimate=pl.CostEstimate(flops=flops, bytes_accessed=moved, transcendentals=0),
    )


def iota(shape, dim):
    return lax.broadcasted_iota(jnp.int32, shape, dim)


def dot(a, b, ca, cb):
    return lax.dot_general(a, b, (((ca,), (cb,)), ((), ())), preferred_element_type=F32)


def prep_body(
    classes_ref, inflow_hbm, category_hbm, state_hbm,
    state_ref, conduct_ref, edge_ref, inflow_ref, category_ref, sems,
):
    copies = [
        pltpu.make_async_copy(category_hbm, category_ref, sems.at[0]),
        pltpu.make_async_copy(inflow_hbm, inflow_ref, sems.at[1]),
        pltpu.make_async_copy(state_hbm, state_ref, sems.at[2]),
    ]
    for copy in copies:
        copy.start()
    copies[0].wait()
    category = category_ref[...]
    conduct = jnp.zeros((ROWS, COLS), F32)
    for i in range(classes_ref.shape[0]):
        conduct = jnp.where(category == i, classes_ref[i], conduct)
    conduct_ref[...] = conduct
    copies[1].wait()
    copies[2].wait()
    state_ref[0] = state_ref[0] + inflow_ref[...]
    upper = iota((8, COLS), 0) < 4
    edges = jnp.where(upper[None], state_ref[:, 0:8, :], state_ref[:, ROWS - 8 : ROWS, :])
    ends = jnp.where(upper, conduct[0:8], conduct[ROWS - 8 : ROWS])[None]
    whole = jnp.concatenate([edges, ends, jnp.zeros((1, 8, COLS), F32)], axis=0)
    edge_ref[...] = whole.reshape((L + 2) * 8, COLS).astype(BF16)


def request_body(slot_hbm, strip_hbm, after_ref, placing_ref, request_ref, slot_ref, strip_ref, sems):
    copies = [
        pltpu.make_async_copy(slot_hbm, slot_ref, sems.at[0]),
        pltpu.make_async_copy(strip_hbm, strip_ref, sems.at[1]),
    ]
    for copy in copies:
        copy.start()
    for copy in copies:
        copy.wait()
    tile = jnp.concatenate([slot_ref[k : k + 1, :] for k in range(TOUCH)], axis=1)
    row = jnp.concatenate([strip_ref[k : k + 1, :] for k in range(TOUCH)], axis=1)
    sub = iota((TILES, REFS), 0)
    named = (sub == tile).astype(F32)
    before = (sub < iota((REFS, REFS), 1)).astype(F32).astype(BF16)
    rank = jnp.sum(dot(named.astype(BF16), before, 1, 0) * named, axis=0, keepdims=True)
    place = tile * CAP + rank.astype(jnp.int32)
    placing = (iota((SLOTS, REFS), 0) == place).astype(F32).astype(BF16)
    placing_ref[...] = placing
    wanted = (sub == row).astype(F32).astype(BF16)
    request_ref[...] = dot(placing, wanted, 1, 1).astype(BF16)


def row_halo(a_ref, b_ref, levels=L + 1):
    odd = lax.rem(lax.axis_index("gx"), 2)
    a = a_ref[...].astype(F32).reshape(L + 2, 8, COLS)
    b = b_ref[...].astype(F32).reshape(L + 2, 8, COLS)
    half = lax.div(iota((8, COLS), 0), 4)
    return jnp.where((half == odd)[None], a, b)


def halo_rows_inside():
    gx = lax.axis_index("gx")
    sub = iota((8, COLS), 0)
    below = (gx < lax.axis_size("gx") - 1).astype(jnp.int32)
    above = (gx > 0).astype(jnp.int32)
    return jnp.where(sub < 4, below, above) > 0


def held(new, inside):
    return jnp.concatenate([new[:ROWS], jnp.where(inside, new[ROWS:], 0.5)], axis=0)


def rows_change(u, k, cd):
    ud = pltpu.roll(u, WIDE - 1, 0)
    f = (k + cd * ud) * (ud - u)
    return f - pltpu.roll(f, 1, 0)


def lanes_change(u, k, cr):
    ur = pltpu.roll(u, COLS - 1, 1)
    f = (k + cr * ur) * (ur - u)
    return f - pltpu.roll(f, 1, 1)


def pack_body(state_ref, conduct_ref, a_ref, b_ref, own_ref, cond_ref, pa_ref, pb_ref):
    halo = row_halo(a_ref, b_ref)
    lane64 = iota((ROWS, COLS), 1)
    lane8 = iota((8, COLS), 1)
    shifts = (0, -4, 4, 8)

    def pack(levels_of, lane):
        acc = [jnp.zeros(lane.shape, F32) for _ in range(4)]
        for l in range(L):
            turned = levels_of(l)
            if l:
                turned = pltpu.roll(turned, 4 * l, 1)
            group = lane // 4
            for i, at in enumerate((l, (l + 1) % L, (l - 1) % L, (l - 2) % L)):
                acc[i] = jnp.where(group == at, turned, acc[i])
        return [pltpu.roll(x, s % COLS, 1) if s else x for x, s in zip(acc, shifts)]

    def spread(x, lane):
        out = []
        for s in (0, COLS - 4, 4, 8):
            y = jnp.where(lane < 4, pltpu.roll(x, s, 1) if s else x, 0.0)
            for d in (4, 8, 16, 32, 64):
                y = y + pltpu.roll(y, d, 1)
            out.append(y)
        return out

    main = pack(lambda l: state_ref[l], lane64)
    ends = pack(lambda l: halo[l], lane8)
    cmain = spread(conduct_ref[...], lane64)
    cends = spread(halo[L], lane8)
    packs = [jnp.concatenate([m, e], axis=0) for m, e in zip(main, ends)]
    conds = [jnp.concatenate([m, e], axis=0) for m, e in zip(cmain, cends)]
    for i in range(4):
        own_ref[i] = packs[i]
        cond_ref[i] = conds[i]
    odd = lax.rem(lax.axis_index("gy"), 2)
    left = jnp.concatenate([packs[0], conds[0]], axis=0)
    right = jnp.concatenate([packs[2], conds[2]], axis=0)
    is_odd = (jnp.zeros((2 * WIDE, COLS), jnp.int32) + odd) > 0
    pa_ref[...] = jnp.where(is_odd, left, right).astype(BF16)
    pb_ref[...] = jnp.where(is_odd, right, left).astype(BF16)


def strip_body(
    own_ref, cond_ref, pa_ref, pb_ref, tops_ref, thermal_ref, picker_ref,
    left_ref, right_ref, adjoint_ref, served_ref, u_ref, c_ref, cd_ref, cr_ref,
):
    gy = lax.axis_index("gy")
    odd = lax.rem(gy, 2)
    a = pa_ref[...].astype(F32)
    b = pb_ref[...].astype(F32)
    is_odd = (jnp.zeros((2 * WIDE, COLS), jnp.int32) + odd) > 0
    from_right = jnp.where(is_odd, b, a)
    from_left = jnp.where(is_odd, a, b)
    lane = iota((WIDE, COLS), 1)
    last = lax.rem(lane, 4) == 3
    first = lax.rem(lane, 4) == 0
    lowest = lane >= COLS - 4
    inside = halo_rows_inside()
    in_left = (jnp.zeros((WIDE, COLS), jnp.int32) + gy) > 0
    in_right = (jnp.zeros((WIDE, COLS), jnp.int32) + gy) < lax.axis_size("gy") - 1
    sources = (
        (from_left[:WIDE], from_left[WIDE:]),
        (own_ref[0], cond_ref[0]),
        (own_ref[1], cond_ref[1]),
        (own_ref[3], cond_ref[3]),
        (own_ref[2], cond_ref[2]),
        (from_right[:WIDE], from_right[WIDE:]),
    )
    for i, (s, c) in enumerate(sources):
        u_ref[i] = s + 0.5
        c_ref[i] = 0.5 * c

    def next_of(ref, i):
        x = pltpu.roll(ref[i], COLS - 1, 1)
        y = pltpu.roll(ref[min(i + 1, i // 3 * 3 + 2)], 3, 1)
        return jnp.where(last, y, x)

    for i in range(6):
        cd_ref[i] = pltpu.roll(c_ref[i], WIDE - 1, 0)
        cr_ref[i] = next_of(c_ref, i)

    for step in range(STEPS):
        fresh = []
        flux = None
        for i in range(6):
            u, c = u_ref[i], c_ref[i]
            k = c * u
            change = rows_change(u, k, cd_ref[i])
            ur = next_of(u_ref, i)
            f = (k + cr_ref[i] * ur) * (ur - u)
            before = pltpu.roll(f, 1, 1)
            if i % 3:
                before = jnp.where(first, pltpu.roll(flux, COLS - 3, 1), before)
            flux = f
            change = change + (f - before)
            uz = pltpu.roll(u, COLS - 4, 1)
            down = jnp.where(lowest, 0.0, (k + c * uz) * ((u - uz) + 0.3))
            change = change + (pltpu.roll(down, 4, 1) - down)
            new = held(u + change, inside)
            if i == 0:
                new = jnp.where(in_left, new, 0.5)
            if i == 5:
                new = jnp.where(in_right, new, 0.5)
            fresh.append(new)
        for i in range(6):
            u_ref[i] = fresh[i]
    left = u_ref[1][:ROWS] - 0.5
    right = u_ref[4][:ROWS] - 0.5
    left_ref[...] = left
    right_ref[...] = right
    lane = iota((ROWS, COLS), 1)

    def joined(l):
        lhs = pltpu.roll(left, COLS - 4 * l, 1) if l else left
        rhs = pltpu.roll(right, COLS - 4 - 4 * l, 1)
        return jnp.where(lane < 4, lhs, jnp.where(lane >= COLS - 4, rhs, tops_ref[l]))

    mix = 0.6 * joined(0) + 0.4 * joined(1)
    thermal = thermal_ref[...]
    bright = (thermal * (1.0 - 0.4 * mix * mix)).astype(BF16)
    adjoint_ref[...] = thermal * (-0.8 * mix)
    bright = jnp.concatenate([bright, jnp.zeros((COLS - ROWS, COLS), BF16)], axis=0)
    served_ref[...] = dot(picker_ref[...], bright, 1, 0).astype(BF16)


def wide_conduct(conduct_ref, halo):
    return 0.5 * jnp.concatenate([conduct_ref[...], halo[L]], axis=0)


def evolve(state_ref, conduct_ref, a_ref, b_ref, u_ref, c_ref, low, high, finish):
    halo = row_halo(a_ref, b_ref)
    c = wide_conduct(conduct_ref, halo)
    c_ref[0] = c
    c_ref[1] = pltpu.roll(c, WIDE - 1, 0)
    c_ref[2] = pltpu.roll(c, COLS - 1, 1)
    inside = halo_rows_inside()
    start, stop = max(0, low - STEPS), min(L, high + STEPS)
    for l in range(start, stop):
        u_ref[l - start] = jnp.concatenate([state_ref[l], halo[l]], axis=0) + 0.5
    for step in range(STEPS):
        top = max(0, low - (STEPS - 1 - step))
        end = min(L, high + (STEPS - 1 - step))
        above = None
        if top > 0:
            u, uz = u_ref[top - 1 - start], u_ref[top - start]
            above = c_ref[0] * (u + uz) * ((u - uz) + 0.3)
        u = u_ref[top - start]
        k = c_ref[0] * u
        for l in range(top, end):
            change = rows_change(u, k, c_ref[1]) + lanes_change(u, k, c_ref[2])
            if above is not None:
                change = change + above
            if l < L - 1:
                uz = u_ref[l + 1 - start]
                kz = c_ref[0] * uz
                above = (k + kz) * ((u - uz) + 0.3)
                change = change - above
            new = u + change
            if step < STEPS - 1:
                u_ref[l - start] = held(new, inside)
            else:
                finish(l, new[:ROWS] - 0.5)
            u, k = uz, kz


def tops_body(state_ref, conduct_ref, a_ref, b_ref, tops_ref, u_ref, c_ref):
    def finish(l, new):
        tops_ref[l] = new

    evolve(state_ref, conduct_ref, a_ref, b_ref, u_ref, c_ref, 0, 2, finish)


HALF = L // 2
PIECE = 4


def half_body(low, state_ref, conduct_ref, a_ref, b_ref, left_ref, right_ref, out_hbm, done_ref, u_ref, c_ref, own_ref, sems):
    lane = iota((ROWS, COLS), 1)
    copies = []

    def finish(l, new):
        lhs = pltpu.roll(left_ref[...], (COLS - 4 * l) % COLS, 1) if l else left_ref[...]
        turn = (COLS - 4 - 4 * l) % COLS
        rhs = pltpu.roll(right_ref[...], turn, 1) if turn else right_ref[...]
        own_ref[l - low] = jnp.where(lane < 4, lhs, jnp.where(lane >= COLS - 4, rhs, new))
        if (l + 1) % PIECE == 0:
            at = l + 1 - PIECE
            copy = pltpu.make_async_copy(
                own_ref.at[pl.ds(at - low, PIECE)], out_hbm.at[pl.ds(at, PIECE)], sems.at[len(copies)]
            )
            copy.start()
            copies.append(copy)

    evolve(state_ref, conduct_ref, a_ref, b_ref, u_ref, c_ref, low, low + HALF, finish)
    if done_ref is not None:
        done_ref[...] = jnp.zeros(done_ref.shape, F32)
    for copy in copies:
        copy.wait()


def upper_body(state_ref, conduct_ref, a_ref, b_ref, left_ref, right_ref, out_hbm, done_ref, *scratch):
    half_body(0, state_ref, conduct_ref, a_ref, b_ref, left_ref, right_ref, out_hbm, done_ref, *scratch)


def lower_body(state_ref, conduct_ref, a_ref, b_ref, left_ref, right_ref, begun_hbm, out_hbm, *scratch):
    half_body(HALF, state_ref, conduct_ref, a_ref, b_ref, left_ref, right_ref, out_hbm, None, *scratch)


def foot_body(
    returned_ref, placing_ref, after_ref, measured_hbm, weights_ref,
    bright_ref, outgoing_ref, measured_ref, held_ref, cells_ref, seen_ref, misfit_ref, contrib_ref, sems,
):
    parts = 8
    each = OWN // parts
    seen_copy = pltpu.make_async_copy(measured_hbm, measured_ref, sems.at[parts])
    seen_copy.start()
    copies = [
        pltpu.make_async_copy(
            weights_ref.at[pl.ds(p * each, each)], held_ref.at[pl.ds(p * each, each)], sems.at[p]
        )
        for p in range(parts)
    ]
    for copy in copies:
        copy.start()
    placing = placing_ref[...]
    cells_ref[...] = dot(placing, returned_ref[...], 0, 0)
    seen_copy.wait()
    seen = jnp.concatenate([measured_ref[...], jnp.zeros((COLS - OWN, FOOT), F32)], axis=0)
    seen_ref[...] = jnp.transpose(seen)
    misfit_ref[...] = jnp.zeros((FOOT, COLS), F32)
    lane = iota((FOOT, COLS), 1)

    def block(b, carry):
        total = jnp.where(lane == b, -seen_ref[...], 0.0)
        for k in range(TOUCH):
            total = total + held_ref[b, k].astype(F32) * cells_ref[pl.ds(k * OWN + b, 1), :]
        misfit = jnp.sum(total, axis=1, keepdims=True)
        misfit_ref[...] = jnp.where(lane == b, misfit, misfit_ref[...])
        rounded = misfit.astype(BF16).astype(F32)
        for k in range(TOUCH):
            contrib_ref[pl.ds(k * OWN + b, 1), :] = jnp.sum(
                held_ref[b, k].astype(F32) * rounded, axis=0, keepdims=True
            )
        return carry

    for p in range(parts):
        copies[p].wait()
        for b in range(p * each, (p + 1) * each):
            block(b, 0)
    evolved = jnp.transpose(misfit_ref[...] + seen_ref[...])
    bright_ref[...] = evolved[:OWN]
    outgoing_ref[...] = dot(placing, contrib_ref[...].astype(BF16), 1, 0).astype(BF16)


def gradient_body(grads_ref, picker_ref, adjoint_ref, out_ref):
    summed = dot(picker_ref[...], grads_ref[...], 0, 0)[:ROWS]
    common = summed * adjoint_ref[...]
    out_ref[0] = 0.6 * common
    out_ref[1] = 0.4 * common


def swapped(x, axis):
    n = lax.axis_size(axis)
    one = [(i, i ^ 1) for i in range(n)]
    two = [(i, i + 1) for i in range(1, n - 1, 2)] + [(i + 1, i) for i in range(1, n - 1, 2)]
    return lax.ppermute(x[0], axis, one), lax.ppermute(x[1], axis, two)


def exchange(x):
    return lax.all_to_all(
        x.reshape(TILES, CAP, COLS), ("gx", "gy"), split_axis=0, concat_axis=0, tiled=True
    ).reshape(SLOTS, COLS)


def on_device(state, inflow, classes, category, thermal, weights, slots, strips, measured):
    def sds(*shape, dtype=F32):
        return jax.ShapeDtypeStruct(shape, dtype)

    held_state, conduct, edge = call(
        prep_body,
        (sds(L, ROWS, COLS), sds(ROWS, COLS), sds((L + 2) * 8, COLS, dtype=BF16)),
        [SMEM, HBM, HBM, HBM],
        "prep",
        [pltpu.VMEM((ROWS, COLS), F32), pltpu.VMEM((ROWS, COLS), jnp.int32), pltpu.SemaphoreType.DMA((3,))],
        flops=1_000_000, moved=2_000_000,
    )(classes, inflow, category, state)
    xa, xb = swapped((edge, edge), "gx")
    placing, request = call(
        request_body,
        (sds(SLOTS, REFS, dtype=BF16), sds(SLOTS, COLS, dtype=BF16)),
        [HBM, HBM, ANY],
        "requests",
        [pltpu.VMEM((TOUCH, OWN), jnp.int32), pltpu.VMEM((TOUCH, OWN), jnp.int32), pltpu.SemaphoreType.DMA((2,))],
        flops=20_000_000, moved=500_000,
    )(slots.T, strips.T, conduct)
    picker = exchange(request)
    own, cond, pa, pb = call(
        pack_body,
        (sds(4, WIDE, COLS), sds(4, WIDE, COLS), sds(2 * WIDE, COLS, dtype=BF16), sds(2 * WIDE, COLS, dtype=BF16)),
        [VMEM] * 4,
        "pack",
        flops=2_000_000, moved=1_500_000,
    )(held_state, conduct, xa, xb)
    ya, yb = swapped((pa, pb), "gy")
    tops = call(
        tops_body,
        sds(2, ROWS, COLS),
        [VMEM] * 4,
        "tops",
        [pltpu.VMEM((STEPS + 2, WIDE, COLS), F32), pltpu.VMEM((3, WIDE, COLS), F32)],
        flops=4_000_000, moved=1_000_000,
    )(held_state, conduct, xa, xb)
    left, right, adjoint, served = call(
        strip_body,
        (sds(ROWS, COLS), sds(ROWS, COLS), sds(ROWS, COLS), sds(SLOTS, COLS, dtype=BF16)),
        [VMEM] * 7,
        "strips",
        [pltpu.VMEM((6, WIDE, COLS), F32)] * 4,
        flops=20_000_000, moved=1_000_000,
    )(own, cond, ya, yb, tops, thermal, picker)
    returned = exchange(served)
    scratch = [
        pltpu.VMEM((HALF + STEPS, WIDE, COLS), F32),
        pltpu.VMEM((3, WIDE, COLS), F32),
        pltpu.VMEM((HALF, ROWS, COLS), F32),
        pltpu.SemaphoreType.DMA((HALF // PIECE,)),
    ]
    begun, done = call(
        upper_body,
        (sds(L, ROWS, COLS), sds(8, COLS)),
        [VMEM] * 6,
        "upper",
        scratch,
        out_specs=(HBM, VMEM),
        flops=500_000_000, moved=3_000_000,
    )(held_state, conduct, xa, xb, left, right)
    brightness, outgoing = call(
        foot_body,
        (sds(OWN, FOOT), sds(SLOTS, COLS, dtype=BF16)),
        [VMEM, VMEM, ANY, HBM, HBM],
        "footprints",
        [
            pltpu.VMEM((OWN, FOOT), F32),
            pltpu.VMEM((OWN, TOUCH, FOOT, COLS), BF16),
            pltpu.VMEM((REFS, COLS), F32),
            pltpu.VMEM((FOOT, COLS), F32),
            pltpu.VMEM((FOOT, COLS), F32),
            pltpu.VMEM((REFS, COLS), F32),
            pltpu.SemaphoreType.DMA((9,)),
        ],
        flops=20_000_000, moved=5_000_000,
    )(returned, placing, done, measured, weights)
    moisture = call(
        lower_body,
        sds(L, ROWS, COLS),
        [VMEM] * 6 + [HBM],
        "lower",
        scratch,
        out_specs=HBM,
        aliases={6: 0},
        flops=500_000_000, moved=3_000_000,
    )(held_state, conduct, xa, xb, left, right, begun)
    grads = exchange(outgoing)
    grad_top = call(
        gradient_body, sds(2, ROWS, COLS), [VMEM] * 3, "gradient", flops=20_000_000, moved=400_000
    )(grads, picker, adjoint)
    return moisture, brightness, grad_top


def solution(mesh):
    placed = (
        P(None, "gx", "gy"),
        P("gx", "gy"),
        P(),
        P("gx", "gy"),
        P("gx", "gy"),
        P(("gx", "gy"), None, None, None),
        P(("gx", "gy"), None),
        P(("gx", "gy"), None),
        P(("gx", "gy"), None),
    )
    return jax.shard_map(
        on_device,
        mesh=mesh,
        in_specs=placed,
        out_specs=(P(None, "gx", "gy"), P(("gx", "gy"), None), P(None, "gx", "gy")),
        check_vma=False,
    )
```

time: 110 us -> 81.9 us (0.74)
  other arithmetic: 33.1 us -> 0 us
  Pallas kernels: 0 us -> 24.6 us
  blocking collectives: 15 us -> 0 us
  matrix products: 6.37 us -> 0 us
  starting transfers between devices: 33.1 us -> 37.9 us
  local copies, waits for them, and re-layouts: 10.5 us -> 7.7 us
    pallas_call x0 -> x9, Pallas kernels: none -> 24.6 us  [the longest x1 6.44 us: on_device(): call(upper_body, (sds(L, ROWS, COLS), sds(8, COLS)), [VMEM] * 6, 'upper',...]
    mul x6 -> x0, other arithmetic: 19.2 us -> none  [the longest x5 16.9 us: trimmed_step(): conduct = conduct_col[None] * (0.5 + state)]
    all_to_all x1 -> x0, blocking collectives: 15 us -> none  [on_device(): lax.all_to_all(outgoing.reshape(ndev, CAP, block_len), ('gx', 'gy'), spli...]
    all_to_all x2 -> x3, starting transfers between devices: 22 us -> 30.7 us  [exchange(): lax.all_to_all(x.reshape(TILES, CAP, COLS), ('gx', 'gy'), split_axis=0, c...]
    neg x4 -> x0, other arithmetic: 8.41 us -> none  [trimmed_step(): -flux_down]
    dot_general x7 -> x0, matrix products: 6.37 us -> none  [the longest x1 3.52 us: on_device(): jnp.einsum('bnfc,bnc->bf', sensor_patch_coefficients, cell_rows, preferre...]
    unnamed x30 -> x18, local copies, waits for them, and re-layouts: 2.59 us -> 7.7 us
    slice x10 -> x0, local copies, waits for them, and re-layouts: 4.3 us -> none  [the longest x4 2.22 us: trimmed_step(): inner = inside[1:-1, 1:-1]]
  transfers between devices with their start and end apart: 6 -> 7, of which waited for: 1 -> 4; matrix products, arithmetic and copies ran while one was open for 8% -> 0% of each run, Pallas kernels for 0% -> 18%
where the time goes in v1:
time: 81.9 us; the launch traced here: 81.3 us
  starting transfers between devices  37.9 us (46%)
  Pallas kernels  24.6 us (30%)
  waiting for transfers between devices  10.4 us (13%)
  local copies, waits for them, and re-layouts  7.7 us (9%)
    all_to_all x3, starting transfers between devices, exchange(): lax.all_to_all(x.reshape(TILES, CAP, COLS), ('gx', 'gy'), split_axis=0, c...  30.7 us
    unnamed x18, local copies, waits for them, and re-layouts  7.7 us
    ppermute x4, starting transfers between devices, swapped(): return (lax.ppermute(x[0], axis, one), lax.ppermute(x[1], axis, two))  7.11 us
    all_to_all x3, waiting for transfers between devices, exchange(): lax.all_to_all(x.reshape(TILES, CAP, COLS), ('gx', 'gy'), split_axis=0, c...  7.07 us
    pallas_call x1, Pallas kernels, on_device(): call(upper_body, (sds(L, ROWS, COLS), sds(8, COLS)), [VMEM] * 6, 'upper',...  6.44 us
    pallas_call x1, Pallas kernels, on_device(): call(lower_body, sds(L, ROWS, COLS), [VMEM] * 6 + [HBM], 'lower', scratch...  6.41 us
    pallas_call x1, Pallas kernels, on_device(): call(strip_body, (sds(ROWS, COLS), sds(ROWS, COLS), sds(ROWS, COLS), sds(...  3.88 us
    pallas_call x1, Pallas kernels, on_device(): call(foot_body, (sds(OWN, FOOT), sds(SLOTS, COLS, dtype=BF16)), [VMEM, VM...  3.56 us
  transfers between devices with their start and end apart: 7, of which 4 were waited for; matrix products, arithmetic and copies ran while one was open for 0% of the time, Pallas kernels for 18%

profile of v1, /device:TPU:1, one launch (start us, length us, event | category | flops | bytes accessed | tf_op | source)
XLA Modules:
  0.0 81.3 jit_solution(10071596463358725016)
XLA Ops:
  0.6 0.0 copy-start.1
  0.6 1.2 %copy-done.1 = f32[32,64,128]{2,1,0:T(8,128)S(1)} copy-done((f32[32,64,128]{2,1,0:T(8,128)S(1)}, f32[32,64,128]{2,1,0:T(8,128)}, u32[]{:S(2)}) %copy-start.1) | copy-done | bytes 1048600
  1.9 0.0 copy-start.2
  1.9 0.8 copy-done.2
  2.6 0.0 copy-start.3
  2.6 0.8 copy-done.3
  3.4 0.0 copy-start.6
  3.4 0.7 copy-done.6
  4.0 0.0 copy-start.5
  4.0 0.8 prep.1
  4.8 0.0 copy-start.7
  4.8 0.7 copy-done.7
  5.5 0.0 copy-start.8
  5.5 0.7 copy-done.8
  6.2 1.1 %requests.1 = (bf16[512,128]{1,0:T(8,128)(2,1)S(1)}, bf16[512,128]{1,0:T(8,128)(2,1)}) custom-call(s32[4,32]{1,0:T(4,128)S(1)} %bitcast.12, s32[4,32]{1,0:T(4,128)S(1)} %bitcast.13, f32[64,128]{1,0:T(8,128)S(1)} %get-tuple-element.21.conduct_ref.after_ref), custom_call_target="tpu_custom_call" | custom-call | flops 20000000 | bytes 500000 | tf_op jit(solution)/shard_map/requests/pallas_call | solution.py:420
  7.3 11.5 %all-to-all-start = ((bf16[128,4,128]{2,1,0:T(4,128)(2,1)}), bf16[128,4,128]{2,1,0:T(4,128)(2,1)S(1)}, u32[]{:S(2)}, u32[]{:S(2)}) async-start(bf16[128,4,128]{2,1,0:T(4,128)(2,1)} %bitcast.2), calls=%async_computation | async-start | bytes 262144 | tf_op jit(solution)/shard_map/all_to_all | solution.py:402
  18.8 1.6 %collective-permute-start = (bf16[272,128]{1,0:T(8,128)(2,1)S(1)}, bf16[272,128]{1,0:T(8,128)(2,1)S(1)}, u32[]{:S(2)}, u32[]{:S(2)}) collective-permute-start(bf16[272,128]{1,0:T(8,128)(2,1)S(1)} %get-tuple-element.22), channel_id=1, source_target_pairs={{0,8},{8,0},{16,24},{24,16},{32,40},{40,32},{48,56},{56,48},{64,72... | collective-permute-start | bytes 208904 | tf_op jit(solution)/shard_map/ppermute | solution.py:398
  20.4 0.7 collective-permute-start.1
  21.0 1.5 %collective-permute-done.a_ref = bf16[272,128]{1,0:T(8,128)(2,1)S(1)} collective-permute-done((bf16[272,128]{1,0:T(8,128)(2,1)S(1)}, bf16[272,128]{1,0:T(8,128)(2,1)S(1)}, u32[]{:S(2)}, u32[]{:S(2)}) %collective-permute-start) | collective-permute-done | bytes 69664 | tf_op jit(solution)/shard_map/ppermute | solution.py:398
  22.5 0.0 collective-permute-done.1.b_ref
  22.5 0.9 %pack.1 = (f32[4,72,128]{2,1,0:T(8,128)S(1)}, f32[4,72,128]{2,1,0:T(8,128)S(1)}, bf16[144,128]{1,0:T(8,128)(2,1)S(1)}, bf16[144,128]{1,0:T(8,128)(2,1)S(1)}) custom-call(f32[32,64,128]{2,1,0:T(8,128)S(1)} %get-tuple-element.20.state_ref, f32[64,128]{1,0:T(8,128)S(1)} %get-tuple-element.21.conduct_ref.after_ref, ...), custom_call_target="tpu_custom_call" | custom-call | flops 2000000 | bytes 1500000 | tf_op jit(solution)/shard_map/pack/pallas_call | solution.py:429
  23.4 2.2 %collective-permute-start.2 = (bf16[144,128]{1,0:T(8,128)(2,1)S(1)}, bf16[144,128]{1,0:T(8,128)(2,1)S(1)}, u32[]{:S(2)}, u32[]{:S(2)}) collective-permute-start(bf16[144,128]{1,0:T(8,128)(2,1)S(1)} %get-tuple-element.25), channel_id=1, source_target_pairs={{0,1},{1,0},{2,3},{3,2},{4,5},{5,4},{6,7},{7,6},{8,9},{9,8},{10,11... | collective-permute-start | bytes 110600 | tf_op jit(solution)/shard_map/ppermute | solution.py:398
  25.6 2.7 %collective-permute-start.3 = (bf16[144,128]{1,0:T(8,128)(2,1)S(1)}, bf16[144,128]{1,0:T(8,128)(2,1)S(1)}, u32[]{:S(2)}, u32[]{:S(2)}) collective-permute-start(bf16[144,128]{1,0:T(8,128)(2,1)S(1)} %get-tuple-element.26), channel_id=1, source_target_pairs={{1,2},{3,4},{5,6},{2,1},{4,3},{6,5},{9,10},{11,12},{13,14},{10,9},... | collective-permute-start | bytes 110600 | tf_op jit(solution)/shard_map/ppermute | solution.py:398
  28.3 0.7 tops.1.tops_ref
  29.0 0.0 collective-permute-done.2.pa_ref
  29.0 1.9 %collective-permute-done.3.pb_ref = bf16[144,128]{1,0:T(8,128)(2,1)S(1)} collective-permute-done((bf16[144,128]{1,0:T(8,128)(2,1)S(1)}, bf16[144,128]{1,0:T(8,128)(2,1)S(1)}, u32[]{:S(2)}, u32[]{:S(2)}) %collective-permute-start.3) | collective-permute-done | bytes 36896 | tf_op jit(solution)/shard_map/ppermute | solution.py:398
  30.8 0.0 all-to-all-done
  30.9 0.0 copy-start.4
  30.9 0.8 copy-done.4
  31.6 3.9 %strips.1 = (f32[64,128]{1,0:T(8,128)S(1)}, f32[64,128]{1,0:T(8,128)S(1)}, f32[64,128]{1,0:T(8,128)S(1)}, bf16[512,128]{1,0:T(8,128)(2,1)}) custom-call(f32[4,72,128]{2,1,0:T(8,128)S(1)} %get-tuple-element.23.own_ref, f32[4,72,128]{2,1,0:T(8,128)S(1)} %get-tuple-element.24.cond_ref, bf16[144,128]{1,0:T(8,128)(2,1)S(1)} %collective-permute-done.2.pa_ref, ...), custom_call_target="tpu_custom_call" | custom-call | flops 20000000 | bytes 1000000 | tf_op jit(solution)/shard_map/strips/pallas_call | solution.py:445
  35.5 13.0 %all-to-all-start.1 = ((bf16[128,4,128]{2,1,0:T(4,128)(2,1)}), bf16[128,4,128]{2,1,0:T(4,128)(2,1)S(1)}, u32[]{:S(2)}, u32[]{:S(2)}) async-start(bf16[128,4,128]{2,1,0:T(4,128)(2,1)} %bitcast.4), calls=%async_computation.1 | async-start | bytes 262144 | tf_op jit(solution)/shard_map/all_to_all | solution.py:402
  48.5 6.4 %upper.1 = (f32[32,64,128]{2,1,0:T(8,128)}, f32[8,128]{1,0:T(8,128)S(1)}) custom-call(f32[32,64,128]{2,1,0:T(8,128)S(1)} %get-tuple-element.20.state_ref, f32[64,128]{1,0:T(8,128)S(1)} %get-tuple-element.21.conduct_ref.after_ref, bf16[272,128]{1,0:T(8,128)(2,1)S(1)} %collective-permute-done.a_ref, bf16[272,128]{1,0:T(8,128)(2,1)S(1)} %collective-permute-done.1.b_ref, ...), custom_call_target="tpu_custom_call" | custom-call | flops 500000000 | bytes 3000000 | tf_op jit(solution)/shard_map/upper/pallas_call | solution.py:460
  54.9 3.5 %all-to-all-done.1 = bf16[128,4,128]{2,1,0:T(4,128)(2,1)S(1)} async-done(((bf16[128,4,128]{2,1,0:T(4,128)(2,1)}), bf16[128,4,128]{2,1,0:T(4,128)(2,1)S(1)}, u32[]{:S(2)}, u32[]{:S(2)}) %all-to-all-start.1) | async-done | bytes 131104 | tf_op jit(solution)/shard_map/all_to_all | solution.py:402
  58.4 0.0 copy-done.5
  58.4 0.0 copy-start
  58.5 2.2 %copy-done = bf16[32,4,128,128]{3,2,1,0:T(8,128)(2,1)S(1)} copy-done((bf16[32,4,128,128]{3,2,1,0:T(8,128)(2,1)S(1)}, bf16[32,4,128,128]{3,2,1,0:T(8,128)(2,1)}, u32[]{:S(2)}) %copy-start) | copy-done | bytes 4194328
  60.6 3.6 %footprints.1 = (f32[32,128]{1,0:T(8,128)}, bf16[512,128]{1,0:T(8,128)(2,1)}) custom-call(bf16[512,128]{1,0:T(8,128)(2,1)S(1)} %bitcast.10, bf16[512,128]{1,0:T(8,128)(2,1)S(1)} %get-tuple-element.32.placing_ref, f32[8,128]{1,0:T(8,128)S(1)} %get-tuple-element.33.after_ref, f32[32,128]{1,0:T(8,128)S(1)} %copy-done.5, bf16[32,4,128,128]{3,2,1,0:T(8,128)(2,1)S(1)} %copy-done), custom_call_target="tpu_custom_call" | custom-call | flops 20000000 | bytes 5000000 | tf_op jit(solution)/shard_map/footprints/pallas_call | solution.py:469
  64.2 6.3 %all-to-all-start.2 = ((bf16[128,4,128]{2,1,0:T(4,128)(2,1)}), bf16[128,4,128]{2,1,0:T(4,128)(2,1)S(1)}, u32[]{:S(2)}, u32[]{:S(2)}) async-start(bf16[128,4,128]{2,1,0:T(4,128)(2,1)} %bitcast.6), calls=%async_computation.2 | async-start | bytes 262144 | tf_op jit(solution)/shard_map/all_to_all | solution.py:402
  70.5 6.4 %lower.1 = f32[32,64,128]{2,1,0:T(8,128)} custom-call(f32[32,64,128]{2,1,0:T(8,128)S(1)} %get-tuple-element.20.state_ref, f32[64,128]{1,0:T(8,128)S(1)} %get-tuple-element.21.conduct_ref.after_ref, bf16[272,128]{1,0:T(8,128)(2,1)S(1)} %collective-permute-done.a_ref, ...), custom_call_target="tpu_custom_call", output_to_operand_aliasing={{}: (6, {})} | custom-call | flops 500000000 | bytes 3000000 | tf_op jit(solution)/shard_map/lower/pallas_call | solution.py:485
  76.9 3.5 %all-to-all-done.2 = bf16[128,4,128]{2,1,0:T(4,128)(2,1)S(1)} async-done(((bf16[128,4,128]{2,1,0:T(4,128)(2,1)}), bf16[128,4,128]{2,1,0:T(4,128)(2,1)S(1)}, u32[]{:S(2)}, u32[]{:S(2)}) %all-to-all-start.2) | async-done | bytes 131104 | tf_op jit(solution)/shard_map/all_to_all | solution.py:402
  80.4 0.9 %gradient.1 = f32[2,64,128]{2,1,0:T(8,128)} custom-call(bf16[512,128]{1,0:T(8,128)(2,1)S(1)} %bitcast.11, bf16[512,128]{1,0:T(8,128)(2,1)S(1)} %bitcast.9, f32[64,128]{1,0:T(8,128)S(1)} %get-tuple-element.36.adjoint_ref), custom_call_target="tpu_custom_call" | custom-call | flops 20000000 | bytes 400000 | tf_op jit(solution)/shard_map/gradient/pallas_call | solution.py:496
Async XLA Ops:
  0.6 1.2 %copy-start.1 = (f32[32,64,128]{2,1,0:T(8,128)S(1)}, f32[32,64,128]{2,1,0:T(8,128)}, u32[]{:S(2)}) copy-start(f32[32,64,128]{2,1,0:T(8,128)} %state_hbm.1) | copy-start | bytes 3145732
  1.9 0.8 copy-start.2
  2.6 0.8 copy-start.3
  3.4 0.7 copy-start.6
  4.0 54.4 %copy-start.5 = (f32[32,128]{1,0:T(8,128)S(1)}, f32[32,128]{1,0:T(8,128)}, u32[]{:S(2)}) copy-start(f32[32,128]{1,0:T(8,128)} %measured_hbm.1) | copy-start | bytes 49156
  4.8 0.7 copy-start.7
  5.5 0.7 copy-start.8
  7.3 23.6 %all-to-all-start = ((bf16[128,4,128]{2,1,0:T(4,128)(2,1)}), bf16[128,4,128]{2,1,0:T(4,128)(2,1)S(1)}, u32[]{:S(2)}, u32[]{:S(2)}) async-start(bf16[128,4,128]{2,1,0:T(4,128)(2,1)} %bitcast.2), calls=%async_computation | async-start | bytes 262144 | tf_op jit(solution)/shard_map/all_to_all | solution.py:402
  18.8 3.7 %collective-permute-start = (bf16[272,128]{1,0:T(8,128)(2,1)S(1)}, bf16[272,128]{1,0:T(8,128)(2,1)S(1)}, u32[]{:S(2)}, u32[]{:S(2)}) collective-permute-start(bf16[272,128]{1,0:T(8,128)(2,1)S(1)} %get-tuple-element.22), channel_id=1, source_target_pairs={{0,8},{8,0},{16,24},{24,16},{32,40},{40,32},{48,56},{56,48},{64,72... | collective-permute-start | bytes 208904 | tf_op jit(solution)/shard_map/ppermute | solution.py:398
  20.4 2.2 %collective-permute-start.1 = (bf16[272,128]{1,0:T(8,128)(2,1)S(1)}, bf16[272,128]{1,0:T(8,128)(2,1)S(1)}, u32[]{:S(2)}, u32[]{:S(2)}) collective-permute-start(bf16[272,128]{1,0:T(8,128)(2,1)S(1)} %get-tuple-element.22), channel_id=1, source_target_pairs={{8,16},{24,32},{40,48},{56,64},{72,80},{88,96},{104,112},{16,8},{3... | collective-permute-start | bytes 208904 | tf_op jit(solution)/shard_map/ppermute | solution.py:398
  23.4 5.6 %collective-permute-start.2 = (bf16[144,128]{1,0:T(8,128)(2,1)S(1)}, bf16[144,128]{1,0:T(8,128)(2,1)S(1)}, u32[]{:S(2)}, u32[]{:S(2)}) collective-permute-start(bf16[144,128]{1,0:T(8,128)(2,1)S(1)} %get-tuple-element.25), channel_id=1, source_target_pairs={{0,1},{1,0},{2,3},{3,2},{4,5},{5,4},{6,7},{7,6},{8,9},{9,8},{10,11... | collective-permute-start | bytes 110600 | tf_op jit(solution)/shard_map/ppermute | solution.py:398
  25.6 5.3 %collective-permute-start.3 = (bf16[144,128]{1,0:T(8,128)(2,1)S(1)}, bf16[144,128]{1,0:T(8,128)(2,1)S(1)}, u32[]{:S(2)}, u32[]{:S(2)}) collective-permute-start(bf16[144,128]{1,0:T(8,128)(2,1)S(1)} %get-tuple-element.26), channel_id=1, source_target_pairs={{1,2},{3,4},{5,6},{2,1},{4,3},{6,5},{9,10},{11,12},{13,14},{10,9},... | collective-permute-start | bytes 110600 | tf_op jit(solution)/shard_map/ppermute | solution.py:398
  30.9 0.8 copy-start.4
  35.5 23.0 %all-to-all-start.1 = ((bf16[128,4,128]{2,1,0:T(4,128)(2,1)}), bf16[128,4,128]{2,1,0:T(4,128)(2,1)S(1)}, u32[]{:S(2)}, u32[]{:S(2)}) async-start(bf16[128,4,128]{2,1,0:T(4,128)(2,1)} %bitcast.4), calls=%async_computation.1 | async-start | bytes 262144 | tf_op jit(solution)/shard_map/all_to_all | solution.py:402
  58.4 2.2 %copy-start = (bf16[32,4,128,128]{3,2,1,0:T(8,128)(2,1)S(1)}, bf16[32,4,128,128]{3,2,1,0:T(8,128)(2,1)}, u32[]{:S(2)}) copy-start(bf16[32,4,128,128]{3,2,1,0:T(8,128)(2,1)} %weights_ref.1) | copy-start | bytes 12582916
  64.2 16.2 %all-to-all-start.2 = ((bf16[128,4,128]{2,1,0:T(4,128)(2,1)}), bf16[128,4,128]{2,1,0:T(4,128)(2,1)S(1)}, u32[]{:S(2)}, u32[]{:S(2)}) async-start(bf16[128,4,128]{2,1,0:T(4,128)(2,1)} %bitcast.6), calls=%async_computation.2 | async-start | bytes 262144 | tf_op jit(solution)/shard_map/all_to_all | solution.py:402

commit v2 on v1

--- a/solution.py
+++ b/solution.py
@@ -44,18 +44,23 @@
     return lax.broadcasted_iota(jnp.int32, shape, dim)
 
 
+def far(x):
+    return pltpu.with_memory_space_constraint(x, pltpu.HBM)
+
+
 def dot(a, b, ca, cb):
     return lax.dot_general(a, b, (((ca,), (cb,)), ((), ())), preferred_element_type=F32)
 
 
 def prep_body(
-    classes_ref, inflow_hbm, category_hbm, state_hbm,
-    state_ref, conduct_ref, edge_ref, inflow_ref, category_ref, sems,
+    classes_ref, inflow_hbm, category_hbm, state_hbm, thermal_hbm,
+    state_ref, conduct_ref, edge_ref, thermal_ref, inflow_ref, category_ref, sems,
 ):
     copies = [
         pltpu.make_async_copy(category_hbm, category_ref, sems.at[0]),
         pltpu.make_async_copy(inflow_hbm, inflow_ref, sems.at[1]),
         pltpu.make_async_copy(state_hbm, state_ref, sems.at[2]),
+        pltpu.make_async_copy(thermal_hbm, thermal_ref, sems.at[3]),
     ]
     for copy in copies:
         copy.start()
@@ -73,6 +78,7 @@
     ends = jnp.where(upper, conduct[0:8], conduct[ROWS - 8 : ROWS])[None]
     whole = jnp.concatenate([edges, ends, jnp.zeros((1, 8, COLS), F32)], axis=0)
     edge_ref[...] = whole.reshape((L + 2) * 8, COLS).astype(BF16)
+    copies[3].wait()
 
 
 def request_body(slot_hbm, strip_hbm, after_ref, placing_ref, request_ref, slot_ref, strip_ref, sems):
@@ -408,14 +414,14 @@
     def sds(*shape, dtype=F32):
         return jax.ShapeDtypeStruct(shape, dtype)
 
-    held_state, conduct, edge = call(
+    held_state, conduct, edge, warm = call(
         prep_body,
-        (sds(L, ROWS, COLS), sds(ROWS, COLS), sds((L + 2) * 8, COLS, dtype=BF16)),
-        [SMEM, HBM, HBM, HBM],
+        (sds(L, ROWS, COLS), sds(ROWS, COLS), sds((L + 2) * 8, COLS, dtype=BF16), sds(ROWS, COLS)),
+        [SMEM, HBM, HBM, HBM, HBM],
         "prep",
-        [pltpu.VMEM((ROWS, COLS), F32), pltpu.VMEM((ROWS, COLS), jnp.int32), pltpu.SemaphoreType.DMA((3,))],
+        [pltpu.VMEM((ROWS, COLS), F32), pltpu.VMEM((ROWS, COLS), jnp.int32), pltpu.SemaphoreType.DMA((4,))],
         flops=1_000_000, moved=2_000_000,
-    )(classes, inflow, category, state)
+    )(classes, far(inflow), far(category), far(state), far(thermal))
     xa, xb = swapped((edge, edge), "gx")
     placing, request = call(
         request_body,
@@ -424,14 +430,14 @@
         "requests",
         [pltpu.VMEM((TOUCH, OWN), jnp.int32), pltpu.VMEM((TOUCH, OWN), jnp.int32), pltpu.SemaphoreType.DMA((2,))],
         flops=20_000_000, moved=500_000,
-    )(slots.T, strips.T, conduct)
+    )(far(slots.T), far(strips.T), conduct)
     picker = exchange(request)
     own, cond, pa, pb = call(
         pack_body,
         (sds(4, WIDE, COLS), sds(4, WIDE, COLS), sds(2 * WIDE, COLS, dtype=BF16), sds(2 * WIDE, COLS, dtype=BF16)),
         [VMEM] * 4,
         "pack",
-        flops=2_000_000, moved=1_500_000,
+        flops=20_000_000_000, moved=1_500_000,
     )(held_state, conduct, xa, xb)
     ya, yb = swapped((pa, pb), "gy")
     tops = call(
@@ -440,7 +446,7 @@
         [VMEM] * 4,
         "tops",
         [pltpu.VMEM((STEPS + 2, WIDE, COLS), F32), pltpu.VMEM((3, WIDE, COLS), F32)],
-        flops=4_000_000, moved=1_000_000,
+        flops=20_000_000_000, moved=1_000_000,
     )(held_state, conduct, xa, xb)
     left, right, adjoint, served = call(
         strip_body,
@@ -449,7 +455,7 @@
         "strips",
         [pltpu.VMEM((6, WIDE, COLS), F32)] * 4,
         flops=20_000_000, moved=1_000_000,
-    )(own, cond, ya, yb, tops, thermal, picker)
+    )(own, cond, ya, yb, tops, warm, picker)
     returned = exchange(served)
     scratch = [
         pltpu.VMEM((HALF + STEPS, WIDE, COLS), F32),
@@ -481,7 +487,7 @@
             pltpu.SemaphoreType.DMA((9,)),
         ],
         flops=20_000_000, moved=5_000_000,
-    )(returned, placing, done, measured, weights)
+    )(returned, placing, done, far(measured), far(weights))
     moisture = call(
         lower_body,
         sds(L, ROWS, COLS),

time: 81.9 us -> 71.8 us (0.88)
  local copies, waits for them, and re-layouts: 7.7 us -> 0.65 us
  starting transfers between devices: 37.9 us -> 31.6 us
  Pallas kernels: 24.6 us -> 26.8 us
  waiting for transfers between devices: 10.4 us -> 11.7 us
    unnamed x18 -> x2, local copies, waits for them, and re-layouts: 7.7 us -> 0.65 us
    all_to_all x3, starting transfers between devices: 30.7 us -> 24.6 us  [exchange(): lax.all_to_all(x.reshape(TILES, CAP, COLS), ('gx', 'gy'), split_axis=0, c...]
    all_to_all x3, waiting for transfers between devices: 7.07 us -> 9.42 us  [exchange(): lax.all_to_all(x.reshape(TILES, CAP, COLS), ('gx', 'gy'), split_axis=0, c...]
    ppermute x4, waiting for transfers between devices: 3.35 us -> 2.25 us  [swapped(): return (lax.ppermute(x[0], axis, one), lax.ppermute(x[1], axis, two))]
    pallas_call x1, Pallas kernels: 0.78 us -> 1.86 us  [on_device(): call(prep_body, (sds(L, ROWS, COLS), sds(ROWS, COLS), sds((L + 2) * 8, CO...]
  transfers between devices with their start and end apart: 7 -> 7, of which waited for: 4 -> 4; matrix products, arithmetic and copies ran while one was open for 0% -> 0% of each run, Pallas kernels for 18% -> 23%
where the time goes in v2:
time: 71.8 us; the launch traced here: 71.4 us
  starting transfers between devices  31.6 us (44%)
  Pallas kernels  26.8 us (37%)
  waiting for transfers between devices  11.7 us (16%)
  between operations  0.76 us (1%)
    all_to_all x3, starting transfers between devices, exchange(): lax.all_to_all(x.reshape(TILES, CAP, COLS), ('gx', 'gy'), split_axis=0, c...  24.6 us
    all_to_all x3, waiting for transfers between devices, exchange(): lax.all_to_all(x.reshape(TILES, CAP, COLS), ('gx', 'gy'), split_axis=0, c...  9.42 us
    ppermute x4, starting transfers between devices, swapped(): return (lax.ppermute(x[0], axis, one), lax.ppermute(x[1], axis, two))  6.96 us
    pallas_call x1, Pallas kernels, on_device(): call(upper_body, (sds(L, ROWS, COLS), sds(8, COLS)), [VMEM] * 6, 'upper',...  6.43 us
    pallas_call x1, Pallas kernels, on_device(): call(lower_body, sds(L, ROWS, COLS), [VMEM] * 6 + [HBM], 'lower', scratch...  6.39 us
    pallas_call x1, Pallas kernels, on_device(): call(foot_body, (sds(OWN, FOOT), sds(SLOTS, COLS, dtype=BF16)), [VMEM, VM...  4.04 us
    pallas_call x1, Pallas kernels, on_device(): call(strip_body, (sds(ROWS, COLS), sds(ROWS, COLS), sds(ROWS, COLS), sds(...  3.9 us
    ppermute x4, waiting for transfers between devices, swapped(): return (lax.ppermute(x[0], axis, one), lax.ppermute(x[1], axis, two))  2.25 us
  transfers between devices with their start and end apart: 7, of which 4 were waited for; matrix products, arithmetic and copies ran while one was open for 0% of the time, Pallas kernels for 23%

profile of v2, /device:TPU:1, one launch (start us, length us, event | category | flops | bytes accessed | tf_op | source)
XLA Modules:
  0.0 71.4 jit_solution(16131250385451729759)
XLA Ops:
  0.6 0.0 copy-start
  0.6 0.6 copy-done
  1.3 1.9 %prep.1 = (f32[32,64,128]{2,1,0:T(8,128)S(1)}, f32[64,128]{1,0:T(8,128)S(1)}, bf16[272,128]{1,0:T(8,128)(2,1)S(1)}, f32[64,128]{1,0:T(8,128)S(1)}) custom-call(f32[12]{0:T(128)S(1)} %copy-done, f32[64,128]{1,0:T(8,128)} %inflow_hbm.1, s32[64,128]{1,0:T(8,128)} %category_hbm.1, f32[32,64,128]{2,1,0:T(8,128)} %state_hbm.1, f32[64,128]{1,0:T(8,128)} %thermal_hbm.1), custom_call_target="tpu_custom_call" | custom-call | flops 1000000 | bytes 2000000 | tf_op jit(solution)/shard_map/prep/pallas_call | solution.py:417
  3.2 2.5 %collective-permute-start = (bf16[272,128]{1,0:T(8,128)(2,1)S(1)}, bf16[272,128]{1,0:T(8,128)(2,1)S(1)}, u32[]{:S(2)}, u32[]{:S(2)}) collective-permute-start(bf16[272,128]{1,0:T(8,128)(2,1)S(1)} %get-tuple-element.23), channel_id=1, source_target_pairs={{0,8},{8,0},{16,24},{24,16},{32,40},{40,32},{48,56},{56,48},{64,72... | collective-permute-start | bytes 208904 | tf_op jit(solution)/shard_map/ppermute | solution.py:404
  5.7 0.7 collective-permute-start.1
  6.4 1.8 %requests.1 = (bf16[512,128]{1,0:T(8,128)(2,1)S(1)}, bf16[512,128]{1,0:T(8,128)(2,1)}) custom-call(s32[4,32]{1,0:T(4,128)} %bitcast.12, s32[4,32]{1,0:T(4,128)} %bitcast.13, f32[64,128]{1,0:T(8,128)S(1)} %get-tuple-element.22.conduct_ref.after_ref), custom_call_target="tpu_custom_call" | custom-call | flops 20000000 | bytes 500000 | tf_op jit(solution)/shard_map/requests/pallas_call | solution.py:426
  8.1 12.1 %all-to-all-start = ((bf16[128,4,128]{2,1,0:T(4,128)(2,1)}), bf16[128,4,128]{2,1,0:T(4,128)(2,1)S(1)}, u32[]{:S(2)}, u32[]{:S(2)}) async-start(bf16[128,4,128]{2,1,0:T(4,128)(2,1)} %bitcast.2), calls=%async_computation | async-start | bytes 262144 | tf_op jit(solution)/shard_map/all_to_all | solution.py:408
  20.3 0.0 collective-permute-done.a_ref
  20.3 0.0 collective-permute-done.1.b_ref
  20.3 0.9 %pack.1 = (f32[4,72,128]{2,1,0:T(8,128)S(1)}, f32[4,72,128]{2,1,0:T(8,128)S(1)}, bf16[144,128]{1,0:T(8,128)(2,1)S(1)}, bf16[144,128]{1,0:T(8,128)(2,1)S(1)}) custom-call(f32[32,64,128]{2,1,0:T(8,128)S(1)} %get-tuple-element.21.state_ref, f32[64,128]{1,0:T(8,128)S(1)} %get-tuple-element.22.conduct_ref.after_ref, ...), custom_call_target="tpu_custom_call" | custom-call | flops 20000000000 | bytes 1500000 | tf_op jit(solution)/shard_map/pack/pallas_call | solution.py:435
  21.2 1.1 %collective-permute-start.2 = (bf16[144,128]{1,0:T(8,128)(2,1)S(1)}, bf16[144,128]{1,0:T(8,128)(2,1)S(1)}, u32[]{:S(2)}, u32[]{:S(2)}) collective-permute-start(bf16[144,128]{1,0:T(8,128)(2,1)S(1)} %get-tuple-element.26), channel_id=1, source_target_pairs={{0,1},{1,0},{2,3},{3,2},{4,5},{5,4},{6,7},{7,6},{8,9},{9,8},{10,11... | collective-permute-start | bytes 110600 | tf_op jit(solution)/shard_map/ppermute | solution.py:404
  22.3 2.6 %collective-permute-start.3 = (bf16[144,128]{1,0:T(8,128)(2,1)S(1)}, bf16[144,128]{1,0:T(8,128)(2,1)S(1)}, u32[]{:S(2)}, u32[]{:S(2)}) collective-permute-start(bf16[144,128]{1,0:T(8,128)(2,1)S(1)} %get-tuple-element.27), channel_id=1, source_target_pairs={{1,2},{3,4},{5,6},{2,1},{4,3},{6,5},{9,10},{11,12},{13,14},{10,9},... | collective-permute-start | bytes 110600 | tf_op jit(solution)/shard_map/ppermute | solution.py:404
  24.9 0.7 tops.1.tops_ref
  25.6 0.0 collective-permute-done.2.pa_ref
  25.6 2.2 %collective-permute-done.3.pb_ref = bf16[144,128]{1,0:T(8,128)(2,1)S(1)} collective-permute-done((bf16[144,128]{1,0:T(8,128)(2,1)S(1)}, bf16[144,128]{1,0:T(8,128)(2,1)S(1)}, u32[]{:S(2)}, u32[]{:S(2)}) %collective-permute-start.3) | collective-permute-done | bytes 36896 | tf_op jit(solution)/shard_map/ppermute | solution.py:404
  27.9 2.3 %all-to-all-done = bf16[128,4,128]{2,1,0:T(4,128)(2,1)S(1)} async-done(((bf16[128,4,128]{2,1,0:T(4,128)(2,1)}), bf16[128,4,128]{2,1,0:T(4,128)(2,1)S(1)}, u32[]{:S(2)}, u32[]{:S(2)}) %all-to-all-start) | async-done | bytes 131104 | tf_op jit(solution)/shard_map/all_to_all | solution.py:408
  30.2 3.9 %strips.1 = (f32[64,128]{1,0:T(8,128)S(1)}, f32[64,128]{1,0:T(8,128)S(1)}, f32[64,128]{1,0:T(8,128)S(1)}, bf16[512,128]{1,0:T(8,128)(2,1)}) custom-call(f32[4,72,128]{2,1,0:T(8,128)S(1)} %get-tuple-element.24.own_ref, f32[4,72,128]{2,1,0:T(8,128)S(1)} %get-tuple-element.25.cond_ref, bf16[144,128]{1,0:T(8,128)(2,1)S(1)} %collective-permute-done.2.pa_ref, ...), custom_call_target="tpu_custom_call" | custom-call | flops 20000000 | bytes 1000000 | tf_op jit(solution)/shard_map/strips/pallas_call | solution.py:451
  34.1 6.2 %all-to-all-start.1 = ((bf16[128,4,128]{2,1,0:T(4,128)(2,1)}), bf16[128,4,128]{2,1,0:T(4,128)(2,1)S(1)}, u32[]{:S(2)}, u32[]{:S(2)}) async-start(bf16[128,4,128]{2,1,0:T(4,128)(2,1)} %bitcast.4), calls=%async_computation.1 | async-start | bytes 262144 | tf_op jit(solution)/shard_map/all_to_all | solution.py:408
  40.4 6.4 %upper.1 = (f32[32,64,128]{2,1,0:T(8,128)}, f32[8,128]{1,0:T(8,128)S(1)}) custom-call(f32[32,64,128]{2,1,0:T(8,128)S(1)} %get-tuple-element.21.state_ref, f32[64,128]{1,0:T(8,128)S(1)} %get-tuple-element.22.conduct_ref.after_ref, bf16[272,128]{1,0:T(8,128)(2,1)S(1)} %collective-permute-done.a_ref, bf16[272,128]{1,0:T(8,128)(2,1)S(1)} %collective-permute-done.1.b_ref, ...), custom_call_target="tpu_custom_call" | custom-call | flops 500000000 | bytes 3000000 | tf_op jit(solution)/shard_map/upper/pallas_call | solution.py:466
  46.8 3.5 %all-to-all-done.1 = bf16[128,4,128]{2,1,0:T(4,128)(2,1)S(1)} async-done(((bf16[128,4,128]{2,1,0:T(4,128)(2,1)}), bf16[128,4,128]{2,1,0:T(4,128)(2,1)S(1)}, u32[]{:S(2)}, u32[]{:S(2)}) %all-to-all-start.1) | async-done | bytes 131104 | tf_op jit(solution)/shard_map/all_to_all | solution.py:408
  50.3 4.0 %footprints.1 = (f32[32,128]{1,0:T(8,128)}, bf16[512,128]{1,0:T(8,128)(2,1)}) custom-call(bf16[512,128]{1,0:T(8,128)(2,1)S(1)} %bitcast.10, bf16[512,128]{1,0:T(8,128)(2,1)S(1)} %get-tuple-element.34.placing_ref, f32[8,128]{1,0:T(8,128)S(1)} %get-tuple-element.35.after_ref, f32[32,128]{1,0:T(8,128)} %measured_hbm.1, bf16[32,4,128,128]{3,2,1,0:T(8,128)(2,1)} %weights_ref.1), custom_call_target="tpu_custom_call" | custom-call | flops 20000000 | bytes 5000000 | tf_op jit(solution)/shard_map/footprints/pallas_call | solution.py:475
  54.4 6.3 %all-to-all-start.2 = ((bf16[128,4,128]{2,1,0:T(4,128)(2,1)}), bf16[128,4,128]{2,1,0:T(4,128)(2,1)S(1)}, u32[]{:S(2)}, u32[]{:S(2)}) async-start(bf16[128,4,128]{2,1,0:T(4,128)(2,1)} %bitcast.6), calls=%async_computation.2 | async-start | bytes 262144 | tf_op jit(solution)/shard_map/all_to_all | solution.py:408
  60.6 6.4 %lower.1 = f32[32,64,128]{2,1,0:T(8,128)} custom-call(f32[32,64,128]{2,1,0:T(8,128)S(1)} %get-tuple-element.21.state_ref, f32[64,128]{1,0:T(8,128)S(1)} %get-tuple-element.22.conduct_ref.after_ref, bf16[272,128]{1,0:T(8,128)(2,1)S(1)} %collective-permute-done.a_ref, ...), custom_call_target="tpu_custom_call", output_to_operand_aliasing={{}: (6, {})} | custom-call | flops 500000000 | bytes 3000000 | tf_op jit(solution)/shard_map/lower/pallas_call | solution.py:491
  67.0 3.6 %all-to-all-done.2 = bf16[128,4,128]{2,1,0:T(4,128)(2,1)S(1)} async-done(((bf16[128,4,128]{2,1,0:T(4,128)(2,1)}), bf16[128,4,128]{2,1,0:T(4,128)(2,1)S(1)}, u32[]{:S(2)}, u32[]{:S(2)}) %all-to-all-start.2) | async-done | bytes 131104 | tf_op jit(solution)/shard_map/all_to_all | solution.py:408
  70.6 0.8 %gradient.1 = f32[2,64,128]{2,1,0:T(8,128)} custom-call(bf16[512,128]{1,0:T(8,128)(2,1)S(1)} %bitcast.11, bf16[512,128]{1,0:T(8,128)(2,1)S(1)} %bitcast.9, f32[64,128]{1,0:T(8,128)S(1)} %get-tuple-element.38.adjoint_ref), custom_call_target="tpu_custom_call" | custom-call | flops 20000000 | bytes 400000 | tf_op jit(solution)/shard_map/gradient/pallas_call | solution.py:502
Async XLA Ops:
  0.6 0.7 copy-start
  3.2 17.1 %collective-permute-start = (bf16[272,128]{1,0:T(8,128)(2,1)S(1)}, bf16[272,128]{1,0:T(8,128)(2,1)S(1)}, u32[]{:S(2)}, u32[]{:S(2)}) collective-permute-start(bf16[272,128]{1,0:T(8,128)(2,1)S(1)} %get-tuple-element.23), channel_id=1, source_target_pairs={{0,8},{8,0},{16,24},{24,16},{32,40},{40,32},{48,56},{56,48},{64,72... | collective-permute-start | bytes 208904 | tf_op jit(solution)/shard_map/ppermute | solution.py:404
  5.7 14.6 %collective-permute-start.1 = (bf16[272,128]{1,0:T(8,128)(2,1)S(1)}, bf16[272,128]{1,0:T(8,128)(2,1)S(1)}, u32[]{:S(2)}, u32[]{:S(2)}) collective-permute-start(bf16[272,128]{1,0:T(8,128)(2,1)S(1)} %get-tuple-element.23), channel_id=1, source_target_pairs={{8,16},{24,32},{40,48},{56,64},{72,80},{88,96},{104,112},{16,8},{3... | collective-permute-start | bytes 208904 | tf_op jit(solution)/shard_map/ppermute | solution.py:404
  8.1 22.1 %all-to-all-start = ((bf16[128,4,128]{2,1,0:T(4,128)(2,1)}), bf16[128,4,128]{2,1,0:T(4,128)(2,1)S(1)}, u32[]{:S(2)}, u32[]{:S(2)}) async-start(bf16[128,4,128]{2,1,0:T(4,128)(2,1)} %bitcast.2), calls=%async_computation | async-start | bytes 262144 | tf_op jit(solution)/shard_map/all_to_all | solution.py:408
  21.2 4.5 %collective-permute-start.2 = (bf16[144,128]{1,0:T(8,128)(2,1)S(1)}, bf16[144,128]{1,0:T(8,128)(2,1)S(1)}, u32[]{:S(2)}, u32[]{:S(2)}) collective-permute-start(bf16[144,128]{1,0:T(8,128)(2,1)S(1)} %get-tuple-element.26), channel_id=1, source_target_pairs={{0,1},{1,0},{2,3},{3,2},{4,5},{5,4},{6,7},{7,6},{8,9},{9,8},{10,11... | collective-permute-start | bytes 110600 | tf_op jit(solution)/shard_map/ppermute | solution.py:404
  22.3 5.6 %collective-permute-start.3 = (bf16[144,128]{1,0:T(8,128)(2,1)S(1)}, bf16[144,128]{1,0:T(8,128)(2,1)S(1)}, u32[]{:S(2)}, u32[]{:S(2)}) collective-permute-start(bf16[144,128]{1,0:T(8,128)(2,1)S(1)} %get-tuple-element.27), channel_id=1, source_target_pairs={{1,2},{3,4},{5,6},{2,1},{4,3},{6,5},{9,10},{11,12},{13,14},{10,9},... | collective-permute-start | bytes 110600 | tf_op jit(solution)/shard_map/ppermute | solution.py:404
  34.1 16.2 %all-to-all-start.1 = ((bf16[128,4,128]{2,1,0:T(4,128)(2,1)}), bf16[128,4,128]{2,1,0:T(4,128)(2,1)S(1)}, u32[]{:S(2)}, u32[]{:S(2)}) async-start(bf16[128,4,128]{2,1,0:T(4,128)(2,1)} %bitcast.4), calls=%async_computation.1 | async-start | bytes 262144 | tf_op jit(solution)/shard_map/all_to_all | solution.py:408
  54.4 16.2 %all-to-all-start.2 = ((bf16[128,4,128]{2,1,0:T(4,128)(2,1)}), bf16[128,4,128]{2,1,0:T(4,128)(2,1)S(1)}, u32[]{:S(2)}, u32[]{:S(2)}) async-start(bf16[128,4,128]{2,1,0:T(4,128)(2,1)} %bitcast.6), calls=%async_computation.2 | async-start | bytes 262144 | tf_op jit(solution)/shard_map/all_to_all | solution.py:408

commit v3 on v2

--- a/solution.py
+++ b/solution.py
@@ -53,43 +53,43 @@
 
 
 def prep_body(
-    classes_ref, inflow_hbm, category_hbm, state_hbm, thermal_hbm,
-    state_ref, conduct_ref, edge_ref, thermal_ref, inflow_ref, category_ref, sems,
+    classes_hbm, inflow_hbm, category_hbm, state_hbm, thermal_hbm, slot_hbm, strip_hbm, measured_hbm,
+    state_ref, conduct_ref, edge_ref, thermal_ref, slot_ref, strip_ref, measured_ref,
+    inflow_ref, category_ref, classes_ref, sems,
 ):
-    copies = [
-        pltpu.make_async_copy(category_hbm, category_ref, sems.at[0]),
-        pltpu.make_async_copy(inflow_hbm, inflow_ref, sems.at[1]),
-        pltpu.make_async_copy(state_hbm, state_ref, sems.at[2]),
-        pltpu.make_async_copy(thermal_hbm, thermal_ref, sems.at[3]),
-    ]
+    pairs = (
+        (classes_hbm, classes_ref),
+        (category_hbm, category_ref),
+        (inflow_hbm, inflow_ref),
+        (state_hbm, state_ref),
+        (slot_hbm, slot_ref),
+        (strip_hbm, strip_ref),
+        (thermal_hbm, thermal_ref),
+        (measured_hbm, measured_ref),
+    )
+    copies = [pltpu.make_async_copy(a, b, sems.at[i]) for i, (a, b) in enumerate(pairs)]
     for copy in copies:
         copy.start()
     copies[0].wait()
+    copies[1].wait()
     category = category_ref[...]
     conduct = jnp.zeros((ROWS, COLS), F32)
     for i in range(classes_ref.shape[0]):
         conduct = jnp.where(category == i, classes_ref[i], conduct)
     conduct_ref[...] = conduct
-    copies[1].wait()
     copies[2].wait()
+    copies[3].wait()
     state_ref[0] = state_ref[0] + inflow_ref[...]
     upper = iota((8, COLS), 0) < 4
     edges = jnp.where(upper[None], state_ref[:, 0:8, :], state_ref[:, ROWS - 8 : ROWS, :])
     ends = jnp.where(upper, conduct[0:8], conduct[ROWS - 8 : ROWS])[None]
     whole = jnp.concatenate([edges, ends, jnp.zeros((1, 8, COLS), F32)], axis=0)
     edge_ref[...] = whole.reshape((L + 2) * 8, COLS).astype(BF16)
-    copies[3].wait()
-
-
-def request_body(slot_hbm, strip_hbm, after_ref, placing_ref, request_ref, slot_ref, strip_ref, sems):
-    copies = [
-        pltpu.make_async_copy(slot_hbm, slot_ref, sems.at[0]),
-        pltpu.make_async_copy(strip_hbm, strip_ref, sems.at[1]),
-    ]
-    for copy in copies:
-        copy.start()
-    for copy in copies:
+    for copy in copies[4:]:
         copy.wait()
+
+
+def request_body(slot_ref, strip_ref, after_ref, placing_ref, request_ref):
     tile = jnp.concatenate([slot_ref[k : k + 1, :] for k in range(TOUCH)], axis=1)
     row = jnp.concatenate([strip_ref[k : k + 1, :] for k in range(TOUCH)], axis=1)
     sub = iota((TILES, REFS), 0)
@@ -129,10 +129,10 @@
     return f - pltpu.roll(f, 1, 0)
 
 
-def lanes_change(u, k, cr):
+def lanes_change(u, k, cr, cl):
     ur = pltpu.roll(u, COLS - 1, 1)
-    f = (k + cr * ur) * (ur - u)
-    return f - pltpu.roll(f, 1, 1)
+    ul = pltpu.roll(u, 1, 1)
+    return (k + cr * ur) * (ur - u) - (k + cl * ul) * (u - ul)
 
 
 def pack_body(state_ref, conduct_ref, a_ref, b_ref, own_ref, cond_ref, pa_ref, pb_ref):
@@ -180,7 +180,7 @@
 
 def strip_body(
     own_ref, cond_ref, pa_ref, pb_ref, tops_ref, thermal_ref, picker_ref,
-    left_ref, right_ref, adjoint_ref, served_ref, u_ref, c_ref, cd_ref, cr_ref,
+    left_ref, right_ref, adjoint_ref, served_ref, u_ref, v_ref, c_ref, cd_ref, cr_ref, cl_ref,
 ):
     gy = lax.axis_index("gy")
     odd = lax.rem(gy, 2)
@@ -193,6 +193,7 @@
     last = lax.rem(lane, 4) == 3
     first = lax.rem(lane, 4) == 0
     lowest = lane >= COLS - 4
+    highest = lane < 4
     inside = halo_rows_inside()
     in_left = (jnp.zeros((WIDE, COLS), jnp.int32) + gy) > 0
     in_right = (jnp.zeros((WIDE, COLS), jnp.int32) + gy) < lax.axis_size("gy") - 1
@@ -210,38 +211,35 @@
 
     def next_of(ref, i):
         x = pltpu.roll(ref[i], COLS - 1, 1)
-        y = pltpu.roll(ref[min(i + 1, i // 3 * 3 + 2)], 3, 1)
-        return jnp.where(last, y, x)
+        return jnp.where(last, pltpu.roll(ref[i + 1], 3, 1), x) if i % 3 < 2 else x
+
+    def prior_of(ref, i):
+        x = pltpu.roll(ref[i], 1, 1)
+        return jnp.where(first, pltpu.roll(ref[i - 1], COLS - 3, 1), x) if i % 3 else x
 
     for i in range(6):
         cd_ref[i] = pltpu.roll(c_ref[i], WIDE - 1, 0)
         cr_ref[i] = next_of(c_ref, i)
+        cl_ref[i] = prior_of(c_ref, i)
 
     for step in range(STEPS):
-        fresh = []
-        flux = None
+        now, then = (u_ref, v_ref) if step % 2 == 0 else (v_ref, u_ref)
         for i in range(6):
-            u, c = u_ref[i], c_ref[i]
+            u, c = now[i], c_ref[i]
             k = c * u
+            ur, ul = next_of(now, i), prior_of(now, i)
+            uz, ua = pltpu.roll(u, COLS - 4, 1), pltpu.roll(u, 4, 1)
             change = rows_change(u, k, cd_ref[i])
-            ur = next_of(u_ref, i)
-            f = (k + cr_ref[i] * ur) * (ur - u)
-            before = pltpu.roll(f, 1, 1)
-            if i % 3:
-                before = jnp.where(first, pltpu.roll(flux, COLS - 3, 1), before)
-            flux = f
-            change = change + (f - before)
-            uz = pltpu.roll(u, COLS - 4, 1)
-            down = jnp.where(lowest, 0.0, (k + c * uz) * ((u - uz) + 0.3))
-            change = change + (pltpu.roll(down, 4, 1) - down)
+            change = change + ((k + cr_ref[i] * ur) * (ur - u) - (k + cl_ref[i] * ul) * (u - ul))
+            down = (k + c * uz) * ((u - uz) + 0.3)
+            fall = (c * ua + k) * ((ua - u) + 0.3)
+            change = change + (jnp.where(highest, 0.0, fall) - jnp.where(lowest, 0.0, down))
             new = held(u + change, inside)
             if i == 0:
                 new = jnp.where(in_left, new, 0.5)
             if i == 5:
                 new = jnp.where(in_right, new, 0.5)
-            fresh.append(new)
-        for i in range(6):
-            u_ref[i] = fresh[i]
+            then[i] = new
     left = u_ref[1][:ROWS] - 0.5
     right = u_ref[4][:ROWS] - 0.5
     left_ref[...] = left
@@ -265,12 +263,16 @@
     return 0.5 * jnp.concatenate([conduct_ref[...], halo[L]], axis=0)
 
 
+NEAR = 12
+
+
 def evolve(state_ref, conduct_ref, a_ref, b_ref, u_ref, c_ref, low, high, finish):
     halo = row_halo(a_ref, b_ref)
     c = wide_conduct(conduct_ref, halo)
     c_ref[0] = c
     c_ref[1] = pltpu.roll(c, WIDE - 1, 0)
     c_ref[2] = pltpu.roll(c, COLS - 1, 1)
+    c_ref[3] = pltpu.roll(c, 1, 1)
     inside = halo_rows_inside()
     start, stop = max(0, low - STEPS), min(L, high + STEPS)
     for l in range(start, stop):
@@ -285,7 +287,7 @@
         u = u_ref[top - start]
         k = c_ref[0] * u
         for l in range(top, end):
-            change = rows_change(u, k, c_ref[1]) + lanes_change(u, k, c_ref[2])
+            change = rows_change(u, k, c_ref[1]) + lanes_change(u, k, c_ref[2], c_ref[3])
             if above is not None:
                 change = change + above
             if l < L - 1:
@@ -312,7 +314,7 @@
 PIECE = 4
 
 
-def half_body(low, state_ref, conduct_ref, a_ref, b_ref, left_ref, right_ref, out_hbm, done_ref, u_ref, c_ref, own_ref, sems):
+def half_body(low, state_ref, conduct_ref, a_ref, b_ref, left_ref, right_ref, out_hbm, u_ref, c_ref, own_ref, sems):
     lane = iota((ROWS, COLS), 1)
     copies = []
 
@@ -330,63 +332,75 @@
             copies.append(copy)
 
     evolve(state_ref, conduct_ref, a_ref, b_ref, u_ref, c_ref, low, low + HALF, finish)
-    if done_ref is not None:
-        done_ref[...] = jnp.zeros(done_ref.shape, F32)
     for copy in copies:
         copy.wait()
 
 
-def upper_body(state_ref, conduct_ref, a_ref, b_ref, left_ref, right_ref, out_hbm, done_ref, *scratch):
-    half_body(0, state_ref, conduct_ref, a_ref, b_ref, left_ref, right_ref, out_hbm, done_ref, *scratch)
-
-
-def lower_body(state_ref, conduct_ref, a_ref, b_ref, left_ref, right_ref, begun_hbm, out_hbm, *scratch):
-    half_body(HALF, state_ref, conduct_ref, a_ref, b_ref, left_ref, right_ref, out_hbm, None, *scratch)
+def upper_body(
+    state_ref, conduct_ref, a_ref, b_ref, left_ref, right_ref, weights_hbm, out_hbm, weights_ref, *scratch
+):
+    copy = pltpu.make_async_copy(weights_hbm.at[pl.ds(0, NEAR)], weights_ref, scratch[-1])
+    copy.start()
+    half_body(0, state_ref, conduct_ref, a_ref, b_ref, left_ref, right_ref, out_hbm, *scratch[:-1])
+    copy.wait()
+
+
+def lower_body(
+    state_hbm, conduct_ref, a_ref, b_ref, left_ref, right_ref, begun_hbm, out_hbm, *scratch
+):
+    state_ref, sem = scratch[-2:]
+    span = pl.ds(HALF - STEPS, L - HALF + STEPS)
+    copy = pltpu.make_async_copy(state_hbm.at[span], state_ref.at[span], sem)
+    copy.start()
+    copy.wait()
+    half_body(HALF, state_ref, conduct_ref, a_ref, b_ref, left_ref, right_ref, out_hbm, *scratch[:-2])
+
+
+PART = 4
 
 
 def foot_body(
-    returned_ref, placing_ref, after_ref, measured_hbm, weights_ref,
-    bright_ref, outgoing_ref, measured_ref, held_ref, cells_ref, seen_ref, misfit_ref, contrib_ref, sems,
+    returned_ref, placing_ref, seen_ref, near_ref, weights_hbm,
+    bright_ref, outgoing_ref, cells_ref, contrib_ref, weights_ref, sems,
 ):
-    parts = 8
-    each = OWN // parts
-    seen_copy = pltpu.make_async_copy(measured_hbm, measured_ref, sems.at[parts])
-    seen_copy.start()
-    copies = [
-        pltpu.make_async_copy(
-            weights_ref.at[pl.ds(p * each, each)], held_ref.at[pl.ds(p * each, each)], sems.at[p]
+    copies = {}
+    for start in range(NEAR, OWN, PART):
+        span = pl.ds(start, PART)
+        copies[start] = pltpu.make_async_copy(
+            weights_hbm.at[span], weights_ref.at[span], sems.at[start // PART]
         )
-        for p in range(parts)
-    ]
-    for copy in copies:
-        copy.start()
+        copies[start].start()
     placing = placing_ref[...]
     cells_ref[...] = dot(placing, returned_ref[...], 0, 0)
-    seen_copy.wait()
-    seen = jnp.concatenate([measured_ref[...], jnp.zeros((COLS - OWN, FOOT), F32)], axis=0)
-    seen_ref[...] = jnp.transpose(seen)
-    misfit_ref[...] = jnp.zeros((FOOT, COLS), F32)
     lane = iota((FOOT, COLS), 1)
 
-    def block(b, carry):
-        total = jnp.where(lane == b, -seen_ref[...], 0.0)
-        for k in range(TOUCH):
-            total = total + held_ref[b, k].astype(F32) * cells_ref[pl.ds(k * OWN + b, 1), :]
-        misfit = jnp.sum(total, axis=1, keepdims=True)
-        misfit_ref[...] = jnp.where(lane == b, misfit, misfit_ref[...])
-        rounded = misfit.astype(BF16).astype(F32)
-        for k in range(TOUCH):
-            contrib_ref[pl.ds(k * OWN + b, 1), :] = jnp.sum(
-                held_ref[b, k].astype(F32) * rounded, axis=0, keepdims=True
-            )
-        return carry
-
-    for p in range(parts):
-        copies[p].wait()
-        for b in range(p * each, (p + 1) * each):
-            block(b, 0)
-    evolved = jnp.transpose(misfit_ref[...] + seen_ref[...])
-    bright_ref[...] = evolved[:OWN]
+    def weights(b, k):
+        return near_ref[b, k] if b < NEAR else weights_ref[b, k]
+
+    def adjoint(start, misfit):
+        for i in range(PART):
+            for k in range(TOUCH):
+                at = k * OWN + start + i
+                contrib_ref[at : at + 1, :] = dot(misfit[i : i + 1], weights(start + i, k), 1, 0)
+
+    misfit = None
+    for start in range(0, OWN, PART):
+        if start in copies:
+            copies[start].wait()
+        sums = jnp.zeros((FOOT, COLS), F32)
+        for i in range(PART):
+            total = None
+            for k in range(TOUCH):
+                at = k * OWN + start + i
+                term = weights(start + i, k).astype(F32) * cells_ref[at : at + 1, :]
+                total = term if total is None else total + term
+            sums = jnp.where(lane == i, jnp.sum(total, axis=1, keepdims=True), sums)
+        if start:
+            adjoint(start - PART, misfit)
+        evolved = jnp.transpose(sums)[:PART]
+        bright_ref[start : start + PART, :] = evolved
+        misfit = (evolved - seen_ref[start : start + PART, :]).astype(BF16)
+    adjoint(OWN - PART, misfit)
     outgoing_ref[...] = dot(placing, contrib_ref[...].astype(BF16), 1, 0).astype(BF16)
 
 
@@ -414,23 +428,30 @@
     def sds(*shape, dtype=F32):
         return jax.ShapeDtypeStruct(shape, dtype)
 
-    held_state, conduct, edge, warm = call(
+    held_state, conduct, edge, warm, slot_ids, strip_ids, seen = call(
         prep_body,
-        (sds(L, ROWS, COLS), sds(ROWS, COLS), sds((L + 2) * 8, COLS, dtype=BF16), sds(ROWS, COLS)),
-        [SMEM, HBM, HBM, HBM, HBM],
+        (
+            sds(L, ROWS, COLS), sds(ROWS, COLS), sds((L + 2) * 8, COLS, dtype=BF16), sds(ROWS, COLS),
+            sds(TOUCH, OWN, dtype=jnp.int32), sds(TOUCH, OWN, dtype=jnp.int32), sds(OWN, FOOT),
+        ),
+        [HBM] * 8,
         "prep",
-        [pltpu.VMEM((ROWS, COLS), F32), pltpu.VMEM((ROWS, COLS), jnp.int32), pltpu.SemaphoreType.DMA((4,))],
+        [
+            pltpu.VMEM((ROWS, COLS), F32),
+            pltpu.VMEM((ROWS, COLS), jnp.int32),
+            pltpu.SMEM(classes.shape, F32),
+            pltpu.SemaphoreType.DMA((8,)),
+        ],
         flops=1_000_000, moved=2_000_000,
-    )(classes, far(inflow), far(category), far(state), far(thermal))
+    )(*(far(x) for x in (classes, inflow, category, state, thermal, slots.T, strips.T, measured)))
     xa, xb = swapped((edge, edge), "gx")
     placing, request = call(
         request_body,
         (sds(SLOTS, REFS, dtype=BF16), sds(SLOTS, COLS, dtype=BF16)),
-        [HBM, HBM, ANY],
+        [VMEM, VMEM, ANY],
         "requests",
-        [pltpu.VMEM((TOUCH, OWN), jnp.int32), pltpu.VMEM((TOUCH, OWN), jnp.int32), pltpu.SemaphoreType.DMA((2,))],
         flops=20_000_000, moved=500_000,
-    )(far(slots.T), far(strips.T), conduct)
+    )(slot_ids, strip_ids, conduct)
     picker = exchange(request)
     own, cond, pa, pb = call(
         pack_body,
@@ -445,7 +466,7 @@
         sds(2, ROWS, COLS),
         [VMEM] * 4,
         "tops",
-        [pltpu.VMEM((STEPS + 2, WIDE, COLS), F32), pltpu.VMEM((3, WIDE, COLS), F32)],
+        [pltpu.VMEM((STEPS + 2, WIDE, COLS), F32), pltpu.VMEM((4, WIDE, COLS), F32)],
         flops=20_000_000_000, moved=1_000_000,
     )(held_state, conduct, xa, xb)
     left, right, adjoint, served = call(
@@ -453,51 +474,48 @@
         (sds(ROWS, COLS), sds(ROWS, COLS), sds(ROWS, COLS), sds(SLOTS, COLS, dtype=BF16)),
         [VMEM] * 7,
         "strips",
-        [pltpu.VMEM((6, WIDE, COLS), F32)] * 4,
+        [pltpu.VMEM((6, WIDE, COLS), F32)] * 6,
         flops=20_000_000, moved=1_000_000,
     )(own, cond, ya, yb, tops, warm, picker)
     returned = exchange(served)
     scratch = [
         pltpu.VMEM((HALF + STEPS, WIDE, COLS), F32),
-        pltpu.VMEM((3, WIDE, COLS), F32),
+        pltpu.VMEM((4, WIDE, COLS), F32),
         pltpu.VMEM((HALF, ROWS, COLS), F32),
         pltpu.SemaphoreType.DMA((HALF // PIECE,)),
     ]
-    begun, done = call(
+    begun, near = call(
         upper_body,
-        (sds(L, ROWS, COLS), sds(8, COLS)),
-        [VMEM] * 6,
+        (sds(L, ROWS, COLS), sds(NEAR, TOUCH, FOOT, COLS, dtype=BF16)),
+        [VMEM] * 6 + [HBM],
         "upper",
-        scratch,
+        scratch + [pltpu.SemaphoreType.DMA],
         out_specs=(HBM, VMEM),
         flops=500_000_000, moved=3_000_000,
-    )(held_state, conduct, xa, xb, left, right)
+    )(held_state, conduct, xa, xb, left, right, far(weights))
     brightness, outgoing = call(
         foot_body,
         (sds(OWN, FOOT), sds(SLOTS, COLS, dtype=BF16)),
-        [VMEM, VMEM, ANY, HBM, HBM],
+        [VMEM] * 4 + [HBM],
         "footprints",
         [
-            pltpu.VMEM((OWN, FOOT), F32),
-            pltpu.VMEM((OWN, TOUCH, FOOT, COLS), BF16),
             pltpu.VMEM((REFS, COLS), F32),
-            pltpu.VMEM((FOOT, COLS), F32),
-            pltpu.VMEM((FOOT, COLS), F32),
             pltpu.VMEM((REFS, COLS), F32),
-            pltpu.SemaphoreType.DMA((9,)),
+            pltpu.VMEM(weights.shape, BF16),
+            pltpu.SemaphoreType.DMA((OWN // PART,)),
         ],
         flops=20_000_000, moved=5_000_000,
-    )(returned, placing, done, far(measured), far(weights))
+    )(returned, placing, seen, near, far(weights))
     moisture = call(
         lower_body,
         sds(L, ROWS, COLS),
-        [VMEM] * 6 + [HBM],
+        [HBM] + [VMEM] * 5 + [HBM],
         "lower",
-        scratch,
+        scratch + [pltpu.VMEM((L, ROWS, COLS), F32), pltpu.SemaphoreType.DMA],
         out_specs=HBM,
         aliases={6: 0},
         flops=500_000_000, moved=3_000_000,
-    )(held_state, conduct, xa, xb, left, right, begun)
+    )(far(state), conduct, xa, xb, left, right, begun)
     grads = exchange(outgoing)
     grad_top = call(
         gradient_body, sds(2, ROWS, COLS), [VMEM] * 3, "gradient", flops=20_000_000, moved=400_000

time: 71.8 us -> 66.2 us (0.922)
  Pallas kernels: 26.8 us -> 19.1 us
  waiting for transfers between devices: 11.7 us -> 16.2 us
  starting transfers between devices: 31.6 us -> 29.8 us
    pallas_call x3, Pallas kernels: 16.9 us -> 12 us  [the longest x1 4.32 us: on_device(): call(lower_body, sds(L, ROWS, COLS), [HBM] + [VMEM] * 5 + [HBM], 'lower',...]
    all_to_all x3, starting transfers between devices: 24.6 us -> 19.9 us  [exchange(): lax.all_to_all(x.reshape(TILES, CAP, COLS), ('gx', 'gy'), split_axis=0, c...]
    all_to_all x3, waiting for transfers between devices: 9.42 us -> 13.8 us  [exchange(): lax.all_to_all(x.reshape(TILES, CAP, COLS), ('gx', 'gy'), split_axis=0, c...]
    ppermute x4, starting transfers between devices: 6.96 us -> 9.85 us  [swapped(): return (lax.ppermute(x[0], axis, one), lax.ppermute(x[1], axis, two))]
    pallas_call x1, Pallas kernels: 3.9 us -> 2.35 us  [on_device(): call(strip_body, (sds(ROWS, COLS), sds(ROWS, COLS), sds(ROWS, COLS), sds(...]
    pallas_call x1, Pallas kernels: 1.76 us -> 1.04 us  [on_device(): call(request_body, (sds(SLOTS, REFS, dtype=BF16), sds(SLOTS, COLS, dtype=...]
  transfers between devices with their start and end apart: 7 -> 7, of which waited for: 4 -> 4; matrix products, arithmetic and copies ran while one was open for 0% -> 0% of each run, Pallas kernels for 23% -> 17%
where the time goes in v3:
time: 66.2 us; the launch traced here: 65.8 us
  starting transfers between devices  29.8 us (45%)
  Pallas kernels  19.1 us (29%)
  waiting for transfers between devices  16.2 us (24%)
  between operations  0.74 us (1%)
    all_to_all x3, starting transfers between devices, exchange(): lax.all_to_all(x.reshape(TILES, CAP, COLS), ('gx', 'gy'), split_axis=0, c...  19.9 us
    all_to_all x3, waiting for transfers between devices, exchange(): lax.all_to_all(x.reshape(TILES, CAP, COLS), ('gx', 'gy'), split_axis=0, c...  13.8 us
    ppermute x4, starting transfers between devices, swapped(): return (lax.ppermute(x[0], axis, one), lax.ppermute(x[1], axis, two))  9.85 us
    pallas_call x1, Pallas kernels, on_device(): call(lower_body, sds(L, ROWS, COLS), [HBM] + [VMEM] * 5 + [HBM], 'lower',...  4.32 us
    pallas_call x1, Pallas kernels, on_device(): call(upper_body, (sds(L, ROWS, COLS), sds(NEAR, TOUCH, FOOT, COLS, dtype=...  4.12 us
    pallas_call x1, Pallas kernels, on_device(): call(foot_body, (sds(OWN, FOOT), sds(SLOTS, COLS, dtype=BF16)), [VMEM] *...  3.6 us
    ppermute x4, waiting for transfers between devices, swapped(): return (lax.ppermute(x[0], axis, one), lax.ppermute(x[1], axis, two))  2.37 us
    pallas_call x1, Pallas kernels, on_device(): call(strip_body, (sds(ROWS, COLS), sds(ROWS, COLS), sds(ROWS, COLS), sds(...  2.35 us
  transfers between devices with their start and end apart: 7, of which 4 were waited for; matrix products, arithmetic and copies ran while one was open for 0% of the time, Pallas kernels for 17%

profile of v3, /device:TPU:1, one launch (start us, length us, event | category | flops | bytes accessed | tf_op | source)
XLA Modules:
  0.0 65.8 jit_solution(2993324525014471213)
XLA Ops:
  0.6 1.4 %prep.1 = (f32[32,64,128]{2,1,0:T(8,128)S(1)}, f32[64,128]{1,0:T(8,128)S(1)}, bf16[272,128]{1,0:T(8,128)(2,1)S(1)}, f32[64,128]{1,0:T(8,128)S(1)}, s32[4,32]{1,0...) custom-call(f32[12]{0:T(128)} %classes_hbm.1, f32[64,128]{1,0:T(8,128)} %inflow_hbm.1, s32[64,128]{1,0:T(8,128)} %category_hbm.1, ...), custom_call_target="tpu_custom_call" | custom-call | flops 1000000 | bytes 2000000 | tf_op jit(solution)/shard_map/prep/pallas_call | solution.py:431
  2.0 0.7 %collective-permute-start.1 = (bf16[272,128]{1,0:T(8,128)(2,1)S(1)}, bf16[272,128]{1,0:T(8,128)(2,1)S(1)}, u32[]{:S(2)}, u32[]{:S(2)}) collective-permute-start(bf16[272,128]{1,0:T(8,128)(2,1)S(1)} %get-tuple-element.25), channel_id=1, source_target_pairs={{8,16},{24,32},{40,48},{56,64},{72,80},{88,96},{104,112},{16,8},{3... | collective-permute-start | bytes 208904 | tf_op jit(solution)/shard_map/ppermute | solution.py:418
  2.7 5.4 %collective-permute-start = (bf16[272,128]{1,0:T(8,128)(2,1)S(1)}, bf16[272,128]{1,0:T(8,128)(2,1)S(1)}, u32[]{:S(2)}, u32[]{:S(2)}) collective-permute-start(bf16[272,128]{1,0:T(8,128)(2,1)S(1)} %get-tuple-element.25), channel_id=1, source_target_pairs={{0,8},{8,0},{16,24},{24,16},{32,40},{40,32},{48,56},{56,48},{64,72... | collective-permute-start | bytes 208904 | tf_op jit(solution)/shard_map/ppermute | solution.py:418
  8.1 1.0 %requests.1 = (bf16[512,128]{1,0:T(8,128)(2,1)S(1)}, bf16[512,128]{1,0:T(8,128)(2,1)}) custom-call(s32[4,32]{1,0:T(4,128)S(1)} %get-tuple-element.32.slot_ref, s32[4,32]{1,0:T(4,128)S(1)} %get-tuple-element.33.strip_ref, f32[64,128]{1,0:T(8,128)S(1)} %get-tuple-element.24.conduct_ref.after_ref), custom_call_target="tpu_custom_call" | custom-call | flops 20000000 | bytes 500000 | tf_op jit(solution)/shard_map/requests/pallas_call | solution.py:448
  9.1 9.4 %all-to-all-start = ((bf16[128,4,128]{2,1,0:T(4,128)(2,1)}), bf16[128,4,128]{2,1,0:T(4,128)(2,1)S(1)}, u32[]{:S(2)}, u32[]{:S(2)}) async-start(bf16[128,4,128]{2,1,0:T(4,128)(2,1)} %bitcast.2), calls=%async_computation | async-start | bytes 262144 | tf_op jit(solution)/shard_map/all_to_all | solution.py:422
  18.6 0.0 collective-permute-done.1.b_ref
  18.6 0.0 collective-permute-done.a_ref
  18.6 0.9 %pack.1 = (f32[4,72,128]{2,1,0:T(8,128)S(1)}, f32[4,72,128]{2,1,0:T(8,128)S(1)}, bf16[144,128]{1,0:T(8,128)(2,1)S(1)}, bf16[144,128]{1,0:T(8,128)(2,1)S(1)}) custom-call(f32[32,64,128]{2,1,0:T(8,128)S(1)} %get-tuple-element.26.state_ref, f32[64,128]{1,0:T(8,128)S(1)} %get-tuple-element.24.conduct_ref.after_ref, ...), custom_call_target="tpu_custom_call" | custom-call | flops 20000000000 | bytes 1500000 | tf_op jit(solution)/shard_map/pack/pallas_call | solution.py:456
  19.5 1.1 %collective-permute-start.2 = (bf16[144,128]{1,0:T(8,128)(2,1)S(1)}, bf16[144,128]{1,0:T(8,128)(2,1)S(1)}, u32[]{:S(2)}, u32[]{:S(2)}) collective-permute-start(bf16[144,128]{1,0:T(8,128)(2,1)S(1)} %get-tuple-element.29), channel_id=1, source_target_pairs={{0,1},{1,0},{2,3},{3,2},{4,5},{5,4},{6,7},{7,6},{8,9},{9,8},{10,11... | collective-permute-start | bytes 110600 | tf_op jit(solution)/shard_map/ppermute | solution.py:418
  20.6 2.6 %collective-permute-start.3 = (bf16[144,128]{1,0:T(8,128)(2,1)S(1)}, bf16[144,128]{1,0:T(8,128)(2,1)S(1)}, u32[]{:S(2)}, u32[]{:S(2)}) collective-permute-start(bf16[144,128]{1,0:T(8,128)(2,1)S(1)} %get-tuple-element.30), channel_id=1, source_target_pairs={{1,2},{3,4},{5,6},{2,1},{4,3},{6,5},{9,10},{11,12},{13,14},{10,9},... | collective-permute-start | bytes 110600 | tf_op jit(solution)/shard_map/ppermute | solution.py:418
  23.3 0.6 tops.1.tops_ref
  23.8 0.0 collective-permute-done.2.pa_ref
  23.8 2.4 %collective-permute-done.3.pb_ref = bf16[144,128]{1,0:T(8,128)(2,1)S(1)} collective-permute-done((bf16[144,128]{1,0:T(8,128)(2,1)S(1)}, bf16[144,128]{1,0:T(8,128)(2,1)S(1)}, u32[]{:S(2)}, u32[]{:S(2)}) %collective-permute-start.3) | collective-permute-done | bytes 36896 | tf_op jit(solution)/shard_map/ppermute | solution.py:418
  26.2 2.3 %all-to-all-done = bf16[128,4,128]{2,1,0:T(4,128)(2,1)S(1)} async-done(((bf16[128,4,128]{2,1,0:T(4,128)(2,1)}), bf16[128,4,128]{2,1,0:T(4,128)(2,1)S(1)}, u32[]{:S(2)}, u32[]{:S(2)}) %all-to-all-start) | async-done | bytes 131104 | tf_op jit(solution)/shard_map/all_to_all | solution.py:422
  28.5 2.4 %strips.1 = (f32[64,128]{1,0:T(8,128)S(1)}, f32[64,128]{1,0:T(8,128)S(1)}, f32[64,128]{1,0:T(8,128)S(1)}, bf16[512,128]{1,0:T(8,128)(2,1)}) custom-call(f32[4,72,128]{2,1,0:T(8,128)S(1)} %get-tuple-element.27.own_ref, f32[4,72,128]{2,1,0:T(8,128)S(1)} %get-tuple-element.28.cond_ref, bf16[144,128]{1,0:T(8,128)(2,1)S(1)} %collective-permute-done.2.pa_ref, ...), custom_call_target="tpu_custom_call" | custom-call | flops 20000000 | bytes 1000000 | tf_op jit(solution)/shard_map/strips/pallas_call | solution.py:472
  30.9 6.2 %all-to-all-start.1 = ((bf16[128,4,128]{2,1,0:T(4,128)(2,1)}), bf16[128,4,128]{2,1,0:T(4,128)(2,1)S(1)}, u32[]{:S(2)}, u32[]{:S(2)}) async-start(bf16[128,4,128]{2,1,0:T(4,128)(2,1)} %bitcast.4), calls=%async_computation.1 | async-start | bytes 262144 | tf_op jit(solution)/shard_map/all_to_all | solution.py:422
  37.1 4.1 %upper.1 = (f32[32,64,128]{2,1,0:T(8,128)}, bf16[12,4,128,128]{3,2,1,0:T(8,128)(2,1)S(1)}) custom-call(f32[32,64,128]{2,1,0:T(8,128)S(1)} %get-tuple-element.26.state_ref, f32[64,128]{1,0:T(8,128)S(1)} %get-tuple-element.24.conduct_ref.after_ref, bf16[272,128]{1,0:T(8,128)(2,1)S(1)} %collective-permute-done.a_ref, ...), custom_call_target="tpu_custom_call" | custom-call | flops 500000000 | bytes 3000000 | tf_op jit(solution)/shard_map/upper/pallas_call | solution.py:487
  41.3 5.8 %all-to-all-done.1 = bf16[128,4,128]{2,1,0:T(4,128)(2,1)S(1)} async-done(((bf16[128,4,128]{2,1,0:T(4,128)(2,1)}), bf16[128,4,128]{2,1,0:T(4,128)(2,1)S(1)}, u32[]{:S(2)}, u32[]{:S(2)}) %all-to-all-start.1) | async-done | bytes 131104 | tf_op jit(solution)/shard_map/all_to_all | solution.py:422
  47.1 3.6 %footprints.1 = (f32[32,128]{1,0:T(8,128)}, bf16[512,128]{1,0:T(8,128)(2,1)}) custom-call(bf16[512,128]{1,0:T(8,128)(2,1)S(1)} %bitcast.10, bf16[512,128]{1,0:T(8,128)(2,1)S(1)} %get-tuple-element.39.placing_ref, f32[32,128]{1,0:T(8,128)S(1)} %get-tuple-element.40.seen_ref, bf16[12,4,128,128]{3,2,1,0:T(8,128)(2,1)S(1)} %get-tuple-element.41.near_ref, ...), custom_call_target="tpu_custom_call" | custom-call | flops 20000000 | bytes 5000000 | tf_op jit(solution)/shard_map/footprints/pallas_call | solution.py:496
  50.7 4.3 %all-to-all-start.2 = ((bf16[128,4,128]{2,1,0:T(4,128)(2,1)}), bf16[128,4,128]{2,1,0:T(4,128)(2,1)S(1)}, u32[]{:S(2)}, u32[]{:S(2)}) async-start(bf16[128,4,128]{2,1,0:T(4,128)(2,1)} %bitcast.6), calls=%async_computation.2 | async-start | bytes 262144 | tf_op jit(solution)/shard_map/all_to_all | solution.py:422
  55.0 4.3 %lower.1 = f32[32,64,128]{2,1,0:T(8,128)} custom-call(f32[32,64,128]{2,1,0:T(8,128)} %state_hbm.3, f32[64,128]{1,0:T(8,128)S(1)} %get-tuple-element.24.conduct_ref.after_ref, bf16[272,128]{1,0:T(8,128)(2,1)S(1)} %collective-permute-done.a_ref, bf16[272,128]{1,0:T(8,128)(2,1)S(1)} %collective-permute-done.1.b_ref, ...), custom_call_target="tpu_custom_call", output_to_operand_aliasing={{}: (6, {})} | custom-call | flops 500000000 | bytes 3000000 | tf_op jit(solution)/shard_map/lower/pallas_call | solution.py:509
  59.3 5.6 %all-to-all-done.2 = bf16[128,4,128]{2,1,0:T(4,128)(2,1)S(1)} async-done(((bf16[128,4,128]{2,1,0:T(4,128)(2,1)}), bf16[128,4,128]{2,1,0:T(4,128)(2,1)S(1)}, u32[]{:S(2)}, u32[]{:S(2)}) %all-to-all-start.2) | async-done | bytes 131104 | tf_op jit(solution)/shard_map/all_to_all | solution.py:422
  65.0 0.8 %gradient.1 = f32[2,64,128]{2,1,0:T(8,128)} custom-call(bf16[512,128]{1,0:T(8,128)(2,1)S(1)} %bitcast.11, bf16[512,128]{1,0:T(8,128)(2,1)S(1)} %bitcast.9, f32[64,128]{1,0:T(8,128)S(1)} %get-tuple-element.44.adjoint_ref), custom_call_target="tpu_custom_call" | custom-call | flops 20000000 | bytes 400000 | tf_op jit(solution)/shard_map/gradient/pallas_call | solution.py:520
Async XLA Ops:
  2.0 16.6 %collective-permute-start.1 = (bf16[272,128]{1,0:T(8,128)(2,1)S(1)}, bf16[272,128]{1,0:T(8,128)(2,1)S(1)}, u32[]{:S(2)}, u32[]{:S(2)}) collective-permute-start(bf16[272,128]{1,0:T(8,128)(2,1)S(1)} %get-tuple-element.25), channel_id=1, source_target_pairs={{8,16},{24,32},{40,48},{56,64},{72,80},{88,96},{104,112},{16,8},{3... | collective-permute-start | bytes 208904 | tf_op jit(solution)/shard_map/ppermute | solution.py:418
  2.7 15.9 %collective-permute-start = (bf16[272,128]{1,0:T(8,128)(2,1)S(1)}, bf16[272,128]{1,0:T(8,128)(2,1)S(1)}, u32[]{:S(2)}, u32[]{:S(2)}) collective-permute-start(bf16[272,128]{1,0:T(8,128)(2,1)S(1)} %get-tuple-element.25), channel_id=1, source_target_pairs={{0,8},{8,0},{16,24},{24,16},{32,40},{40,32},{48,56},{56,48},{64,72... | collective-permute-start | bytes 208904 | tf_op jit(solution)/shard_map/ppermute | solution.py:418
  9.1 19.4 %all-to-all-start = ((bf16[128,4,128]{2,1,0:T(4,128)(2,1)}), bf16[128,4,128]{2,1,0:T(4,128)(2,1)S(1)}, u32[]{:S(2)}, u32[]{:S(2)}) async-start(bf16[128,4,128]{2,1,0:T(4,128)(2,1)} %bitcast.2), calls=%async_computation | async-start | bytes 262144 | tf_op jit(solution)/shard_map/all_to_all | solution.py:422
  19.5 4.3 %collective-permute-start.2 = (bf16[144,128]{1,0:T(8,128)(2,1)S(1)}, bf16[144,128]{1,0:T(8,128)(2,1)S(1)}, u32[]{:S(2)}, u32[]{:S(2)}) collective-permute-start(bf16[144,128]{1,0:T(8,128)(2,1)S(1)} %get-tuple-element.29), channel_id=1, source_target_pairs={{0,1},{1,0},{2,3},{3,2},{4,5},{5,4},{6,7},{7,6},{8,9},{9,8},{10,11... | collective-permute-start | bytes 110600 | tf_op jit(solution)/shard_map/ppermute | solution.py:418
  20.6 5.6 %collective-permute-start.3 = (bf16[144,128]{1,0:T(8,128)(2,1)S(1)}, bf16[144,128]{1,0:T(8,128)(2,1)S(1)}, u32[]{:S(2)}, u32[]{:S(2)}) collective-permute-start(bf16[144,128]{1,0:T(8,128)(2,1)S(1)} %get-tuple-element.30), channel_id=1, source_target_pairs={{1,2},{3,4},{5,6},{2,1},{4,3},{6,5},{9,10},{11,12},{13,14},{10,9},... | collective-permute-start | bytes 110600 | tf_op jit(solution)/shard_map/ppermute | solution.py:418
  30.9 16.2 %all-to-all-start.1 = ((bf16[128,4,128]{2,1,0:T(4,128)(2,1)}), bf16[128,4,128]{2,1,0:T(4,128)(2,1)S(1)}, u32[]{:S(2)}, u32[]{:S(2)}) async-start(bf16[128,4,128]{2,1,0:T(4,128)(2,1)} %bitcast.4), calls=%async_computation.1 | async-start | bytes 262144 | tf_op jit(solution)/shard_map/all_to_all | solution.py:422
  50.7 14.3 %all-to-all-start.2 = ((bf16[128,4,128]{2,1,0:T(4,128)(2,1)}), bf16[128,4,128]{2,1,0:T(4,128)(2,1)S(1)}, u32[]{:S(2)}, u32[]{:S(2)}) async-start(bf16[128,4,128]{2,1,0:T(4,128)(2,1)} %bitcast.6), calls=%async_computation.2 | async-start | bytes 262144 | tf_op jit(solution)/shard_map/all_to_all | solution.py:422

commit v4 on v3

--- a/solution.py
+++ b/solution.py
@@ -54,16 +54,16 @@
 
 def prep_body(
     classes_hbm, inflow_hbm, category_hbm, state_hbm, thermal_hbm, slot_hbm, strip_hbm, measured_hbm,
-    state_ref, conduct_ref, edge_ref, thermal_ref, slot_ref, strip_ref, measured_ref,
-    inflow_ref, category_ref, classes_ref, sems,
+    state_ref, conduct_ref, edge_ref, thermal_ref, measured_ref, placing_ref, request_ref,
+    inflow_ref, category_ref, classes_ref, slot_ref, strip_ref, sems,
 ):
     pairs = (
+        (slot_hbm, slot_ref),
+        (strip_hbm, strip_ref),
         (classes_hbm, classes_ref),
         (category_hbm, category_ref),
         (inflow_hbm, inflow_ref),
         (state_hbm, state_ref),
-        (slot_hbm, slot_ref),
-        (strip_hbm, strip_ref),
         (thermal_hbm, thermal_ref),
         (measured_hbm, measured_ref),
     )
@@ -72,24 +72,6 @@
         copy.start()
     copies[0].wait()
     copies[1].wait()
-    category = category_ref[...]
-    conduct = jnp.zeros((ROWS, COLS), F32)
-    for i in range(classes_ref.shape[0]):
-        conduct = jnp.where(category == i, classes_ref[i], conduct)
-    conduct_ref[...] = conduct
-    copies[2].wait()
-    copies[3].wait()
-    state_ref[0] = state_ref[0] + inflow_ref[...]
-    upper = iota((8, COLS), 0) < 4
-    edges = jnp.where(upper[None], state_ref[:, 0:8, :], state_ref[:, ROWS - 8 : ROWS, :])
-    ends = jnp.where(upper, conduct[0:8], conduct[ROWS - 8 : ROWS])[None]
-    whole = jnp.concatenate([edges, ends, jnp.zeros((1, 8, COLS), F32)], axis=0)
-    edge_ref[...] = whole.reshape((L + 2) * 8, COLS).astype(BF16)
-    for copy in copies[4:]:
-        copy.wait()
-
-
-def request_body(slot_ref, strip_ref, after_ref, placing_ref, request_ref):
     tile = jnp.concatenate([slot_ref[k : k + 1, :] for k in range(TOUCH)], axis=1)
     row = jnp.concatenate([strip_ref[k : k + 1, :] for k in range(TOUCH)], axis=1)
     sub = iota((TILES, REFS), 0)
@@ -101,6 +83,23 @@
     placing_ref[...] = placing
     wanted = (sub == row).astype(F32).astype(BF16)
     request_ref[...] = dot(placing, wanted, 1, 1).astype(BF16)
+    copies[2].wait()
+    copies[3].wait()
+    category = category_ref[...]
+    conduct = jnp.zeros((ROWS, COLS), F32)
+    for i in range(classes_ref.shape[0]):
+        conduct = jnp.where(category == i, classes_ref[i], conduct)
+    conduct_ref[...] = conduct
+    copies[4].wait()
+    copies[5].wait()
+    state_ref[0] = state_ref[0] + inflow_ref[...]
+    upper = iota((8, COLS), 0) < 4
+    edges = jnp.where(upper[None], state_ref[:, 0:8, :], state_ref[:, ROWS - 8 : ROWS, :])
+    ends = jnp.where(upper, conduct[0:8], conduct[ROWS - 8 : ROWS])[None]
+    whole = jnp.concatenate([edges, ends, jnp.zeros((1, 8, COLS), F32)], axis=0)
+    edge_ref[...] = whole.reshape((L + 2) * 8, COLS).astype(BF16)
+    for copy in copies[6:]:
+        copy.wait()
 
 
 def row_halo(a_ref, b_ref, levels=L + 1):
@@ -179,8 +178,8 @@
 
 
 def strip_body(
-    own_ref, cond_ref, pa_ref, pb_ref, tops_ref, thermal_ref, picker_ref,
-    left_ref, right_ref, adjoint_ref, served_ref, u_ref, v_ref, c_ref, cd_ref, cr_ref, cl_ref,
+    own_ref, cond_ref, pa_ref, pb_ref, tops_ref, thermal_ref,
+    left_ref, right_ref, adjoint_ref, bright_ref, u_ref, v_ref, c_ref, cd_ref, cr_ref, cl_ref, lower_ref, upper_ref,
 ):
     gy = lax.axis_index("gy")
     odd = lax.rem(gy, 2)
@@ -209,14 +208,20 @@
         u_ref[i] = s + 0.5
         c_ref[i] = 0.5 * c
 
+    def turn(ref):
+        for i in range(6):
+            lower_ref[i] = pltpu.roll(ref[i], COLS - 4, 1)
+            upper_ref[i] = pltpu.roll(ref[i], 4, 1)
+
     def next_of(ref, i):
-        x = pltpu.roll(ref[i], COLS - 1, 1)
-        return jnp.where(last, pltpu.roll(ref[i + 1], 3, 1), x) if i % 3 < 2 else x
+        x = jnp.where(first, upper_ref[i + 1], ref[i]) if i % 3 < 2 else ref[i]
+        return pltpu.roll(x, COLS - 1, 1)
 
     def prior_of(ref, i):
-        x = pltpu.roll(ref[i], 1, 1)
-        return jnp.where(first, pltpu.roll(ref[i - 1], COLS - 3, 1), x) if i % 3 else x
-
+        x = jnp.where(last, lower_ref[i - 1], ref[i]) if i % 3 else ref[i]
+        return pltpu.roll(x, 1, 1)
+
+    turn(c_ref)
     for i in range(6):
         cd_ref[i] = pltpu.roll(c_ref[i], WIDE - 1, 0)
         cr_ref[i] = next_of(c_ref, i)
@@ -224,11 +229,12 @@
 
     for step in range(STEPS):
         now, then = (u_ref, v_ref) if step % 2 == 0 else (v_ref, u_ref)
-        for i in range(6):
+        turn(now)
+        for i in range(6) if step < STEPS - 1 else (1, 4):
             u, c = now[i], c_ref[i]
             k = c * u
             ur, ul = next_of(now, i), prior_of(now, i)
-            uz, ua = pltpu.roll(u, COLS - 4, 1), pltpu.roll(u, 4, 1)
+            uz, ua = lower_ref[i], upper_ref[i]
             change = rows_change(u, k, cd_ref[i])
             change = change + ((k + cr_ref[i] * ur) * (ur - u) - (k + cl_ref[i] * ul) * (u - ul))
             down = (k + c * uz) * ((u - uz) + 0.3)
@@ -255,8 +261,11 @@
     thermal = thermal_ref[...]
     bright = (thermal * (1.0 - 0.4 * mix * mix)).astype(BF16)
     adjoint_ref[...] = thermal * (-0.8 * mix)
-    bright = jnp.concatenate([bright, jnp.zeros((COLS - ROWS, COLS), BF16)], axis=0)
-    served_ref[...] = dot(picker_ref[...], bright, 1, 0).astype(BF16)
+    bright_ref[...] = jnp.concatenate([bright, jnp.zeros((COLS - ROWS, COLS), BF16)], axis=0)
+
+
+def serve_body(picker_ref, bright_ref, served_ref):
+    served_ref[...] = dot(picker_ref[...], bright_ref[...], 1, 0).astype(BF16)
 
 
 def wide_conduct(conduct_ref, halo):
@@ -357,6 +366,7 @@
 
 
 PART = 4
+CHUNKS = (8, 12)
 
 
 def foot_body(
@@ -364,12 +374,12 @@
     bright_ref, outgoing_ref, cells_ref, contrib_ref, weights_ref, sems,
 ):
     copies = {}
-    for start in range(NEAR, OWN, PART):
-        span = pl.ds(start, PART)
-        copies[start] = pltpu.make_async_copy(
-            weights_hbm.at[span], weights_ref.at[span], sems.at[start // PART]
-        )
-        copies[start].start()
+    at = NEAR
+    for i, count in enumerate(CHUNKS):
+        span = pl.ds(at, count)
+        copies[at] = pltpu.make_async_copy(weights_hbm.at[span], weights_ref.at[span], sems.at[i])
+        copies[at].start()
+        at += count
     placing = placing_ref[...]
     cells_ref[...] = dot(placing, returned_ref[...], 0, 0)
     lane = iota((FOOT, COLS), 1)
@@ -428,11 +438,11 @@
     def sds(*shape, dtype=F32):
         return jax.ShapeDtypeStruct(shape, dtype)
 
-    held_state, conduct, edge, warm, slot_ids, strip_ids, seen = call(
+    held_state, conduct, edge, warm, seen, placing, request = call(
         prep_body,
         (
             sds(L, ROWS, COLS), sds(ROWS, COLS), sds((L + 2) * 8, COLS, dtype=BF16), sds(ROWS, COLS),
-            sds(TOUCH, OWN, dtype=jnp.int32), sds(TOUCH, OWN, dtype=jnp.int32), sds(OWN, FOOT),
+            sds(OWN, FOOT), sds(SLOTS, REFS, dtype=BF16), sds(SLOTS, COLS, dtype=BF16),
         ),
         [HBM] * 8,
         "prep",
@@ -440,18 +450,13 @@
             pltpu.VMEM((ROWS, COLS), F32),
             pltpu.VMEM((ROWS, COLS), jnp.int32),
             pltpu.SMEM(classes.shape, F32),
+            pltpu.VMEM((TOUCH, OWN), jnp.int32),
+            pltpu.VMEM((TOUCH, OWN), jnp.int32),
             pltpu.SemaphoreType.DMA((8,)),
         ],
-        flops=1_000_000, moved=2_000_000,
+        flops=20_000_000, moved=2_000_000,
     )(*(far(x) for x in (classes, inflow, category, state, thermal, slots.T, strips.T, measured)))
     xa, xb = swapped((edge, edge), "gx")
-    placing, request = call(
-        request_body,
-        (sds(SLOTS, REFS, dtype=BF16), sds(SLOTS, COLS, dtype=BF16)),
-        [VMEM, VMEM, ANY],
-        "requests",
-        flops=20_000_000, moved=500_000,
-    )(slot_ids, strip_ids, conduct)
     picker = exchange(request)
     own, cond, pa, pb = call(
         pack_body,
@@ -469,14 +474,21 @@
         [pltpu.VMEM((STEPS + 2, WIDE, COLS), F32), pltpu.VMEM((4, WIDE, COLS), F32)],
         flops=20_000_000_000, moved=1_000_000,
     )(held_state, conduct, xa, xb)
-    left, right, adjoint, served = call(
+    left, right, adjoint, bright = call(
         strip_body,
-        (sds(ROWS, COLS), sds(ROWS, COLS), sds(ROWS, COLS), sds(SLOTS, COLS, dtype=BF16)),
-        [VMEM] * 7,
+        (sds(ROWS, COLS), sds(ROWS, COLS), sds(ROWS, COLS), sds(COLS, COLS, dtype=BF16)),
+        [VMEM] * 6,
         "strips",
-        [pltpu.VMEM((6, WIDE, COLS), F32)] * 6,
-        flops=20_000_000, moved=1_000_000,
-    )(own, cond, ya, yb, tops, warm, picker)
+        [pltpu.VMEM((6, WIDE, COLS), F32)] * 8,
+        flops=10_000_000_000, moved=1_000_000,
+    )(own, cond, ya, yb, tops, warm)
+    served = call(
+        serve_body,
+        sds(SLOTS, COLS, dtype=BF16),
+        [VMEM] * 2,
+        "serve",
+        flops=20_000_000, moved=300_000,
+    )(picker, bright)
     returned = exchange(served)
     scratch = [
         pltpu.VMEM((HALF + STEPS, WIDE, COLS), F32),
@@ -502,7 +514,7 @@
             pltpu.VMEM((REFS, COLS), F32),
             pltpu.VMEM((REFS, COLS), F32),
             pltpu.VMEM(weights.shape, BF16),
-            pltpu.SemaphoreType.DMA((OWN // PART,)),
+            pltpu.SemaphoreType.DMA((len(CHUNKS),)),
         ],
         flops=20_000_000, moved=5_000_000,
     )(returned, placing, seen, near, far(weights))

time: 66.2 us -> 65.4 us (0.988)
  waiting for transfers between devices: 16.2 us -> 14.7 us
  starting transfers between devices: 29.8 us -> 31.1 us
    all_to_all x3, starting transfers between devices: 19.9 us -> 24.1 us  [exchange(): lax.all_to_all(x.reshape(TILES, CAP, COLS), ('gx', 'gy'), split_axis=0, c...]
    ppermute x4, starting transfers between devices: 9.85 us -> 6.96 us  [swapped(): return (lax.ppermute(x[0], axis, one), lax.ppermute(x[1], axis, two))]
    all_to_all x3, waiting for transfers between devices: 13.8 us -> 12.3 us  [exchange(): lax.all_to_all(x.reshape(TILES, CAP, COLS), ('gx', 'gy'), split_axis=0, c...]
    pallas_call x1, Pallas kernels: 2.35 us -> 1.46 us  [on_device(): call(strip_body, (sds(ROWS, COLS), sds(ROWS, COLS), sds(ROWS, COLS), sds(...]
    pallas_call x1, Pallas kernels: 1.37 us -> 2.05 us  [on_device(): call(prep_body, (sds(L, ROWS, COLS), sds(ROWS, COLS), sds((L + 2) * 8, CO...]
where the time goes in v4:
time: 65.4 us; the launch traced here: 65 us
  starting transfers between devices  31.1 us (48%)
  Pallas kernels  18.5 us (28%)
  waiting for transfers between devices  14.7 us (22%)
  between operations  0.75 us (1%)
    all_to_all x3, starting transfers between devices, exchange(): lax.all_to_all(x.reshape(TILES, CAP, COLS), ('gx', 'gy'), split_axis=0, c...  24.1 us
    all_to_all x3, waiting for transfers between devices, exchange(): lax.all_to_all(x.reshape(TILES, CAP, COLS), ('gx', 'gy'), split_axis=0, c...  12.3 us
    ppermute x4, starting transfers between devices, swapped(): return (lax.ppermute(x[0], axis, one), lax.ppermute(x[1], axis, two))  6.96 us
    pallas_call x1, Pallas kernels, on_device(): call(lower_body, sds(L, ROWS, COLS), [HBM] + [VMEM] * 5 + [HBM], 'lower',...  4.32 us
    pallas_call x1, Pallas kernels, on_device(): call(upper_body, (sds(L, ROWS, COLS), sds(NEAR, TOUCH, FOOT, COLS, dtype=...  4.12 us
    pallas_call x1, Pallas kernels, on_device(): call(foot_body, (sds(OWN, FOOT), sds(SLOTS, COLS, dtype=BF16)), [VMEM] *...  3.44 us
    ppermute x4, waiting for transfers between devices, swapped(): return (lax.ppermute(x[0], axis, one), lax.ppermute(x[1], axis, two))  2.37 us
    pallas_call x1, Pallas kernels, on_device(): call(prep_body, (sds(L, ROWS, COLS), sds(ROWS, COLS), sds((L + 2) * 8, CO...  2.05 us
  transfers between devices with their start and end apart: 7, of which 4 were waited for; matrix products, arithmetic and copies ran while one was open for 0% of the time, Pallas kernels for 17%

profile of v4, /device:TPU:1, one launch (start us, length us, event | category | flops | bytes accessed | tf_op | source)
XLA Modules:
  0.0 65.0 jit_solution(10913219548401299555)
XLA Ops:
  0.6 2.0 %prep.1 = (f32[32,64,128]{2,1,0:T(8,128)S(1)}, f32[64,128]{1,0:T(8,128)S(1)}, bf16[272,128]{1,0:T(8,128)(2,1)S(1)}, f32[64,128]{1,0:T(8,128)S(1)}, f32[32,128]{1...) custom-call(f32[12]{0:T(128)} %classes_hbm.1, f32[64,128]{1,0:T(8,128)} %inflow_hbm.1, ...), custom_call_target="tpu_custom_call" | custom-call | flops 20000000 | bytes 2000000 | tf_op jit(solution)/shard_map/prep/pallas_call | solution.py:441
  2.7 2.5 %collective-permute-start = (bf16[272,128]{1,0:T(8,128)(2,1)S(1)}, bf16[272,128]{1,0:T(8,128)(2,1)S(1)}, u32[]{:S(2)}, u32[]{:S(2)}) collective-permute-start(bf16[272,128]{1,0:T(8,128)(2,1)S(1)} %get-tuple-element.23), channel_id=1, source_target_pairs={{0,8},{8,0},{16,24},{24,16},{32,40},{40,32},{48,56},{56,48},{64,72... | collective-permute-start | bytes 208904 | tf_op jit(solution)/shard_map/ppermute | solution.py:428
  5.2 0.7 %collective-permute-start.1 = (bf16[272,128]{1,0:T(8,128)(2,1)S(1)}, bf16[272,128]{1,0:T(8,128)(2,1)S(1)}, u32[]{:S(2)}, u32[]{:S(2)}) collective-permute-start(bf16[272,128]{1,0:T(8,128)(2,1)S(1)} %get-tuple-element.23), channel_id=1, source_target_pairs={{8,16},{24,32},{40,48},{56,64},{72,80},{88,96},{104,112},{16,8},{3... | collective-permute-start | bytes 208904 | tf_op jit(solution)/shard_map/ppermute | solution.py:428
  5.9 12.1 %all-to-all-start = ((bf16[128,4,128]{2,1,0:T(4,128)(2,1)}), bf16[128,4,128]{2,1,0:T(4,128)(2,1)S(1)}, u32[]{:S(2)}, u32[]{:S(2)}) async-start(bf16[128,4,128]{2,1,0:T(4,128)(2,1)} %bitcast.2), calls=%async_computation | async-start | bytes 262144 | tf_op jit(solution)/shard_map/all_to_all | solution.py:432
  18.0 0.0 collective-permute-done.a_ref
  18.0 0.0 collective-permute-done.1.b_ref
  18.0 0.9 %pack.1 = (f32[4,72,128]{2,1,0:T(8,128)S(1)}, f32[4,72,128]{2,1,0:T(8,128)S(1)}, bf16[144,128]{1,0:T(8,128)(2,1)S(1)}, bf16[144,128]{1,0:T(8,128)(2,1)S(1)}) custom-call(f32[32,64,128]{2,1,0:T(8,128)S(1)} %get-tuple-element.24.state_ref, f32[64,128]{1,0:T(8,128)S(1)} %get-tuple-element.22.conduct_ref, bf16[272,128]{1,0:T(8,128)(2,1)S(1)} %collective-permute-done.a_ref, ...), custom_call_target="tpu_custom_call" | custom-call | flops 20000000000 | bytes 1500000 | tf_op jit(solution)/shard_map/pack/pallas_call | solution.py:461
  18.9 1.1 %collective-permute-start.2 = (bf16[144,128]{1,0:T(8,128)(2,1)S(1)}, bf16[144,128]{1,0:T(8,128)(2,1)S(1)}, u32[]{:S(2)}, u32[]{:S(2)}) collective-permute-start(bf16[144,128]{1,0:T(8,128)(2,1)S(1)} %get-tuple-element.27), channel_id=1, source_target_pairs={{0,1},{1,0},{2,3},{3,2},{4,5},{5,4},{6,7},{7,6},{8,9},{9,8},{10,11... | collective-permute-start | bytes 110600 | tf_op jit(solution)/shard_map/ppermute | solution.py:428
  20.1 2.6 %collective-permute-start.3 = (bf16[144,128]{1,0:T(8,128)(2,1)S(1)}, bf16[144,128]{1,0:T(8,128)(2,1)S(1)}, u32[]{:S(2)}, u32[]{:S(2)}) collective-permute-start(bf16[144,128]{1,0:T(8,128)(2,1)S(1)} %get-tuple-element.28), channel_id=1, source_target_pairs={{1,2},{3,4},{5,6},{2,1},{4,3},{6,5},{9,10},{11,12},{13,14},{10,9},... | collective-permute-start | bytes 110600 | tf_op jit(solution)/shard_map/ppermute | solution.py:428
  22.7 0.6 tops.1.tops_ref
  23.3 0.0 collective-permute-done.2.pa_ref
  23.3 2.4 %collective-permute-done.3.pb_ref = bf16[144,128]{1,0:T(8,128)(2,1)S(1)} collective-permute-done((bf16[144,128]{1,0:T(8,128)(2,1)S(1)}, bf16[144,128]{1,0:T(8,128)(2,1)S(1)}, u32[]{:S(2)}, u32[]{:S(2)}) %collective-permute-start.3) | collective-permute-done | bytes 36896 | tf_op jit(solution)/shard_map/ppermute | solution.py:428
  25.6 1.5 %strips.1 = (f32[64,128]{1,0:T(8,128)S(1)}, f32[64,128]{1,0:T(8,128)S(1)}, f32[64,128]{1,0:T(8,128)S(1)}, bf16[128,128]{1,0:T(8,128)(2,1)S(1)}) custom-call(f32[4,72,128]{2,1,0:T(8,128)S(1)} %get-tuple-element.25.own_ref, f32[4,72,128]{2,1,0:T(8,128)S(1)} %get-tuple-element.26.cond_ref, bf16[144,128]{1,0:T(8,128)(2,1)S(1)} %collective-permute-done.2.pa_ref, ...), custom_call_target="tpu_custom_call" | custom-call | flops 10000000000 | bytes 1000000 | tf_op jit(solution)/shard_map/strips/pallas_call | solution.py:477
  27.1 0.9 %all-to-all-done = bf16[128,4,128]{2,1,0:T(4,128)(2,1)S(1)} async-done(((bf16[128,4,128]{2,1,0:T(4,128)(2,1)}), bf16[128,4,128]{2,1,0:T(4,128)(2,1)S(1)}, u32[]{:S(2)}, u32[]{:S(2)}) %all-to-all-start) | async-done | bytes 131104 | tf_op jit(solution)/shard_map/all_to_all | solution.py:432
  28.0 0.8 %serve.1 = bf16[512,128]{1,0:T(8,128)(2,1)} custom-call(bf16[512,128]{1,0:T(8,128)(2,1)S(1)} %bitcast.8, bf16[128,128]{1,0:T(8,128)(2,1)S(1)} %get-tuple-element.34.bright_ref), custom_call_target="tpu_custom_call" | custom-call | flops 20000000 | bytes 300000 | tf_op jit(solution)/shard_map/serve/pallas_call | solution.py:485
  28.8 7.7 %all-to-all-start.1 = ((bf16[128,4,128]{2,1,0:T(4,128)(2,1)}), bf16[128,4,128]{2,1,0:T(4,128)(2,1)S(1)}, u32[]{:S(2)}, u32[]{:S(2)}) async-start(bf16[128,4,128]{2,1,0:T(4,128)(2,1)} %bitcast.4), calls=%async_computation.1 | async-start | bytes 262144 | tf_op jit(solution)/shard_map/all_to_all | solution.py:432
  36.5 4.1 %upper.1 = (f32[32,64,128]{2,1,0:T(8,128)}, bf16[12,4,128,128]{3,2,1,0:T(8,128)(2,1)S(1)}) custom-call(f32[32,64,128]{2,1,0:T(8,128)S(1)} %get-tuple-element.24.state_ref, f32[64,128]{1,0:T(8,128)S(1)} %get-tuple-element.22.conduct_ref, bf16[272,128]{1,0:T(8,128)(2,1)S(1)} %collective-permute-done.a_ref, bf16[272,128]{1,0:T(8,128)(2,1)S(1)} %collective-permute-done.1.b_ref, ...), custom_call_target="tpu_custom_call" | custom-call | flops 500000000 | bytes 3000000 | tf_op jit(solution)/shard_map/upper/pallas_call | solution.py:499
  40.7 5.8 %all-to-all-done.1 = bf16[128,4,128]{2,1,0:T(4,128)(2,1)S(1)} async-done(((bf16[128,4,128]{2,1,0:T(4,128)(2,1)}), bf16[128,4,128]{2,1,0:T(4,128)(2,1)S(1)}, u32[]{:S(2)}, u32[]{:S(2)}) %all-to-all-start.1) | async-done | bytes 131104 | tf_op jit(solution)/shard_map/all_to_all | solution.py:432
  46.5 3.4 %footprints.1 = (f32[32,128]{1,0:T(8,128)}, bf16[512,128]{1,0:T(8,128)(2,1)}) custom-call(bf16[512,128]{1,0:T(8,128)(2,1)S(1)} %bitcast.10, bf16[512,128]{1,0:T(8,128)(2,1)S(1)} %get-tuple-element.35.placing_ref, f32[32,128]{1,0:T(8,128)S(1)} %get-tuple-element.36.seen_ref, bf16[12,4,128,128]{3,2,1,0:T(8,128)(2,1)S(1)} %get-tuple-element.37.near_ref, ...), custom_call_target="tpu_custom_call" | custom-call | flops 20000000 | bytes 5000000 | tf_op jit(solution)/shard_map/footprints/pallas_call | solution.py:508
  49.9 4.3 %all-to-all-start.2 = ((bf16[128,4,128]{2,1,0:T(4,128)(2,1)}), bf16[128,4,128]{2,1,0:T(4,128)(2,1)S(1)}, u32[]{:S(2)}, u32[]{:S(2)}) async-start(bf16[128,4,128]{2,1,0:T(4,128)(2,1)} %bitcast.6), calls=%async_computation.2 | async-start | bytes 262144 | tf_op jit(solution)/shard_map/all_to_all | solution.py:432
  54.2 4.3 %lower.1 = f32[32,64,128]{2,1,0:T(8,128)} custom-call(f32[32,64,128]{2,1,0:T(8,128)} %state_hbm.3, f32[64,128]{1,0:T(8,128)S(1)} %get-tuple-element.22.conduct_ref, bf16[272,128]{1,0:T(8,128)(2,1)S(1)} %collective-permute-done.a_ref, bf16[272,128]{1,0:T(8,128)(2,1)S(1)} %collective-permute-done.1.b_ref, ...), custom_call_target="tpu_custom_call", output_to_operand_aliasing={{}: (6, {})} | custom-call | flops 500000000 | bytes 3000000 | tf_op jit(solution)/shard_map/lower/pallas_call | solution.py:521
  58.5 5.6 %all-to-all-done.2 = bf16[128,4,128]{2,1,0:T(4,128)(2,1)S(1)} async-done(((bf16[128,4,128]{2,1,0:T(4,128)(2,1)}), bf16[128,4,128]{2,1,0:T(4,128)(2,1)S(1)}, u32[]{:S(2)}, u32[]{:S(2)}) %all-to-all-start.2) | async-done | bytes 131104 | tf_op jit(solution)/shard_map/all_to_all | solution.py:432
  64.2 0.8 %gradient.1 = f32[2,64,128]{2,1,0:T(8,128)} custom-call(bf16[512,128]{1,0:T(8,128)(2,1)S(1)} %bitcast.11, bf16[512,128]{1,0:T(8,128)(2,1)S(1)} %bitcast.9, f32[64,128]{1,0:T(8,128)S(1)} %get-tuple-element.40.adjoint_ref), custom_call_target="tpu_custom_call" | custom-call | flops 20000000 | bytes 400000 | tf_op jit(solution)/shard_map/gradient/pallas_call | solution.py:532
Async XLA Ops:
  2.7 15.3 %collective-permute-start = (bf16[272,128]{1,0:T(8,128)(2,1)S(1)}, bf16[272,128]{1,0:T(8,128)(2,1)S(1)}, u32[]{:S(2)}, u32[]{:S(2)}) collective-permute-start(bf16[272,128]{1,0:T(8,128)(2,1)S(1)} %get-tuple-element.23), channel_id=1, source_target_pairs={{0,8},{8,0},{16,24},{24,16},{32,40},{40,32},{48,56},{56,48},{64,72... | collective-permute-start | bytes 208904 | tf_op jit(solution)/shard_map/ppermute | solution.py:428
  5.2 12.8 %collective-permute-start.1 = (bf16[272,128]{1,0:T(8,128)(2,1)S(1)}, bf16[272,128]{1,0:T(8,128)(2,1)S(1)}, u32[]{:S(2)}, u32[]{:S(2)}) collective-permute-start(bf16[272,128]{1,0:T(8,128)(2,1)S(1)} %get-tuple-element.23), channel_id=1, source_target_pairs={{8,16},{24,32},{40,48},{56,64},{72,80},{88,96},{104,112},{16,8},{3... | collective-permute-start | bytes 208904 | tf_op jit(solution)/shard_map/ppermute | solution.py:428
  5.9 22.1 %all-to-all-start = ((bf16[128,4,128]{2,1,0:T(4,128)(2,1)}), bf16[128,4,128]{2,1,0:T(4,128)(2,1)S(1)}, u32[]{:S(2)}, u32[]{:S(2)}) async-start(bf16[128,4,128]{2,1,0:T(4,128)(2,1)} %bitcast.2), calls=%async_computation | async-start | bytes 262144 | tf_op jit(solution)/shard_map/all_to_all | solution.py:432
  18.9 4.3 %collective-permute-start.2 = (bf16[144,128]{1,0:T(8,128)(2,1)S(1)}, bf16[144,128]{1,0:T(8,128)(2,1)S(1)}, u32[]{:S(2)}, u32[]{:S(2)}) collective-permute-start(bf16[144,128]{1,0:T(8,128)(2,1)S(1)} %get-tuple-element.27), channel_id=1, source_target_pairs={{0,1},{1,0},{2,3},{3,2},{4,5},{5,4},{6,7},{7,6},{8,9},{9,8},{10,11... | collective-permute-start | bytes 110600 | tf_op jit(solution)/shard_map/ppermute | solution.py:428
  20.1 5.6 %collective-permute-start.3 = (bf16[144,128]{1,0:T(8,128)(2,1)S(1)}, bf16[144,128]{1,0:T(8,128)(2,1)S(1)}, u32[]{:S(2)}, u32[]{:S(2)}) collective-permute-start(bf16[144,128]{1,0:T(8,128)(2,1)S(1)} %get-tuple-element.28), channel_id=1, source_target_pairs={{1,2},{3,4},{5,6},{2,1},{4,3},{6,5},{9,10},{11,12},{13,14},{10,9},... | collective-permute-start | bytes 110600 | tf_op jit(solution)/shard_map/ppermute | solution.py:428
  28.8 17.7 %all-to-all-start.1 = ((bf16[128,4,128]{2,1,0:T(4,128)(2,1)}), bf16[128,4,128]{2,1,0:T(4,128)(2,1)S(1)}, u32[]{:S(2)}, u32[]{:S(2)}) async-start(bf16[128,4,128]{2,1,0:T(4,128)(2,1)} %bitcast.4), calls=%async_computation.1 | async-start | bytes 262144 | tf_op jit(solution)/shard_map/all_to_all | solution.py:432
  49.9 14.3 %all-to-all-start.2 = ((bf16[128,4,128]{2,1,0:T(4,128)(2,1)}), bf16[128,4,128]{2,1,0:T(4,128)(2,1)S(1)}, u32[]{:S(2)}, u32[]{:S(2)}) async-start(bf16[128,4,128]{2,1,0:T(4,128)(2,1)} %bitcast.6), calls=%async_computation.2 | async-start | bytes 262144 | tf_op jit(solution)/shard_map/all_to_all | solution.py:432

commit v5 on v4

--- a/solution.py
+++ b/solution.py
@@ -107,7 +107,7 @@
     a = a_ref[...].astype(F32).reshape(L + 2, 8, COLS)
     b = b_ref[...].astype(F32).reshape(L + 2, 8, COLS)
     half = lax.div(iota((8, COLS), 0), 4)
-    return jnp.where((half == odd)[None], a, b)
+    return jnp.where(halo_rows_inside()[None], jnp.where((half == odd)[None], a, b), 0.0)
 
 
 def halo_rows_inside():
@@ -186,8 +186,9 @@
     a = pa_ref[...].astype(F32)
     b = pb_ref[...].astype(F32)
     is_odd = (jnp.zeros((2 * WIDE, COLS), jnp.int32) + odd) > 0
-    from_right = jnp.where(is_odd, b, a)
-    from_left = jnp.where(is_odd, a, b)
+    at = jnp.zeros((2 * WIDE, COLS), jnp.int32) + gy
+    from_right = jnp.where(at < lax.axis_size("gy") - 1, jnp.where(is_odd, b, a), 0.0)
+    from_left = jnp.where(at > 0, jnp.where(is_odd, a, b), 0.0)
     lane = iota((WIDE, COLS), 1)
     last = lax.rem(lane, 4) == 3
     first = lax.rem(lane, 4) == 0
@@ -424,7 +425,7 @@
 def swapped(x, axis):
     n = lax.axis_size(axis)
     one = [(i, i ^ 1) for i in range(n)]
-    two = [(i, i + 1) for i in range(1, n - 1, 2)] + [(i + 1, i) for i in range(1, n - 1, 2)]
+    two = [(i, (i + 1) % n) for i in range(1, n, 2)] + [((i + 1) % n, i) for i in range(1, n, 2)]
     return lax.ppermute(x[0], axis, one), lax.ppermute(x[1], axis, two)
 
 

time: 65.4 us -> 62.4 us (0.954)
  starting transfers between devices: 31.1 us -> 26.2 us
  waiting for transfers between devices: 14.7 us -> 16.7 us
    all_to_all x3, starting transfers between devices: 24.1 us -> 17.1 us  [exchange(): lax.all_to_all(x.reshape(TILES, CAP, COLS), ('gx', 'gy'), split_axis=0, c...]
    ppermute x4, starting transfers between devices: 6.96 us -> 9.1 us  [swapped(): return (lax.ppermute(x[0], axis, one), lax.ppermute(x[1], axis, two))]
    all_to_all x3, waiting for transfers between devices: 12.3 us -> 14.3 us  [exchange(): lax.all_to_all(x.reshape(TILES, CAP, COLS), ('gx', 'gy'), split_axis=0, c...]
  transfers between devices with their start and end apart: 7 -> 7, of which waited for: 4 -> 4; matrix products, arithmetic and copies ran while one was open for 0% -> 0% of each run, Pallas kernels for 17% -> 18%
where the time goes in v5:
time: 62.4 us; the launch traced here: 62.1 us
  starting transfers between devices  26.2 us (42%)
  Pallas kernels  18.5 us (30%)
  waiting for transfers between devices  16.7 us (27%)
  between operations  0.74 us (1%)
    all_to_all x3, starting transfers between devices, exchange(): lax.all_to_all(x.reshape(TILES, CAP, COLS), ('gx', 'gy'), split_axis=0, c...  17.1 us
    all_to_all x3, waiting for transfers between devices, exchange(): lax.all_to_all(x.reshape(TILES, CAP, COLS), ('gx', 'gy'), split_axis=0, c...  14.3 us
    ppermute x4, starting transfers between devices, swapped(): return (lax.ppermute(x[0], axis, one), lax.ppermute(x[1], axis, two))  9.1 us
    pallas_call x1, Pallas kernels, on_device(): call(lower_body, sds(L, ROWS, COLS), [HBM] + [VMEM] * 5 + [HBM], 'lower',...  4.31 us
    pallas_call x1, Pallas kernels, on_device(): call(upper_body, (sds(L, ROWS, COLS), sds(NEAR, TOUCH, FOOT, COLS, dtype=...  4.12 us
    pallas_call x1, Pallas kernels, on_device(): call(foot_body, (sds(OWN, FOOT), sds(SLOTS, COLS, dtype=BF16)), [VMEM] *...  3.44 us
    ppermute x4, waiting for transfers between devices, swapped(): return (lax.ppermute(x[0], axis, one), lax.ppermute(x[1], axis, two))  2.4 us
    pallas_call x1, Pallas kernels, on_device(): call(prep_body, (sds(L, ROWS, COLS), sds(ROWS, COLS), sds((L + 2) * 8, CO...  2.05 us
  transfers between devices with their start and end apart: 7, of which 4 were waited for; matrix products, arithmetic and copies ran while one was open for 0% of the time, Pallas kernels for 18%

profile of v5, /device:TPU:1, one launch (start us, length us, event | category | flops | bytes accessed | tf_op | source)
XLA Modules:
  0.0 62.1 jit_solution(811041738797360820)
XLA Ops:
  0.6 2.0 %prep.1 = (f32[32,64,128]{2,1,0:T(8,128)S(1)}, f32[64,128]{1,0:T(8,128)S(1)}, bf16[272,128]{1,0:T(8,128)(2,1)S(1)}, f32[64,128]{1,0:T(8,128)S(1)}, f32[32,128]{1...) custom-call(f32[12]{0:T(128)} %classes_hbm.1, f32[64,128]{1,0:T(8,128)} %inflow_hbm.1, ...), custom_call_target="tpu_custom_call" | custom-call | flops 20000000 | bytes 2000000 | tf_op jit(solution)/shard_map/prep/pallas_call | solution.py:442
  2.7 2.5 %collective-permute-start = (bf16[272,128]{1,0:T(8,128)(2,1)S(1)}, bf16[272,128]{1,0:T(8,128)(2,1)S(1)}, u32[]{:S(2)}, u32[]{:S(2)}) collective-permute-start(bf16[272,128]{1,0:T(8,128)(2,1)S(1)} %get-tuple-element.23), channel_id=1, source_target_pairs={{0,8},{8,0},{16,24},{24,16},{32,40},{40,32},{48,56},{56,48},{64,72... | collective-permute-start | bytes 208904 | tf_op jit(solution)/shard_map/ppermute | solution.py:429
  5.2 4.7 %collective-permute-start.1 = (bf16[272,128]{1,0:T(8,128)(2,1)S(1)}, bf16[272,128]{1,0:T(8,128)(2,1)S(1)}, u32[]{:S(2)}, u32[]{:S(2)}) collective-permute-start(bf16[272,128]{1,0:T(8,128)(2,1)S(1)} %get-tuple-element.23), channel_id=1, source_target_pairs={{8,16},{24,32},{40,48},{56,64},{72,80},{88,96},{104,112},{120,0},{... | collective-permute-start | bytes 208904 | tf_op jit(solution)/shard_map/ppermute | solution.py:429
  9.9 6.2 %all-to-all-start = ((bf16[128,4,128]{2,1,0:T(4,128)(2,1)}), bf16[128,4,128]{2,1,0:T(4,128)(2,1)S(1)}, u32[]{:S(2)}, u32[]{:S(2)}) async-start(bf16[128,4,128]{2,1,0:T(4,128)(2,1)} %bitcast.2), calls=%async_computation | async-start | bytes 262144 | tf_op jit(solution)/shard_map/all_to_all | solution.py:433
  16.1 0.0 collective-permute-done.a_ref
  16.1 0.0 collective-permute-done.1.b_ref
  16.1 0.9 %pack.1 = (f32[4,72,128]{2,1,0:T(8,128)S(1)}, f32[4,72,128]{2,1,0:T(8,128)S(1)}, bf16[144,128]{1,0:T(8,128)(2,1)S(1)}, bf16[144,128]{1,0:T(8,128)(2,1)S(1)}) custom-call(f32[32,64,128]{2,1,0:T(8,128)S(1)} %get-tuple-element.24.state_ref, f32[64,128]{1,0:T(8,128)S(1)} %get-tuple-element.22.conduct_ref, bf16[272,128]{1,0:T(8,128)(2,1)S(1)} %collective-permute-done.a_ref, ...), custom_call_target="tpu_custom_call" | custom-call | flops 20000000000 | bytes 1500000 | tf_op jit(solution)/shard_map/pack/pallas_call | solution.py:462
  17.0 1.1 %collective-permute-start.2 = (bf16[144,128]{1,0:T(8,128)(2,1)S(1)}, bf16[144,128]{1,0:T(8,128)(2,1)S(1)}, u32[]{:S(2)}, u32[]{:S(2)}) collective-permute-start(bf16[144,128]{1,0:T(8,128)(2,1)S(1)} %get-tuple-element.27), channel_id=1, source_target_pairs={{0,1},{1,0},{2,3},{3,2},{4,5},{5,4},{6,7},{7,6},{8,9},{9,8},{10,11... | collective-permute-start | bytes 110600 | tf_op jit(solution)/shard_map/ppermute | solution.py:429
  18.2 0.7 %collective-permute-start.3 = (bf16[144,128]{1,0:T(8,128)(2,1)S(1)}, bf16[144,128]{1,0:T(8,128)(2,1)S(1)}, u32[]{:S(2)}, u32[]{:S(2)}) collective-permute-start(bf16[144,128]{1,0:T(8,128)(2,1)S(1)} %get-tuple-element.28), channel_id=1, source_target_pairs={{1,2},{3,4},{5,6},{7,0},{2,1},{4,3},{6,5},{0,7},{9,10},{11,12},{13... | collective-permute-start | bytes 110600 | tf_op jit(solution)/shard_map/ppermute | solution.py:429
  18.9 0.6 tops.1.tops_ref
  19.5 0.0 collective-permute-done.2.pa_ref
  19.5 2.4 %collective-permute-done.3.pb_ref = bf16[144,128]{1,0:T(8,128)(2,1)S(1)} collective-permute-done((bf16[144,128]{1,0:T(8,128)(2,1)S(1)}, bf16[144,128]{1,0:T(8,128)(2,1)S(1)}, u32[]{:S(2)}, u32[]{:S(2)}) %collective-permute-start.3) | collective-permute-done | bytes 36896 | tf_op jit(solution)/shard_map/ppermute | solution.py:429
  21.9 1.4 %strips.1 = (f32[64,128]{1,0:T(8,128)S(1)}, f32[64,128]{1,0:T(8,128)S(1)}, f32[64,128]{1,0:T(8,128)S(1)}, bf16[128,128]{1,0:T(8,128)(2,1)S(1)}) custom-call(f32[4,72,128]{2,1,0:T(8,128)S(1)} %get-tuple-element.25.own_ref, f32[4,72,128]{2,1,0:T(8,128)S(1)} %get-tuple-element.26.cond_ref, bf16[144,128]{1,0:T(8,128)(2,1)S(1)} %collective-permute-done.2.pa_ref, ...), custom_call_target="tpu_custom_call" | custom-call | flops 10000000000 | bytes 1000000 | tf_op jit(solution)/shard_map/strips/pallas_call | solution.py:478
  23.3 2.8 %all-to-all-done = bf16[128,4,128]{2,1,0:T(4,128)(2,1)S(1)} async-done(((bf16[128,4,128]{2,1,0:T(4,128)(2,1)}), bf16[128,4,128]{2,1,0:T(4,128)(2,1)S(1)}, u32[]{:S(2)}, u32[]{:S(2)}) %all-to-all-start) | async-done | bytes 131104 | tf_op jit(solution)/shard_map/all_to_all | solution.py:433
  26.1 0.8 %serve.1 = bf16[512,128]{1,0:T(8,128)(2,1)} custom-call(bf16[512,128]{1,0:T(8,128)(2,1)S(1)} %bitcast.8, bf16[128,128]{1,0:T(8,128)(2,1)S(1)} %get-tuple-element.34.bright_ref), custom_call_target="tpu_custom_call" | custom-call | flops 20000000 | bytes 300000 | tf_op jit(solution)/shard_map/serve/pallas_call | solution.py:486
  26.9 6.7 %all-to-all-start.1 = ((bf16[128,4,128]{2,1,0:T(4,128)(2,1)}), bf16[128,4,128]{2,1,0:T(4,128)(2,1)S(1)}, u32[]{:S(2)}, u32[]{:S(2)}) async-start(bf16[128,4,128]{2,1,0:T(4,128)(2,1)} %bitcast.4), calls=%async_computation.1 | async-start | bytes 262144 | tf_op jit(solution)/shard_map/all_to_all | solution.py:433
  33.6 4.1 %upper.1 = (f32[32,64,128]{2,1,0:T(8,128)}, bf16[12,4,128,128]{3,2,1,0:T(8,128)(2,1)S(1)}) custom-call(f32[32,64,128]{2,1,0:T(8,128)S(1)} %get-tuple-element.24.state_ref, f32[64,128]{1,0:T(8,128)S(1)} %get-tuple-element.22.conduct_ref, bf16[272,128]{1,0:T(8,128)(2,1)S(1)} %collective-permute-done.a_ref, bf16[272,128]{1,0:T(8,128)(2,1)S(1)} %collective-permute-done.1.b_ref, ...), custom_call_target="tpu_custom_call" | custom-call | flops 500000000 | bytes 3000000 | tf_op jit(solution)/shard_map/upper/pallas_call | solution.py:500
  37.7 5.8 %all-to-all-done.1 = bf16[128,4,128]{2,1,0:T(4,128)(2,1)S(1)} async-done(((bf16[128,4,128]{2,1,0:T(4,128)(2,1)}), bf16[128,4,128]{2,1,0:T(4,128)(2,1)S(1)}, u32[]{:S(2)}, u32[]{:S(2)}) %all-to-all-start.1) | async-done | bytes 131104 | tf_op jit(solution)/shard_map/all_to_all | solution.py:433
  43.5 3.4 %footprints.1 = (f32[32,128]{1,0:T(8,128)}, bf16[512,128]{1,0:T(8,128)(2,1)}) custom-call(bf16[512,128]{1,0:T(8,128)(2,1)S(1)} %bitcast.10, bf16[512,128]{1,0:T(8,128)(2,1)S(1)} %get-tuple-element.35.placing_ref, f32[32,128]{1,0:T(8,128)S(1)} %get-tuple-element.36.seen_ref, bf16[12,4,128,128]{3,2,1,0:T(8,128)(2,1)S(1)} %get-tuple-element.37.near_ref, ...), custom_call_target="tpu_custom_call" | custom-call | flops 20000000 | bytes 5000000 | tf_op jit(solution)/shard_map/footprints/pallas_call | solution.py:509
  47.0 4.3 %all-to-all-start.2 = ((bf16[128,4,128]{2,1,0:T(4,128)(2,1)}), bf16[128,4,128]{2,1,0:T(4,128)(2,1)S(1)}, u32[]{:S(2)}, u32[]{:S(2)}) async-start(bf16[128,4,128]{2,1,0:T(4,128)(2,1)} %bitcast.6), calls=%async_computation.2 | async-start | bytes 262144 | tf_op jit(solution)/shard_map/all_to_all | solution.py:433
  51.3 4.3 %lower.1 = f32[32,64,128]{2,1,0:T(8,128)} custom-call(f32[32,64,128]{2,1,0:T(8,128)} %state_hbm.3, f32[64,128]{1,0:T(8,128)S(1)} %get-tuple-element.22.conduct_ref, bf16[272,128]{1,0:T(8,128)(2,1)S(1)} %collective-permute-done.a_ref, bf16[272,128]{1,0:T(8,128)(2,1)S(1)} %collective-permute-done.1.b_ref, ...), custom_call_target="tpu_custom_call", output_to_operand_aliasing={{}: (6, {})} | custom-call | flops 500000000 | bytes 3000000 | tf_op jit(solution)/shard_map/lower/pallas_call | solution.py:522
  55.6 5.6 %all-to-all-done.2 = bf16[128,4,128]{2,1,0:T(4,128)(2,1)S(1)} async-done(((bf16[128,4,128]{2,1,0:T(4,128)(2,1)}), bf16[128,4,128]{2,1,0:T(4,128)(2,1)S(1)}, u32[]{:S(2)}, u32[]{:S(2)}) %all-to-all-start.2) | async-done | bytes 131104 | tf_op jit(solution)/shard_map/all_to_all | solution.py:433
  61.2 0.8 %gradient.1 = f32[2,64,128]{2,1,0:T(8,128)} custom-call(bf16[512,128]{1,0:T(8,128)(2,1)S(1)} %bitcast.11, bf16[512,128]{1,0:T(8,128)(2,1)S(1)} %bitcast.9, f32[64,128]{1,0:T(8,128)S(1)} %get-tuple-element.40.adjoint_ref), custom_call_target="tpu_custom_call" | custom-call | flops 20000000 | bytes 400000 | tf_op jit(solution)/shard_map/gradient/pallas_call | solution.py:533
Async XLA Ops:
  2.7 13.4 %collective-permute-start = (bf16[272,128]{1,0:T(8,128)(2,1)S(1)}, bf16[272,128]{1,0:T(8,128)(2,1)S(1)}, u32[]{:S(2)}, u32[]{:S(2)}) collective-permute-start(bf16[272,128]{1,0:T(8,128)(2,1)S(1)} %get-tuple-element.23), channel_id=1, source_target_pairs={{0,8},{8,0},{16,24},{24,16},{32,40},{40,32},{48,56},{56,48},{64,72... | collective-permute-start | bytes 208904 | tf_op jit(solution)/shard_map/ppermute | solution.py:429
  5.2 10.9 %collective-permute-start.1 = (bf16[272,128]{1,0:T(8,128)(2,1)S(1)}, bf16[272,128]{1,0:T(8,128)(2,1)S(1)}, u32[]{:S(2)}, u32[]{:S(2)}) collective-permute-start(bf16[272,128]{1,0:T(8,128)(2,1)S(1)} %get-tuple-element.23), channel_id=1, source_target_pairs={{8,16},{24,32},{40,48},{56,64},{72,80},{88,96},{104,112},{120,0},{... | collective-permute-start | bytes 208904 | tf_op jit(solution)/shard_map/ppermute | solution.py:429
  9.9 16.1 %all-to-all-start = ((bf16[128,4,128]{2,1,0:T(4,128)(2,1)}), bf16[128,4,128]{2,1,0:T(4,128)(2,1)S(1)}, u32[]{:S(2)}, u32[]{:S(2)}) async-start(bf16[128,4,128]{2,1,0:T(4,128)(2,1)} %bitcast.2), calls=%async_computation | async-start | bytes 262144 | tf_op jit(solution)/shard_map/all_to_all | solution.py:433
  17.0 2.4 %collective-permute-start.2 = (bf16[144,128]{1,0:T(8,128)(2,1)S(1)}, bf16[144,128]{1,0:T(8,128)(2,1)S(1)}, u32[]{:S(2)}, u32[]{:S(2)}) collective-permute-start(bf16[144,128]{1,0:T(8,128)(2,1)S(1)} %get-tuple-element.27), channel_id=1, source_target_pairs={{0,1},{1,0},{2,3},{3,2},{4,5},{5,4},{6,7},{7,6},{8,9},{9,8},{10,11... | collective-permute-start | bytes 110600 | tf_op jit(solution)/shard_map/ppermute | solution.py:429
  18.2 3.7 %collective-permute-start.3 = (bf16[144,128]{1,0:T(8,128)(2,1)S(1)}, bf16[144,128]{1,0:T(8,128)(2,1)S(1)}, u32[]{:S(2)}, u32[]{:S(2)}) collective-permute-start(bf16[144,128]{1,0:T(8,128)(2,1)S(1)} %get-tuple-element.28), channel_id=1, source_target_pairs={{1,2},{3,4},{5,6},{7,0},{2,1},{4,3},{6,5},{0,7},{9,10},{11,12},{13... | collective-permute-start | bytes 110600 | tf_op jit(solution)/shard_map/ppermute | solution.py:429
  26.9 16.6 %all-to-all-start.1 = ((bf16[128,4,128]{2,1,0:T(4,128)(2,1)}), bf16[128,4,128]{2,1,0:T(4,128)(2,1)S(1)}, u32[]{:S(2)}, u32[]{:S(2)}) async-start(bf16[128,4,128]{2,1,0:T(4,128)(2,1)} %bitcast.4), calls=%async_computation.1 | async-start | bytes 262144 | tf_op jit(solution)/shard_map/all_to_all | solution.py:433
  47.0 14.3 %all-to-all-start.2 = ((bf16[128,4,128]{2,1,0:T(4,128)(2,1)}), bf16[128,4,128]{2,1,0:T(4,128)(2,1)S(1)}, u32[]{:S(2)}, u32[]{:S(2)}) async-start(bf16[128,4,128]{2,1,0:T(4,128)(2,1)} %bitcast.6), calls=%async_computation.2 | async-start | bytes 262144 | tf_op jit(solution)/shard_map/all_to_all | solution.py:433

commit v6 on v5

--- a/solution.py
+++ b/solution.py
@@ -54,8 +54,8 @@
 
 def prep_body(
     classes_hbm, inflow_hbm, category_hbm, state_hbm, thermal_hbm, slot_hbm, strip_hbm, measured_hbm,
-    state_ref, conduct_ref, edge_ref, thermal_ref, measured_ref, placing_ref, request_ref,
-    inflow_ref, category_ref, classes_ref, slot_ref, strip_ref, sems,
+    state_ref, conduct_ref, edge_ref, thermal_ref, measured_ref, placing_ref, request_hbm,
+    inflow_ref, category_ref, classes_ref, slot_ref, strip_ref, asked_ref, sems,
 ):
     pairs = (
         (slot_hbm, slot_ref),
@@ -70,8 +70,8 @@
     copies = [pltpu.make_async_copy(a, b, sems.at[i]) for i, (a, b) in enumerate(pairs)]
     for copy in copies:
         copy.start()
-    copies[0].wait()
-    copies[1].wait()
+    for copy in copies[:4]:
+        copy.wait()
     tile = jnp.concatenate([slot_ref[k : k + 1, :] for k in range(TOUCH)], axis=1)
     row = jnp.concatenate([strip_ref[k : k + 1, :] for k in range(TOUCH)], axis=1)
     sub = iota((TILES, REFS), 0)
@@ -82,9 +82,9 @@
     placing = (iota((SLOTS, REFS), 0) == place).astype(F32).astype(BF16)
     placing_ref[...] = placing
     wanted = (sub == row).astype(F32).astype(BF16)
-    request_ref[...] = dot(placing, wanted, 1, 1).astype(BF16)
-    copies[2].wait()
-    copies[3].wait()
+    asked_ref[...] = dot(placing, wanted, 1, 1).astype(BF16)
+    leaving = pltpu.make_async_copy(asked_ref, request_hbm, sems.at[len(pairs)])
+    leaving.start()
     category = category_ref[...]
     conduct = jnp.zeros((ROWS, COLS), F32)
     for i in range(classes_ref.shape[0]):
@@ -100,6 +100,7 @@
     edge_ref[...] = whole.reshape((L + 2) * 8, COLS).astype(BF16)
     for copy in copies[6:]:
         copy.wait()
+    leaving.wait()
 
 
 def row_halo(a_ref, b_ref, levels=L + 1):
@@ -313,6 +314,13 @@
             u, k = uz, kz
 
 
+def turned(ref):
+    parts = [
+        jnp.transpose(ref[i : i + COLS, :].astype(F32)).astype(BF16) for i in range(0, SLOTS, COLS)
+    ]
+    return jnp.concatenate(parts, axis=1)
+
+
 def tops_body(state_ref, conduct_ref, a_ref, b_ref, tops_ref, u_ref, c_ref):
     def finish(l, new):
         tops_ref[l] = new
@@ -347,10 +355,12 @@
 
 
 def upper_body(
-    state_ref, conduct_ref, a_ref, b_ref, left_ref, right_ref, weights_hbm, out_hbm, weights_ref, *scratch
+    state_ref, conduct_ref, a_ref, b_ref, left_ref, right_ref, picker_ref, weights_hbm,
+    out_hbm, weights_ref, across_ref, *scratch,
 ):
     copy = pltpu.make_async_copy(weights_hbm.at[pl.ds(0, NEAR)], weights_ref, scratch[-1])
     copy.start()
+    across_ref[...] = turned(picker_ref)
     half_body(0, state_ref, conduct_ref, a_ref, b_ref, left_ref, right_ref, out_hbm, *scratch[:-1])
     copy.wait()
 
@@ -415,18 +425,26 @@
     outgoing_ref[...] = dot(placing, contrib_ref[...].astype(BF16), 1, 0).astype(BF16)
 
 
-def gradient_body(grads_ref, picker_ref, adjoint_ref, out_ref):
-    summed = dot(picker_ref[...], grads_ref[...], 0, 0)[:ROWS]
+def gradient_body(grads_ref, across_ref, adjoint_ref, out_ref):
+    summed = dot(across_ref[0:ROWS, :], grads_ref[...], 1, 0)
     common = summed * adjoint_ref[...]
     out_ref[0] = 0.6 * common
     out_ref[1] = 0.4 * common
 
 
 def swapped(x, axis):
-    n = lax.axis_size(axis)
+    n, m = lax.axis_size(axis), lax.axis_size("gy" if axis == "gx" else "gx")
+
+    def place(along, across):
+        return along * m + across if axis == "gx" else across * n + along
+
     one = [(i, i ^ 1) for i in range(n)]
-    two = [(i, (i + 1) % n) for i in range(1, n, 2)] + [((i + 1) % n, i) for i in range(1, n, 2)]
-    return lax.ppermute(x[0], axis, one), lax.ppermute(x[1], axis, two)
+    two = []
+    for j in range(m):
+        two += [(place(i, j), place(i, j ^ 1)) for i in (0, n - 1)]
+        for i in range(1, n - 1, 2):
+            two += [(place(i, j), place(i + 1, j)), (place(i + 1, j), place(i, j))]
+    return lax.ppermute(x[0], axis, one), lax.ppermute(x[1], ("gx", "gy"), two)
 
 
 def exchange(x):
@@ -453,8 +471,10 @@
             pltpu.SMEM(classes.shape, F32),
             pltpu.VMEM((TOUCH, OWN), jnp.int32),
             pltpu.VMEM((TOUCH, OWN), jnp.int32),
-            pltpu.SemaphoreType.DMA((8,)),
+            pltpu.VMEM((SLOTS, COLS), BF16),
+            pltpu.SemaphoreType.DMA((9,)),
         ],
+        out_specs=(VMEM,) * 6 + (HBM,),
         flops=20_000_000, moved=2_000_000,
     )(*(far(x) for x in (classes, inflow, category, state, thermal, slots.T, strips.T, measured)))
     xa, xb = swapped((edge, edge), "gx")
@@ -497,15 +517,17 @@
         pltpu.VMEM((HALF, ROWS, COLS), F32),
         pltpu.SemaphoreType.DMA((HALF // PIECE,)),
     ]
-    begun, near = call(
+    begun, near, picker_across = call(
         upper_body,
-        (sds(L, ROWS, COLS), sds(NEAR, TOUCH, FOOT, COLS, dtype=BF16)),
-        [VMEM] * 6 + [HBM],
+        (
+            sds(L, ROWS, COLS), sds(NEAR, TOUCH, FOOT, COLS, dtype=BF16), sds(COLS, SLOTS, dtype=BF16)
+        ),
+        [VMEM] * 7 + [HBM],
         "upper",
         scratch + [pltpu.SemaphoreType.DMA],
-        out_specs=(HBM, VMEM),
+        out_specs=(HBM, VMEM, VMEM),
         flops=500_000_000, moved=3_000_000,
-    )(held_state, conduct, xa, xb, left, right, far(weights))
+    )(held_state, conduct, xa, xb, left, right, picker, far(weights))
     brightness, outgoing = call(
         foot_body,
         (sds(OWN, FOOT), sds(SLOTS, COLS, dtype=BF16)),
@@ -532,7 +554,7 @@
     grads = exchange(outgoing)
     grad_top = call(
         gradient_body, sds(2, ROWS, COLS), [VMEM] * 3, "gradient", flops=20_000_000, moved=400_000
-    )(grads, picker, adjoint)
+    )(grads, picker_across, adjoint)
     return moisture, brightness, grad_top
 
 

time: 62.4 us -> 61.4 us (0.984)
  starting transfers between devices: 26.2 us -> 25.3 us
    ppermute x4, starting transfers between devices: 9.1 us -> 5.36 us  [the longest x2 3.69 us: swapped(): lax.ppermute(x[0], axis, one)]
    all_to_all x3, starting transfers between devices: 17.1 us -> 20 us  [exchange(): lax.all_to_all(x.reshape(TILES, CAP, COLS), ('gx', 'gy'), split_axis=0, c...]
  transfers between devices with their start and end apart: 7 -> 7, of which waited for: 4 -> 4; matrix products, arithmetic and copies ran while one was open for 0% -> 0% of each run, Pallas kernels for 18% -> 19%
where the time goes in v6:
time: 61.4 us; the launch traced here: 61 us
  starting transfers between devices  25.3 us (41%)
  Pallas kernels  18.3 us (30%)
  waiting for transfers between devices  16.6 us (27%)
  between operations  0.74 us (1%)
    all_to_all x3, starting transfers between devices, exchange(): lax.all_to_all(x.reshape(TILES, CAP, COLS), ('gx', 'gy'), split_axis=0, c...  20 us
    all_to_all x3, waiting for transfers between devices, exchange(): lax.all_to_all(x.reshape(TILES, CAP, COLS), ('gx', 'gy'), split_axis=0, c...  14.2 us
    pallas_call x1, Pallas kernels, on_device(): call(lower_body, sds(L, ROWS, COLS), [HBM] + [VMEM] * 5 + [HBM], 'lower',...  4.31 us
    pallas_call x1, Pallas kernels, on_device(): call(upper_body, (sds(L, ROWS, COLS), sds(NEAR, TOUCH, FOOT, COLS, dtype=...  4.18 us
    ppermute x2, starting transfers between devices, swapped(): lax.ppermute(x[0], axis, one)  3.69 us
    pallas_call x1, Pallas kernels, on_device(): call(foot_body, (sds(OWN, FOOT), sds(SLOTS, COLS, dtype=BF16)), [VMEM] *...  3.44 us
    ppermute x2, waiting for transfers between devices, swapped(): lax.ppermute(x[1], ('gx', 'gy'), two)  2.39 us
    pallas_call x1, Pallas kernels, on_device(): call(prep_body, (sds(L, ROWS, COLS), sds(ROWS, COLS), sds((L + 2) * 8, CO...  1.92 us
  transfers between devices with their start and end apart: 7, of which 4 were waited for; matrix products, arithmetic and copies ran while one was open for 0% of the time, Pallas kernels for 19%

profile of v6, /device:TPU:1, one launch (start us, length us, event | category | flops | bytes accessed | tf_op | source)
XLA Modules:
  0.0 61.0 jit_solution(15172143160747617393)
XLA Ops:
  0.6 1.9 %prep.1 = (f32[32,64,128]{2,1,0:T(8,128)S(1)}, f32[64,128]{1,0:T(8,128)S(1)}, bf16[272,128]{1,0:T(8,128)(2,1)S(1)}, f32[64,128]{1,0:T(8,128)S(1)}, f32[32,128]{1...) custom-call(f32[12]{0:T(128)} %classes_hbm.1, f32[64,128]{1,0:T(8,128)} %inflow_hbm.1, ...), custom_call_target="tpu_custom_call" | custom-call | flops 20000000 | bytes 2000000 | tf_op jit(solution)/shard_map/prep/pallas_call | solution.py:460
  2.6 2.5 %collective-permute-start = (bf16[272,128]{1,0:T(8,128)(2,1)S(1)}, bf16[272,128]{1,0:T(8,128)(2,1)S(1)}, u32[]{:S(2)}, u32[]{:S(2)}) collective-permute-start(bf16[272,128]{1,0:T(8,128)(2,1)S(1)} %get-tuple-element.24), channel_id=1, source_target_pairs={{0,8},{8,0},{16,24},{24,16},{32,40},{40,32},{48,56},{56,48},{64,72... | collective-permute-start | bytes 208904 | tf_op jit(solution)/shard_map/ppermute | solution.py:447
  5.1 1.0 %collective-permute-start.1 = (bf16[272,128]{1,0:T(8,128)(2,1)S(1)}, bf16[272,128]{1,0:T(8,128)(2,1)S(1)}, u32[]{:S(2)}, u32[]{:S(2)}) collective-permute-start(bf16[272,128]{1,0:T(8,128)(2,1)S(1)} %get-tuple-element.24), channel_id=1, source_target_pairs={{0,1},{120,121},{8,16},{16,8},{24,32},{32,24},{40,48},{48,40},{56,... | collective-permute-start | bytes 208904 | tf_op jit(solution)/shard_map/ppermute | solution.py:447
  6.1 9.9 %all-to-all-start = ((bf16[128,4,128]{2,1,0:T(4,128)(2,1)}), bf16[128,4,128]{2,1,0:T(4,128)(2,1)S(1)}, u32[]{:S(2)}, u32[]{:S(2)}) async-start(bf16[128,4,128]{2,1,0:T(4,128)(2,1)} %bitcast.2), calls=%async_computation | async-start | bytes 262144 | tf_op jit(solution)/shard_map/all_to_all | solution.py:451
  16.0 0.0 collective-permute-done.a_ref
  16.0 0.0 collective-permute-done.1.b_ref
  16.0 0.9 %pack.1 = (f32[4,72,128]{2,1,0:T(8,128)S(1)}, f32[4,72,128]{2,1,0:T(8,128)S(1)}, bf16[144,128]{1,0:T(8,128)(2,1)S(1)}, bf16[144,128]{1,0:T(8,128)(2,1)S(1)}) custom-call(f32[32,64,128]{2,1,0:T(8,128)S(1)} %get-tuple-element.25.state_ref, f32[64,128]{1,0:T(8,128)S(1)} %get-tuple-element.23.conduct_ref, bf16[272,128]{1,0:T(8,128)(2,1)S(1)} %collective-permute-done.a_ref, ...), custom_call_target="tpu_custom_call" | custom-call | flops 20000000000 | bytes 1500000 | tf_op jit(solution)/shard_map/pack/pallas_call | solution.py:482
  16.9 1.1 %collective-permute-start.2 = (bf16[144,128]{1,0:T(8,128)(2,1)S(1)}, bf16[144,128]{1,0:T(8,128)(2,1)S(1)}, u32[]{:S(2)}, u32[]{:S(2)}) collective-permute-start(bf16[144,128]{1,0:T(8,128)(2,1)S(1)} %get-tuple-element.28), channel_id=1, source_target_pairs={{0,1},{1,0},{2,3},{3,2},{4,5},{5,4},{6,7},{7,6},{8,9},{9,8},{10,11... | collective-permute-start | bytes 110600 | tf_op jit(solution)/shard_map/ppermute | solution.py:447
  18.1 0.7 %collective-permute-start.3 = (bf16[144,128]{1,0:T(8,128)(2,1)S(1)}, bf16[144,128]{1,0:T(8,128)(2,1)S(1)}, u32[]{:S(2)}, u32[]{:S(2)}) collective-permute-start(bf16[144,128]{1,0:T(8,128)(2,1)S(1)} %get-tuple-element.29), channel_id=1, source_target_pairs={{0,8},{7,15},{1,2},{2,1},{3,4},{4,3},{5,6},{6,5},{8,0},{15,7},{9,1... | collective-permute-start | bytes 110600 | tf_op jit(solution)/shard_map/ppermute | solution.py:447
  18.8 0.6 tops.1.tops_ref
  19.3 0.0 collective-permute-done.2.pa_ref
  19.3 2.4 %collective-permute-done.3.pb_ref = bf16[144,128]{1,0:T(8,128)(2,1)S(1)} collective-permute-done((bf16[144,128]{1,0:T(8,128)(2,1)S(1)}, bf16[144,128]{1,0:T(8,128)(2,1)S(1)}, u32[]{:S(2)}, u32[]{:S(2)}) %collective-permute-start.3) | collective-permute-done | bytes 36896 | tf_op jit(solution)/shard_map/ppermute | solution.py:447
  21.7 1.4 %strips.1 = (f32[64,128]{1,0:T(8,128)S(1)}, f32[64,128]{1,0:T(8,128)S(1)}, f32[64,128]{1,0:T(8,128)S(1)}, bf16[128,128]{1,0:T(8,128)(2,1)S(1)}) custom-call(f32[4,72,128]{2,1,0:T(8,128)S(1)} %get-tuple-element.26.own_ref, f32[4,72,128]{2,1,0:T(8,128)S(1)} %get-tuple-element.27.cond_ref, bf16[144,128]{1,0:T(8,128)(2,1)S(1)} %collective-permute-done.2.pa_ref, ...), custom_call_target="tpu_custom_call" | custom-call | flops 10000000000 | bytes 1000000 | tf_op jit(solution)/shard_map/strips/pallas_call | solution.py:498
  23.2 2.8 %all-to-all-done = bf16[128,4,128]{2,1,0:T(4,128)(2,1)S(1)} async-done(((bf16[128,4,128]{2,1,0:T(4,128)(2,1)}), bf16[128,4,128]{2,1,0:T(4,128)(2,1)S(1)}, u32[]{:S(2)}, u32[]{:S(2)}) %all-to-all-start) | async-done | bytes 131104 | tf_op jit(solution)/shard_map/all_to_all | solution.py:451
  25.9 0.8 %serve.1 = bf16[512,128]{1,0:T(8,128)(2,1)} custom-call(bf16[512,128]{1,0:T(8,128)(2,1)S(1)} %bitcast.8, bf16[128,128]{1,0:T(8,128)(2,1)S(1)} %get-tuple-element.35.bright_ref), custom_call_target="tpu_custom_call" | custom-call | flops 20000000 | bytes 300000 | tf_op jit(solution)/shard_map/serve/pallas_call | solution.py:506
  26.8 5.8 %all-to-all-start.1 = ((bf16[128,4,128]{2,1,0:T(4,128)(2,1)}), bf16[128,4,128]{2,1,0:T(4,128)(2,1)S(1)}, u32[]{:S(2)}, u32[]{:S(2)}) async-start(bf16[128,4,128]{2,1,0:T(4,128)(2,1)} %bitcast.4), calls=%async_computation.1 | async-start | bytes 262144 | tf_op jit(solution)/shard_map/all_to_all | solution.py:451
  32.6 4.2 %upper.1 = (f32[32,64,128]{2,1,0:T(8,128)}, bf16[12,4,128,128]{3,2,1,0:T(8,128)(2,1)S(1)}, bf16[128,512]{1,0:T(8,128)(2,1)S(1)}) custom-call(f32[32,64,128]{2,1,0:T(8,128)S(1)} %get-tuple-element.25.state_ref, f32[64,128]{1,0:T(8,128)S(1)} %get-tuple-element.23.conduct_ref, bf16[272,128]{1,0:T(8,128)(2,1)S(1)} %collective-permute-done.a_ref, ...), custom_call_target="tpu_custom_call" | custom-call | flops 500000000 | bytes 3000000 | tf_op jit(solution)/shard_map/upper/pallas_call | solution.py:520
  36.8 5.8 %all-to-all-done.1 = bf16[128,4,128]{2,1,0:T(4,128)(2,1)S(1)} async-done(((bf16[128,4,128]{2,1,0:T(4,128)(2,1)}), bf16[128,4,128]{2,1,0:T(4,128)(2,1)S(1)}, u32[]{:S(2)}, u32[]{:S(2)}) %all-to-all-start.1) | async-done | bytes 131104 | tf_op jit(solution)/shard_map/all_to_all | solution.py:451
  42.5 3.4 %footprints.1 = (f32[32,128]{1,0:T(8,128)}, bf16[512,128]{1,0:T(8,128)(2,1)}) custom-call(bf16[512,128]{1,0:T(8,128)(2,1)S(1)} %bitcast.10, bf16[512,128]{1,0:T(8,128)(2,1)S(1)} %get-tuple-element.36.placing_ref, f32[32,128]{1,0:T(8,128)S(1)} %get-tuple-element.37.seen_ref, bf16[12,4,128,128]{3,2,1,0:T(8,128)(2,1)S(1)} %get-tuple-element.38.near_ref, ...), custom_call_target="tpu_custom_call" | custom-call | flops 20000000 | bytes 5000000 | tf_op jit(solution)/shard_map/footprints/pallas_call | solution.py:531
  46.0 4.3 %all-to-all-start.2 = ((bf16[128,4,128]{2,1,0:T(4,128)(2,1)}), bf16[128,4,128]{2,1,0:T(4,128)(2,1)S(1)}, u32[]{:S(2)}, u32[]{:S(2)}) async-start(bf16[128,4,128]{2,1,0:T(4,128)(2,1)} %bitcast.6), calls=%async_computation.2 | async-start | bytes 262144 | tf_op jit(solution)/shard_map/all_to_all | solution.py:451
  50.3 4.3 %lower.1 = f32[32,64,128]{2,1,0:T(8,128)} custom-call(f32[32,64,128]{2,1,0:T(8,128)} %state_hbm.3, f32[64,128]{1,0:T(8,128)S(1)} %get-tuple-element.23.conduct_ref, bf16[272,128]{1,0:T(8,128)(2,1)S(1)} %collective-permute-done.a_ref, bf16[272,128]{1,0:T(8,128)(2,1)S(1)} %collective-permute-done.1.b_ref, ...), custom_call_target="tpu_custom_call", output_to_operand_aliasing={{}: (6, {})} | custom-call | flops 500000000 | bytes 3000000 | tf_op jit(solution)/shard_map/lower/pallas_call | solution.py:544
  54.6 5.6 %all-to-all-done.2 = bf16[128,4,128]{2,1,0:T(4,128)(2,1)S(1)} async-done(((bf16[128,4,128]{2,1,0:T(4,128)(2,1)}), bf16[128,4,128]{2,1,0:T(4,128)(2,1)S(1)}, u32[]{:S(2)}, u32[]{:S(2)}) %all-to-all-start.2) | async-done | bytes 131104 | tf_op jit(solution)/shard_map/all_to_all | solution.py:451
  60.2 0.8 %gradient.1 = f32[2,64,128]{2,1,0:T(8,128)} custom-call(bf16[512,128]{1,0:T(8,128)(2,1)S(1)} %bitcast.11, bf16[128,512]{1,0:T(8,128)(2,1)S(1)} %get-tuple-element.41.across_ref, f32[64,128]{1,0:T(8,128)S(1)} %get-tuple-element.42.adjoint_ref), custom_call_target="tpu_custom_call" | custom-call | flops 20000000 | bytes 400000 | tf_op jit(solution)/shard_map/gradient/pallas_call | solution.py:555
Async XLA Ops:
  2.6 13.4 %collective-permute-start = (bf16[272,128]{1,0:T(8,128)(2,1)S(1)}, bf16[272,128]{1,0:T(8,128)(2,1)S(1)}, u32[]{:S(2)}, u32[]{:S(2)}) collective-permute-start(bf16[272,128]{1,0:T(8,128)(2,1)S(1)} %get-tuple-element.24), channel_id=1, source_target_pairs={{0,8},{8,0},{16,24},{24,16},{32,40},{40,32},{48,56},{56,48},{64,72... | collective-permute-start | bytes 208904 | tf_op jit(solution)/shard_map/ppermute | solution.py:447
  5.1 10.9 %collective-permute-start.1 = (bf16[272,128]{1,0:T(8,128)(2,1)S(1)}, bf16[272,128]{1,0:T(8,128)(2,1)S(1)}, u32[]{:S(2)}, u32[]{:S(2)}) collective-permute-start(bf16[272,128]{1,0:T(8,128)(2,1)S(1)} %get-tuple-element.24), channel_id=1, source_target_pairs={{0,1},{120,121},{8,16},{16,8},{24,32},{32,24},{40,48},{48,40},{56,... | collective-permute-start | bytes 208904 | tf_op jit(solution)/shard_map/ppermute | solution.py:447
  6.1 19.9 %all-to-all-start = ((bf16[128,4,128]{2,1,0:T(4,128)(2,1)}), bf16[128,4,128]{2,1,0:T(4,128)(2,1)S(1)}, u32[]{:S(2)}, u32[]{:S(2)}) async-start(bf16[128,4,128]{2,1,0:T(4,128)(2,1)} %bitcast.2), calls=%async_computation | async-start | bytes 262144 | tf_op jit(solution)/shard_map/all_to_all | solution.py:451
  16.9 2.4 %collective-permute-start.2 = (bf16[144,128]{1,0:T(8,128)(2,1)S(1)}, bf16[144,128]{1,0:T(8,128)(2,1)S(1)}, u32[]{:S(2)}, u32[]{:S(2)}) collective-permute-start(bf16[144,128]{1,0:T(8,128)(2,1)S(1)} %get-tuple-element.28), channel_id=1, source_target_pairs={{0,1},{1,0},{2,3},{3,2},{4,5},{5,4},{6,7},{7,6},{8,9},{9,8},{10,11... | collective-permute-start | bytes 110600 | tf_op jit(solution)/shard_map/ppermute | solution.py:447
  18.1 3.7 %collective-permute-start.3 = (bf16[144,128]{1,0:T(8,128)(2,1)S(1)}, bf16[144,128]{1,0:T(8,128)(2,1)S(1)}, u32[]{:S(2)}, u32[]{:S(2)}) collective-permute-start(bf16[144,128]{1,0:T(8,128)(2,1)S(1)} %get-tuple-element.29), channel_id=1, source_target_pairs={{0,8},{7,15},{1,2},{2,1},{3,4},{4,3},{5,6},{6,5},{8,0},{15,7},{9,1... | collective-permute-start | bytes 110600 | tf_op jit(solution)/shard_map/ppermute | solution.py:447
  26.8 15.8 %all-to-all-start.1 = ((bf16[128,4,128]{2,1,0:T(4,128)(2,1)}), bf16[128,4,128]{2,1,0:T(4,128)(2,1)S(1)}, u32[]{:S(2)}, u32[]{:S(2)}) async-start(bf16[128,4,128]{2,1,0:T(4,128)(2,1)} %bitcast.4), calls=%async_computation.1 | async-start | bytes 262144 | tf_op jit(solution)/shard_map/all_to_all | solution.py:451
  46.0 14.3 %all-to-all-start.2 = ((bf16[128,4,128]{2,1,0:T(4,128)(2,1)}), bf16[128,4,128]{2,1,0:T(4,128)(2,1)S(1)}, u32[]{:S(2)}, u32[]{:S(2)}) async-start(bf16[128,4,128]{2,1,0:T(4,128)(2,1)} %bitcast.6), calls=%async_computation.2 | async-start | bytes 262144 | tf_op jit(solution)/shard_map/all_to_all | solution.py:451

commit v7 on v6

--- a/solution.py
+++ b/solution.py
@@ -135,51 +135,52 @@
     return (k + cr * ur) * (ur - u) - (k + cl * ul) * (u - ul)
 
 
-def pack_body(state_ref, conduct_ref, a_ref, b_ref, own_ref, cond_ref, pa_ref, pb_ref):
-    halo = row_halo(a_ref, b_ref)
-    lane64 = iota((ROWS, COLS), 1)
-    lane8 = iota((8, COLS), 1)
-    shifts = (0, -4, 4, 8)
-
-    def pack(levels_of, lane):
-        acc = [jnp.zeros(lane.shape, F32) for _ in range(4)]
+def packed(state_ref, conduct_ref, halo, sides):
+    ahead = (0, 1, -1, -2)
+
+    def pack(level_of, lane):
+        acc = [jnp.zeros(lane.shape, F32) for _ in sides]
+        group = lane // 4
         for l in range(L):
-            turned = levels_of(l)
-            if l:
-                turned = pltpu.roll(turned, 4 * l, 1)
-            group = lane // 4
-            for i, at in enumerate((l, (l + 1) % L, (l - 1) % L, (l - 2) % L)):
-                acc[i] = jnp.where(group == at, turned, acc[i])
-        return [pltpu.roll(x, s % COLS, 1) if s else x for x, s in zip(acc, shifts)]
+            x = pltpu.roll(level_of(l), 4 * l, 1) if l else level_of(l)
+            for i, side in enumerate(sides):
+                acc[i] = jnp.where(group == (l + ahead[side]) % L, x, acc[i])
+        turns = [-4 * ahead[side] % COLS for side in sides]
+        return [pltpu.roll(x, t, 1) if t else x for x, t in zip(acc, turns)]
 
     def spread(x, lane):
         out = []
-        for s in (0, COLS - 4, 4, 8):
-            y = jnp.where(lane < 4, pltpu.roll(x, s, 1) if s else x, 0.0)
+        for side in sides:
+            t = -4 * ahead[side] % COLS
+            y = jnp.where(lane < 4, pltpu.roll(x, t, 1) if t else x, 0.0)
             for d in (4, 8, 16, 32, 64):
                 y = y + pltpu.roll(y, d, 1)
             out.append(y)
         return out
 
-    main = pack(lambda l: state_ref[l], lane64)
-    ends = pack(lambda l: halo[l], lane8)
-    cmain = spread(conduct_ref[...], lane64)
-    cends = spread(halo[L], lane8)
-    packs = [jnp.concatenate([m, e], axis=0) for m, e in zip(main, ends)]
+    lane64, lane8 = iota((ROWS, COLS), 1), iota((8, COLS), 1)
+    main, ends = pack(lambda l: state_ref[l], lane64), pack(lambda l: halo[l], lane8)
+    cmain, cends = spread(conduct_ref[...], lane64), spread(halo[L], lane8)
+    states = [jnp.concatenate([m, e], axis=0) for m, e in zip(main, ends)]
     conds = [jnp.concatenate([m, e], axis=0) for m, e in zip(cmain, cends)]
-    for i in range(4):
-        own_ref[i] = packs[i]
+    return states, conds
+
+
+def pack_body(state_ref, conduct_ref, a_ref, b_ref, own_ref, cond_ref, pa_ref, pb_ref):
+    states, conds = packed(state_ref, conduct_ref, row_halo(a_ref, b_ref), (0, 2))
+    for i in range(2):
+        own_ref[i] = states[i]
         cond_ref[i] = conds[i]
     odd = lax.rem(lax.axis_index("gy"), 2)
-    left = jnp.concatenate([packs[0], conds[0]], axis=0)
-    right = jnp.concatenate([packs[2], conds[2]], axis=0)
+    left = jnp.concatenate([states[0], conds[0]], axis=0)
+    right = jnp.concatenate([states[1], conds[1]], axis=0)
     is_odd = (jnp.zeros((2 * WIDE, COLS), jnp.int32) + odd) > 0
     pa_ref[...] = jnp.where(is_odd, left, right).astype(BF16)
     pb_ref[...] = jnp.where(is_odd, right, left).astype(BF16)
 
 
 def strip_body(
-    own_ref, cond_ref, pa_ref, pb_ref, tops_ref, thermal_ref,
+    own_ref, cond_ref, inner_ref, inner_cond_ref, pa_ref, pb_ref, tops_ref, thermal_ref,
     left_ref, right_ref, adjoint_ref, bright_ref, u_ref, v_ref, c_ref, cd_ref, cr_ref, cl_ref, lower_ref, upper_ref,
 ):
     gy = lax.axis_index("gy")
@@ -201,9 +202,9 @@
     sources = (
         (from_left[:WIDE], from_left[WIDE:]),
         (own_ref[0], cond_ref[0]),
+        (inner_ref[0], inner_cond_ref[0]),
+        (inner_ref[1], inner_cond_ref[1]),
         (own_ref[1], cond_ref[1]),
-        (own_ref[3], cond_ref[3]),
-        (own_ref[2], cond_ref[2]),
         (from_right[:WIDE], from_right[WIDE:]),
     )
     for i, (s, c) in enumerate(sources):
@@ -321,7 +322,14 @@
     return jnp.concatenate(parts, axis=1)
 
 
-def tops_body(state_ref, conduct_ref, a_ref, b_ref, tops_ref, u_ref, c_ref):
+def tops_body(
+    state_ref, conduct_ref, a_ref, b_ref, tops_ref, inner_ref, inner_cond_ref, u_ref, c_ref
+):
+    states, conds = packed(state_ref, conduct_ref, row_halo(a_ref, b_ref), (1, 3))
+    for i in range(2):
+        inner_ref[i] = states[i]
+        inner_cond_ref[i] = conds[i]
+
     def finish(l, new):
         tops_ref[l] = new
 
@@ -481,15 +489,15 @@
     picker = exchange(request)
     own, cond, pa, pb = call(
         pack_body,
-        (sds(4, WIDE, COLS), sds(4, WIDE, COLS), sds(2 * WIDE, COLS, dtype=BF16), sds(2 * WIDE, COLS, dtype=BF16)),
+        (sds(2, WIDE, COLS), sds(2, WIDE, COLS), sds(2 * WIDE, COLS, dtype=BF16), sds(2 * WIDE, COLS, dtype=BF16)),
         [VMEM] * 4,
         "pack",
         flops=20_000_000_000, moved=1_500_000,
     )(held_state, conduct, xa, xb)
     ya, yb = swapped((pa, pb), "gy")
-    tops = call(
+    tops, inner, inner_cond = call(
         tops_body,
-        sds(2, ROWS, COLS),
+        (sds(2, ROWS, COLS), sds(2, WIDE, COLS), sds(2, WIDE, COLS)),
         [VMEM] * 4,
         "tops",
         [pltpu.VMEM((STEPS + 2, WIDE, COLS), F32), pltpu.VMEM((4, WIDE, COLS), F32)],
@@ -498,11 +506,11 @@
     left, right, adjoint, bright = call(
         strip_body,
         (sds(ROWS, COLS), sds(ROWS, COLS), sds(ROWS, COLS), sds(COLS, COLS, dtype=BF16)),
-        [VMEM] * 6,
+        [VMEM] * 8,
         "strips",
         [pltpu.VMEM((6, WIDE, COLS), F32)] * 8,
         flops=10_000_000_000, moved=1_000_000,
-    )(own, cond, ya, yb, tops, warm)
+    )(own, cond, inner, inner_cond, ya, yb, tops, warm)
     served = call(
         serve_body,
         sds(SLOTS, COLS, dtype=BF16),

time: 61.4 us -> 61.2 us (level)
  Pallas kernels: 18.3 us -> 19.7 us
  waiting for transfers between devices: 16.6 us -> 15.3 us
    ppermute x2, waiting for transfers between devices: 2.39 us -> 0.84 us  [swapped(): lax.ppermute(x[1], ('gx', 'gy'), two)]
    pallas_call x2, Pallas kernels: 1.46 us -> 2.8 us  [the longest x1 2.11 us: on_device(): call(tops_body, (sds(2, ROWS, COLS), sds(2, WIDE, COLS), sds(2, WIDE, COL...]
  transfers between devices with their start and end apart: 7 -> 7, of which waited for: 4 -> 4; matrix products, arithmetic and copies ran while one was open for 0% -> 0% of each run, Pallas kernels for 19% -> 21%
where the time goes in v7:
time: 61.2 us; the launch traced here: 60.8 us
  starting transfers between devices  25.1 us (41%)
  Pallas kernels  19.7 us (32%)
  waiting for transfers between devices  15.3 us (25%)
  between operations  0.73 us (1%)
    all_to_all x3, starting transfers between devices, exchange(): lax.all_to_all(x.reshape(TILES, CAP, COLS), ('gx', 'gy'), split_axis=0, c...  19.8 us
    all_to_all x3, waiting for transfers between devices, exchange(): lax.all_to_all(x.reshape(TILES, CAP, COLS), ('gx', 'gy'), split_axis=0, c...  14.4 us
    pallas_call x1, Pallas kernels, on_device(): call(lower_body, sds(L, ROWS, COLS), [HBM] + [VMEM] * 5 + [HBM], 'lower',...  4.31 us
    pallas_call x1, Pallas kernels, on_device(): call(upper_body, (sds(L, ROWS, COLS), sds(NEAR, TOUCH, FOOT, COLS, dtype=...  4.18 us
    ppermute x2, starting transfers between devices, swapped(): lax.ppermute(x[0], axis, one)  3.69 us
    pallas_call x1, Pallas kernels, on_device(): call(foot_body, (sds(OWN, FOOT), sds(SLOTS, COLS, dtype=BF16)), [VMEM] *...  3.45 us
    pallas_call x1, Pallas kernels, on_device(): call(tops_body, (sds(2, ROWS, COLS), sds(2, WIDE, COLS), sds(2, WIDE, COL...  2.11 us
    pallas_call x1, Pallas kernels, on_device(): call(prep_body, (sds(L, ROWS, COLS), sds(ROWS, COLS), sds((L + 2) * 8, CO...  1.92 us
  transfers between devices with their start and end apart: 7, of which 4 were waited for; matrix products, arithmetic and copies ran while one was open for 0% of the time, Pallas kernels for 21%

profile of v7, /device:TPU:1, one launch (start us, length us, event | category | flops | bytes accessed | tf_op | source)
XLA Modules:
  0.0 60.8 jit_solution(9592675980152263306)
XLA Ops:
  0.6 1.9 %prep.1 = (f32[32,64,128]{2,1,0:T(8,128)S(1)}, f32[64,128]{1,0:T(8,128)S(1)}, bf16[272,128]{1,0:T(8,128)(2,1)S(1)}, f32[64,128]{1,0:T(8,128)S(1)}, f32[32,128]{1...) custom-call(f32[12]{0:T(128)} %classes_hbm.1, f32[64,128]{1,0:T(8,128)} %inflow_hbm.1, ...), custom_call_target="tpu_custom_call" | custom-call | flops 20000000 | bytes 2000000 | tf_op jit(solution)/shard_map/prep/pallas_call | solution.py:468
  2.6 2.5 %collective-permute-start = (bf16[272,128]{1,0:T(8,128)(2,1)S(1)}, bf16[272,128]{1,0:T(8,128)(2,1)S(1)}, u32[]{:S(2)}, u32[]{:S(2)}) collective-permute-start(bf16[272,128]{1,0:T(8,128)(2,1)S(1)} %get-tuple-element.27), channel_id=1, source_target_pairs={{0,8},{8,0},{16,24},{24,16},{32,40},{40,32},{48,56},{56,48},{64,72... | collective-permute-start | bytes 208904 | tf_op jit(solution)/shard_map/ppermute | solution.py:455
  5.1 1.0 %collective-permute-start.1 = (bf16[272,128]{1,0:T(8,128)(2,1)S(1)}, bf16[272,128]{1,0:T(8,128)(2,1)S(1)}, u32[]{:S(2)}, u32[]{:S(2)}) collective-permute-start(bf16[272,128]{1,0:T(8,128)(2,1)S(1)} %get-tuple-element.27), channel_id=1, source_target_pairs={{0,1},{120,121},{8,16},{16,8},{24,32},{32,24},{40,48},{48,40},{56,... | collective-permute-start | bytes 208904 | tf_op jit(solution)/shard_map/ppermute | solution.py:455
  6.1 9.9 %all-to-all-start = ((bf16[128,4,128]{2,1,0:T(4,128)(2,1)}), bf16[128,4,128]{2,1,0:T(4,128)(2,1)S(1)}, u32[]{:S(2)}, u32[]{:S(2)}) async-start(bf16[128,4,128]{2,1,0:T(4,128)(2,1)} %bitcast.2), calls=%async_computation | async-start | bytes 262144 | tf_op jit(solution)/shard_map/all_to_all | solution.py:459
  16.0 0.0 collective-permute-done.a_ref
  16.0 0.0 collective-permute-done.1.b_ref
  16.0 0.7 %pack.1 = (f32[2,72,128]{2,1,0:T(8,128)S(1)}, f32[2,72,128]{2,1,0:T(8,128)S(1)}, bf16[144,128]{1,0:T(8,128)(2,1)S(1)}, bf16[144,128]{1,0:T(8,128)(2,1)S(1)}) custom-call(f32[32,64,128]{2,1,0:T(8,128)S(1)} %get-tuple-element.28.state_ref, f32[64,128]{1,0:T(8,128)S(1)} %get-tuple-element.26.conduct_ref, bf16[272,128]{1,0:T(8,128)(2,1)S(1)} %collective-permute-done.a_ref, ...), custom_call_target="tpu_custom_call" | custom-call | flops 20000000000 | bytes 1500000 | tf_op jit(solution)/shard_map/pack/pallas_call | solution.py:490
  16.7 1.1 %collective-permute-start.2 = (bf16[144,128]{1,0:T(8,128)(2,1)S(1)}, bf16[144,128]{1,0:T(8,128)(2,1)S(1)}, u32[]{:S(2)}, u32[]{:S(2)}) collective-permute-start(bf16[144,128]{1,0:T(8,128)(2,1)S(1)} %get-tuple-element.33), channel_id=1, source_target_pairs={{0,1},{1,0},{2,3},{3,2},{4,5},{5,4},{6,7},{7,6},{8,9},{9,8},{10,11... | collective-permute-start | bytes 110600 | tf_op jit(solution)/shard_map/ppermute | solution.py:455
  17.8 0.7 %collective-permute-start.3 = (bf16[144,128]{1,0:T(8,128)(2,1)S(1)}, bf16[144,128]{1,0:T(8,128)(2,1)S(1)}, u32[]{:S(2)}, u32[]{:S(2)}) collective-permute-start(bf16[144,128]{1,0:T(8,128)(2,1)S(1)} %get-tuple-element.34), channel_id=1, source_target_pairs={{0,8},{7,15},{1,2},{2,1},{3,4},{4,3},{5,6},{6,5},{8,0},{15,7},{9,1... | collective-permute-start | bytes 110600 | tf_op jit(solution)/shard_map/ppermute | solution.py:455
  18.6 2.1 %tops.1 = (f32[2,64,128]{2,1,0:T(8,128)S(1)}, f32[2,72,128]{2,1,0:T(8,128)S(1)}, f32[2,72,128]{2,1,0:T(8,128)S(1)}) custom-call(f32[32,64,128]{2,1,0:T(8,128)S(1)} %get-tuple-element.28.state_ref, f32[64,128]{1,0:T(8,128)S(1)} %get-tuple-element.26.conduct_ref, bf16[272,128]{1,0:T(8,128)(2,1)S(1)} %collective-permute-done.a_ref, ...), custom_call_target="tpu_custom_call" | custom-call | flops 20000000000 | bytes 1000000 | tf_op jit(solution)/shard_map/tops/pallas_call | solution.py:498
  20.7 0.0 collective-permute-done.2.pa_ref
  20.7 0.8 %collective-permute-done.3.pb_ref = bf16[144,128]{1,0:T(8,128)(2,1)S(1)} collective-permute-done((bf16[144,128]{1,0:T(8,128)(2,1)S(1)}, bf16[144,128]{1,0:T(8,128)(2,1)S(1)}, u32[]{:S(2)}, u32[]{:S(2)}) %collective-permute-start.3) | collective-permute-done | bytes 36896 | tf_op jit(solution)/shard_map/ppermute | solution.py:455
  21.5 1.4 %strips.1 = (f32[64,128]{1,0:T(8,128)S(1)}, f32[64,128]{1,0:T(8,128)S(1)}, f32[64,128]{1,0:T(8,128)S(1)}, bf16[128,128]{1,0:T(8,128)(2,1)S(1)}) custom-call(f32[2,72,128]{2,1,0:T(8,128)S(1)} %get-tuple-element.29.own_ref, f32[2,72,128]{2,1,0:T(8,128)S(1)} %get-tuple-element.30.cond_ref, f32[2,72,128]{2,1,0:T(8,128)S(1)} %get-tuple-element.31.inner_ref, ...), custom_call_target="tpu_custom_call" | custom-call | flops 10000000000 | bytes 1000000 | tf_op jit(solution)/shard_map/strips/pallas_call | solution.py:506
  23.0 3.0 %all-to-all-done = bf16[128,4,128]{2,1,0:T(4,128)(2,1)S(1)} async-done(((bf16[128,4,128]{2,1,0:T(4,128)(2,1)}), bf16[128,4,128]{2,1,0:T(4,128)(2,1)S(1)}, u32[]{:S(2)}, u32[]{:S(2)}) %all-to-all-start) | async-done | bytes 131104 | tf_op jit(solution)/shard_map/all_to_all | solution.py:459
  25.9 0.8 %serve.1 = bf16[512,128]{1,0:T(8,128)(2,1)} custom-call(bf16[512,128]{1,0:T(8,128)(2,1)S(1)} %bitcast.8, bf16[128,128]{1,0:T(8,128)(2,1)S(1)} %get-tuple-element.41.bright_ref), custom_call_target="tpu_custom_call" | custom-call | flops 20000000 | bytes 300000 | tf_op jit(solution)/shard_map/serve/pallas_call | solution.py:514
  26.8 5.6 %all-to-all-start.1 = ((bf16[128,4,128]{2,1,0:T(4,128)(2,1)}), bf16[128,4,128]{2,1,0:T(4,128)(2,1)S(1)}, u32[]{:S(2)}, u32[]{:S(2)}) async-start(bf16[128,4,128]{2,1,0:T(4,128)(2,1)} %bitcast.4), calls=%async_computation.1 | async-start | bytes 262144 | tf_op jit(solution)/shard_map/all_to_all | solution.py:459
  32.4 4.2 %upper.1 = (f32[32,64,128]{2,1,0:T(8,128)}, bf16[12,4,128,128]{3,2,1,0:T(8,128)(2,1)S(1)}, bf16[128,512]{1,0:T(8,128)(2,1)S(1)}) custom-call(f32[32,64,128]{2,1,0:T(8,128)S(1)} %get-tuple-element.28.state_ref, f32[64,128]{1,0:T(8,128)S(1)} %get-tuple-element.26.conduct_ref, bf16[272,128]{1,0:T(8,128)(2,1)S(1)} %collective-permute-done.a_ref, ...), custom_call_target="tpu_custom_call" | custom-call | flops 500000000 | bytes 3000000 | tf_op jit(solution)/shard_map/upper/pallas_call | solution.py:528
  36.6 5.8 %all-to-all-done.1 = bf16[128,4,128]{2,1,0:T(4,128)(2,1)S(1)} async-done(((bf16[128,4,128]{2,1,0:T(4,128)(2,1)}), bf16[128,4,128]{2,1,0:T(4,128)(2,1)S(1)}, u32[]{:S(2)}, u32[]{:S(2)}) %all-to-all-start.1) | async-done | bytes 131104 | tf_op jit(solution)/shard_map/all_to_all | solution.py:459
  42.3 3.4 %footprints.1 = (f32[32,128]{1,0:T(8,128)}, bf16[512,128]{1,0:T(8,128)(2,1)}) custom-call(bf16[512,128]{1,0:T(8,128)(2,1)S(1)} %bitcast.10, bf16[512,128]{1,0:T(8,128)(2,1)S(1)} %get-tuple-element.42.placing_ref, f32[32,128]{1,0:T(8,128)S(1)} %get-tuple-element.43.seen_ref, bf16[12,4,128,128]{3,2,1,0:T(8,128)(2,1)S(1)} %get-tuple-element.44.near_ref, ...), custom_call_target="tpu_custom_call" | custom-call | flops 20000000 | bytes 5000000 | tf_op jit(solution)/shard_map/footprints/pallas_call | solution.py:539
  45.8 4.3 %all-to-all-start.2 = ((bf16[128,4,128]{2,1,0:T(4,128)(2,1)}), bf16[128,4,128]{2,1,0:T(4,128)(2,1)S(1)}, u32[]{:S(2)}, u32[]{:S(2)}) async-start(bf16[128,4,128]{2,1,0:T(4,128)(2,1)} %bitcast.6), calls=%async_computation.2 | async-start | bytes 262144 | tf_op jit(solution)/shard_map/all_to_all | solution.py:459
  50.1 4.3 %lower.1 = f32[32,64,128]{2,1,0:T(8,128)} custom-call(f32[32,64,128]{2,1,0:T(8,128)} %state_hbm.3, f32[64,128]{1,0:T(8,128)S(1)} %get-tuple-element.26.conduct_ref, bf16[272,128]{1,0:T(8,128)(2,1)S(1)} %collective-permute-done.a_ref, bf16[272,128]{1,0:T(8,128)(2,1)S(1)} %collective-permute-done.1.b_ref, ...), custom_call_target="tpu_custom_call", output_to_operand_aliasing={{}: (6, {})} | custom-call | flops 500000000 | bytes 3000000 | tf_op jit(solution)/shard_map/lower/pallas_call | solution.py:552
  54.4 5.6 %all-to-all-done.2 = bf16[128,4,128]{2,1,0:T(4,128)(2,1)S(1)} async-done(((bf16[128,4,128]{2,1,0:T(4,128)(2,1)}), bf16[128,4,128]{2,1,0:T(4,128)(2,1)S(1)}, u32[]{:S(2)}, u32[]{:S(2)}) %all-to-all-start.2) | async-done | bytes 131104 | tf_op jit(solution)/shard_map/all_to_all | solution.py:459
  60.0 0.8 %gradient.1 = f32[2,64,128]{2,1,0:T(8,128)} custom-call(bf16[512,128]{1,0:T(8,128)(2,1)S(1)} %bitcast.11, bf16[128,512]{1,0:T(8,128)(2,1)S(1)} %get-tuple-element.47.across_ref, f32[64,128]{1,0:T(8,128)S(1)} %get-tuple-element.48.adjoint_ref), custom_call_target="tpu_custom_call" | custom-call | flops 20000000 | bytes 400000 | tf_op jit(solution)/shard_map/gradient/pallas_call | solution.py:563
Async XLA Ops:
  2.6 13.4 %collective-permute-start = (bf16[272,128]{1,0:T(8,128)(2,1)S(1)}, bf16[272,128]{1,0:T(8,128)(2,1)S(1)}, u32[]{:S(2)}, u32[]{:S(2)}) collective-permute-start(bf16[272,128]{1,0:T(8,128)(2,1)S(1)} %get-tuple-element.27), channel_id=1, source_target_pairs={{0,8},{8,0},{16,24},{24,16},{32,40},{40,32},{48,56},{56,48},{64,72... | collective-permute-start | bytes 208904 | tf_op jit(solution)/shard_map/ppermute | solution.py:455
  5.1 10.9 %collective-permute-start.1 = (bf16[272,128]{1,0:T(8,128)(2,1)S(1)}, bf16[272,128]{1,0:T(8,128)(2,1)S(1)}, u32[]{:S(2)}, u32[]{:S(2)}) collective-permute-start(bf16[272,128]{1,0:T(8,128)(2,1)S(1)} %get-tuple-element.27), channel_id=1, source_target_pairs={{0,1},{120,121},{8,16},{16,8},{24,32},{32,24},{40,48},{48,40},{56,... | collective-permute-start | bytes 208904 | tf_op jit(solution)/shard_map/ppermute | solution.py:455
  6.1 19.9 %all-to-all-start = ((bf16[128,4,128]{2,1,0:T(4,128)(2,1)}), bf16[128,4,128]{2,1,0:T(4,128)(2,1)S(1)}, u32[]{:S(2)}, u32[]{:S(2)}) async-start(bf16[128,4,128]{2,1,0:T(4,128)(2,1)} %bitcast.2), calls=%async_computation | async-start | bytes 262144 | tf_op jit(solution)/shard_map/all_to_all | solution.py:459
  16.7 4.0 %collective-permute-start.2 = (bf16[144,128]{1,0:T(8,128)(2,1)S(1)}, bf16[144,128]{1,0:T(8,128)(2,1)S(1)}, u32[]{:S(2)}, u32[]{:S(2)}) collective-permute-start(bf16[144,128]{1,0:T(8,128)(2,1)S(1)} %get-tuple-element.33), channel_id=1, source_target_pairs={{0,1},{1,0},{2,3},{3,2},{4,5},{5,4},{6,7},{7,6},{8,9},{9,8},{10,11... | collective-permute-start | bytes 110600 | tf_op jit(solution)/shard_map/ppermute | solution.py:455
  17.8 3.7 %collective-permute-start.3 = (bf16[144,128]{1,0:T(8,128)(2,1)S(1)}, bf16[144,128]{1,0:T(8,128)(2,1)S(1)}, u32[]{:S(2)}, u32[]{:S(2)}) collective-permute-start(bf16[144,128]{1,0:T(8,128)(2,1)S(1)} %get-tuple-element.34), channel_id=1, source_target_pairs={{0,8},{7,15},{1,2},{2,1},{3,4},{4,3},{5,6},{6,5},{8,0},{15,7},{9,1... | collective-permute-start | bytes 110600 | tf_op jit(solution)/shard_map/ppermute | solution.py:455
  26.8 15.5 %all-to-all-start.1 = ((bf16[128,4,128]{2,1,0:T(4,128)(2,1)}), bf16[128,4,128]{2,1,0:T(4,128)(2,1)S(1)}, u32[]{:S(2)}, u32[]{:S(2)}) async-start(bf16[128,4,128]{2,1,0:T(4,128)(2,1)} %bitcast.4), calls=%async_computation.1 | async-start | bytes 262144 | tf_op jit(solution)/shard_map/all_to_all | solution.py:459
  45.8 14.3 %all-to-all-start.2 = ((bf16[128,4,128]{2,1,0:T(4,128)(2,1)}), bf16[128,4,128]{2,1,0:T(4,128)(2,1)S(1)}, u32[]{:S(2)}, u32[]{:S(2)}) async-start(bf16[128,4,128]{2,1,0:T(4,128)(2,1)} %bitcast.6), calls=%async_computation.2 | async-start | bytes 262144 | tf_op jit(solution)/shard_map/all_to_all | solution.py:459

commit v8 on v7

--- a/solution.py
+++ b/solution.py
@@ -267,8 +267,20 @@
     bright_ref[...] = jnp.concatenate([bright, jnp.zeros((COLS - ROWS, COLS), BF16)], axis=0)
 
 
-def serve_body(picker_ref, bright_ref, served_ref):
-    served_ref[...] = dot(picker_ref[...], bright_ref[...], 1, 0).astype(BF16)
+def sent(left_ref, right, out_hbm, held_ref, sems):
+    half = SLOTS // 2
+    copies = []
+    for i in range(2):
+        span = pl.ds(i * half, half)
+        held_ref[span, :] = dot(left_ref[span, :], right, 1, 0).astype(BF16)
+        copies.append(pltpu.make_async_copy(held_ref.at[span], out_hbm.at[span], sems.at[i]))
+        copies[i].start()
+    for copy in copies:
+        copy.wait()
+
+
+def serve_body(picker_ref, bright_ref, served_hbm, held_ref, sems):
+    sent(picker_ref, bright_ref[...], served_hbm, held_ref, sems)
 
 
 def wide_conduct(conduct_ref, halo):
@@ -390,7 +402,7 @@
 
 def foot_body(
     returned_ref, placing_ref, seen_ref, near_ref, weights_hbm,
-    bright_ref, outgoing_ref, cells_ref, contrib_ref, weights_ref, sems,
+    bright_ref, outgoing_hbm, cells_ref, contrib_ref, weights_ref, sems, leaving_ref, leaving_sems,
 ):
     copies = {}
     at = NEAR
@@ -430,7 +442,7 @@
         bright_ref[start : start + PART, :] = evolved
         misfit = (evolved - seen_ref[start : start + PART, :]).astype(BF16)
     adjoint(OWN - PART, misfit)
-    outgoing_ref[...] = dot(placing, contrib_ref[...].astype(BF16), 1, 0).astype(BF16)
+    sent(placing_ref, contrib_ref[...].astype(BF16), outgoing_hbm, leaving_ref, leaving_sems)
 
 
 def gradient_body(grads_ref, across_ref, adjoint_ref, out_ref):
@@ -516,6 +528,8 @@
         sds(SLOTS, COLS, dtype=BF16),
         [VMEM] * 2,
         "serve",
+        [pltpu.VMEM((SLOTS, COLS), BF16), pltpu.SemaphoreType.DMA((2,))],
+        out_specs=HBM,
         flops=20_000_000, moved=300_000,
     )(picker, bright)
     returned = exchange(served)
@@ -546,7 +560,10 @@
             pltpu.VMEM((REFS, COLS), F32),
             pltpu.VMEM(weights.shape, BF16),
             pltpu.SemaphoreType.DMA((len(CHUNKS),)),
+            pltpu.VMEM((SLOTS, COLS), BF16),
+            pltpu.SemaphoreType.DMA((2,)),
         ],
+        out_specs=(VMEM, HBM),
         flops=20_000_000, moved=5_000_000,
     )(returned, placing, seen, near, far(weights))
     moisture = call(

time: 61.2 us -> 61.8 us (level)
  no operation moved by 1% of the time
where the time goes in v8:
time: 61.8 us; the launch traced here: 61.4 us
  starting transfers between devices  25.1 us (41%)
  Pallas kernels  20.3 us (33%)
  waiting for transfers between devices  15.3 us (25%)
  between operations  0.74 us (1%)
    all_to_all x3, starting transfers between devices, exchange(): lax.all_to_all(x.reshape(TILES, CAP, COLS), ('gx', 'gy'), split_axis=0, c...  19.8 us
    all_to_all x3, waiting for transfers between devices, exchange(): lax.all_to_all(x.reshape(TILES, CAP, COLS), ('gx', 'gy'), split_axis=0, c...  14.4 us
    pallas_call x1, Pallas kernels, on_device(): call(lower_body, sds(L, ROWS, COLS), [HBM] + [VMEM] * 5 + [HBM], 'lower',...  4.31 us
    pallas_call x1, Pallas kernels, on_device(): call(upper_body, (sds(L, ROWS, COLS), sds(NEAR, TOUCH, FOOT, COLS, dtype=...  4.18 us
    pallas_call x1, Pallas kernels, on_device(): call(foot_body, (sds(OWN, FOOT), sds(SLOTS, COLS, dtype=BF16)), [VMEM] *...  4.03 us
    ppermute x2, starting transfers between devices, swapped(): lax.ppermute(x[0], axis, one)  3.69 us
    pallas_call x1, Pallas kernels, on_device(): call(tops_body, (sds(2, ROWS, COLS), sds(2, WIDE, COLS), sds(2, WIDE, COL...  2.11 us
    pallas_call x1, Pallas kernels, on_device(): call(prep_body, (sds(L, ROWS, COLS), sds(ROWS, COLS), sds((L + 2) * 8, CO...  1.92 us
  transfers between devices with their start and end apart: 7, of which 4 were waited for; matrix products, arithmetic and copies ran while one was open for 0% of the time, Pallas kernels for 21%

profile of v8, /device:TPU:1, one launch (start us, length us, event | category | flops | bytes accessed | tf_op | source)
XLA Modules:
  0.0 61.4 jit_solution(1909341986257555569)
XLA Ops:
  0.6 1.9 %prep.1 = (f32[32,64,128]{2,1,0:T(8,128)S(1)}, f32[64,128]{1,0:T(8,128)S(1)}, bf16[272,128]{1,0:T(8,128)(2,1)S(1)}, f32[64,128]{1,0:T(8,128)S(1)}, f32[32,128]{1...) custom-call(f32[12]{0:T(128)} %classes_hbm.1, f32[64,128]{1,0:T(8,128)} %inflow_hbm.1, ...), custom_call_target="tpu_custom_call" | custom-call | flops 20000000 | bytes 2000000 | tf_op jit(solution)/shard_map/prep/pallas_call | solution.py:480
  2.6 2.5 %collective-permute-start = (bf16[272,128]{1,0:T(8,128)(2,1)S(1)}, bf16[272,128]{1,0:T(8,128)(2,1)S(1)}, u32[]{:S(2)}, u32[]{:S(2)}) collective-permute-start(bf16[272,128]{1,0:T(8,128)(2,1)S(1)} %get-tuple-element.27), channel_id=1, source_target_pairs={{0,8},{8,0},{16,24},{24,16},{32,40},{40,32},{48,56},{56,48},{64,72... | collective-permute-start | bytes 208904 | tf_op jit(solution)/shard_map/ppermute | solution.py:467
  5.1 1.0 %collective-permute-start.1 = (bf16[272,128]{1,0:T(8,128)(2,1)S(1)}, bf16[272,128]{1,0:T(8,128)(2,1)S(1)}, u32[]{:S(2)}, u32[]{:S(2)}) collective-permute-start(bf16[272,128]{1,0:T(8,128)(2,1)S(1)} %get-tuple-element.27), channel_id=1, source_target_pairs={{0,1},{120,121},{8,16},{16,8},{24,32},{32,24},{40,48},{48,40},{56,... | collective-permute-start | bytes 208904 | tf_op jit(solution)/shard_map/ppermute | solution.py:467
  6.1 9.9 %all-to-all-start = ((bf16[128,4,128]{2,1,0:T(4,128)(2,1)}), bf16[128,4,128]{2,1,0:T(4,128)(2,1)S(1)}, u32[]{:S(2)}, u32[]{:S(2)}) async-start(bf16[128,4,128]{2,1,0:T(4,128)(2,1)} %bitcast.2), calls=%async_computation | async-start | bytes 262144 | tf_op jit(solution)/shard_map/all_to_all | solution.py:471
  16.0 0.0 collective-permute-done.a_ref
  16.0 0.0 collective-permute-done.1.b_ref
  16.0 0.7 %pack.1 = (f32[2,72,128]{2,1,0:T(8,128)S(1)}, f32[2,72,128]{2,1,0:T(8,128)S(1)}, bf16[144,128]{1,0:T(8,128)(2,1)S(1)}, bf16[144,128]{1,0:T(8,128)(2,1)S(1)}) custom-call(f32[32,64,128]{2,1,0:T(8,128)S(1)} %get-tuple-element.28.state_ref, f32[64,128]{1,0:T(8,128)S(1)} %get-tuple-element.26.conduct_ref, bf16[272,128]{1,0:T(8,128)(2,1)S(1)} %collective-permute-done.a_ref, ...), custom_call_target="tpu_custom_call" | custom-call | flops 20000000000 | bytes 1500000 | tf_op jit(solution)/shard_map/pack/pallas_call | solution.py:502
  16.7 1.1 %collective-permute-start.2 = (bf16[144,128]{1,0:T(8,128)(2,1)S(1)}, bf16[144,128]{1,0:T(8,128)(2,1)S(1)}, u32[]{:S(2)}, u32[]{:S(2)}) collective-permute-start(bf16[144,128]{1,0:T(8,128)(2,1)S(1)} %get-tuple-element.33), channel_id=1, source_target_pairs={{0,1},{1,0},{2,3},{3,2},{4,5},{5,4},{6,7},{7,6},{8,9},{9,8},{10,11... | collective-permute-start | bytes 110600 | tf_op jit(solution)/shard_map/ppermute | solution.py:467
  17.8 0.7 %collective-permute-start.3 = (bf16[144,128]{1,0:T(8,128)(2,1)S(1)}, bf16[144,128]{1,0:T(8,128)(2,1)S(1)}, u32[]{:S(2)}, u32[]{:S(2)}) collective-permute-start(bf16[144,128]{1,0:T(8,128)(2,1)S(1)} %get-tuple-element.34), channel_id=1, source_target_pairs={{0,8},{7,15},{1,2},{2,1},{3,4},{4,3},{5,6},{6,5},{8,0},{15,7},{9,1... | collective-permute-start | bytes 110600 | tf_op jit(solution)/shard_map/ppermute | solution.py:467
  18.6 2.1 %tops.1 = (f32[2,64,128]{2,1,0:T(8,128)S(1)}, f32[2,72,128]{2,1,0:T(8,128)S(1)}, f32[2,72,128]{2,1,0:T(8,128)S(1)}) custom-call(f32[32,64,128]{2,1,0:T(8,128)S(1)} %get-tuple-element.28.state_ref, f32[64,128]{1,0:T(8,128)S(1)} %get-tuple-element.26.conduct_ref, bf16[272,128]{1,0:T(8,128)(2,1)S(1)} %collective-permute-done.a_ref, ...), custom_call_target="tpu_custom_call" | custom-call | flops 20000000000 | bytes 1000000 | tf_op jit(solution)/shard_map/tops/pallas_call | solution.py:510
  20.7 0.0 collective-permute-done.2.pa_ref
  20.7 0.8 %collective-permute-done.3.pb_ref = bf16[144,128]{1,0:T(8,128)(2,1)S(1)} collective-permute-done((bf16[144,128]{1,0:T(8,128)(2,1)S(1)}, bf16[144,128]{1,0:T(8,128)(2,1)S(1)}, u32[]{:S(2)}, u32[]{:S(2)}) %collective-permute-start.3) | collective-permute-done | bytes 36896 | tf_op jit(solution)/shard_map/ppermute | solution.py:467
  21.5 1.4 %strips.1 = (f32[64,128]{1,0:T(8,128)S(1)}, f32[64,128]{1,0:T(8,128)S(1)}, f32[64,128]{1,0:T(8,128)S(1)}, bf16[128,128]{1,0:T(8,128)(2,1)S(1)}) custom-call(f32[2,72,128]{2,1,0:T(8,128)S(1)} %get-tuple-element.29.own_ref, f32[2,72,128]{2,1,0:T(8,128)S(1)} %get-tuple-element.30.cond_ref, f32[2,72,128]{2,1,0:T(8,128)S(1)} %get-tuple-element.31.inner_ref, ...), custom_call_target="tpu_custom_call" | custom-call | flops 10000000000 | bytes 1000000 | tf_op jit(solution)/shard_map/strips/pallas_call | solution.py:518
  23.0 3.0 %all-to-all-done = bf16[128,4,128]{2,1,0:T(4,128)(2,1)S(1)} async-done(((bf16[128,4,128]{2,1,0:T(4,128)(2,1)}), bf16[128,4,128]{2,1,0:T(4,128)(2,1)S(1)}, u32[]{:S(2)}, u32[]{:S(2)}) %all-to-all-start) | async-done | bytes 131104 | tf_op jit(solution)/shard_map/all_to_all | solution.py:471
  25.9 0.8 %serve.1 = bf16[512,128]{1,0:T(8,128)(2,1)} custom-call(bf16[512,128]{1,0:T(8,128)(2,1)S(1)} %bitcast.8, bf16[128,128]{1,0:T(8,128)(2,1)S(1)} %get-tuple-element.41.bright_ref), custom_call_target="tpu_custom_call" | custom-call | flops 20000000 | bytes 300000 | tf_op jit(solution)/shard_map/serve/pallas_call | solution.py:526
  26.8 5.6 %all-to-all-start.1 = ((bf16[128,4,128]{2,1,0:T(4,128)(2,1)}), bf16[128,4,128]{2,1,0:T(4,128)(2,1)S(1)}, u32[]{:S(2)}, u32[]{:S(2)}) async-start(bf16[128,4,128]{2,1,0:T(4,128)(2,1)} %bitcast.4), calls=%async_computation.1 | async-start | bytes 262144 | tf_op jit(solution)/shard_map/all_to_all | solution.py:471
  32.4 4.2 %upper.1 = (f32[32,64,128]{2,1,0:T(8,128)}, bf16[12,4,128,128]{3,2,1,0:T(8,128)(2,1)S(1)}, bf16[128,512]{1,0:T(8,128)(2,1)S(1)}) custom-call(f32[32,64,128]{2,1,0:T(8,128)S(1)} %get-tuple-element.28.state_ref, f32[64,128]{1,0:T(8,128)S(1)} %get-tuple-element.26.conduct_ref, bf16[272,128]{1,0:T(8,128)(2,1)S(1)} %collective-permute-done.a_ref, ...), custom_call_target="tpu_custom_call" | custom-call | flops 500000000 | bytes 3000000 | tf_op jit(solution)/shard_map/upper/pallas_call | solution.py:542
  36.6 5.8 %all-to-all-done.1 = bf16[128,4,128]{2,1,0:T(4,128)(2,1)S(1)} async-done(((bf16[128,4,128]{2,1,0:T(4,128)(2,1)}), bf16[128,4,128]{2,1,0:T(4,128)(2,1)S(1)}, u32[]{:S(2)}, u32[]{:S(2)}) %all-to-all-start.1) | async-done | bytes 131104 | tf_op jit(solution)/shard_map/all_to_all | solution.py:471
  42.4 4.0 %footprints.1 = (f32[32,128]{1,0:T(8,128)}, bf16[512,128]{1,0:T(8,128)(2,1)}) custom-call(bf16[512,128]{1,0:T(8,128)(2,1)S(1)} %bitcast.10, bf16[512,128]{1,0:T(8,128)(2,1)S(1)} %get-tuple-element.42.placing_ref, f32[32,128]{1,0:T(8,128)S(1)} %get-tuple-element.43.seen_ref, bf16[12,4,128,128]{3,2,1,0:T(8,128)(2,1)S(1)} %get-tuple-element.44.near_ref, ...), custom_call_target="tpu_custom_call" | custom-call | flops 20000000 | bytes 5000000 | tf_op jit(solution)/shard_map/footprints/pallas_call | solution.py:553
  46.4 4.3 %all-to-all-start.2 = ((bf16[128,4,128]{2,1,0:T(4,128)(2,1)}), bf16[128,4,128]{2,1,0:T(4,128)(2,1)S(1)}, u32[]{:S(2)}, u32[]{:S(2)}) async-start(bf16[128,4,128]{2,1,0:T(4,128)(2,1)} %bitcast.6), calls=%async_computation.2 | async-start | bytes 262144 | tf_op jit(solution)/shard_map/all_to_all | solution.py:471
  50.7 4.3 %lower.1 = f32[32,64,128]{2,1,0:T(8,128)} custom-call(f32[32,64,128]{2,1,0:T(8,128)} %state_hbm.3, f32[64,128]{1,0:T(8,128)S(1)} %get-tuple-element.26.conduct_ref, bf16[272,128]{1,0:T(8,128)(2,1)S(1)} %collective-permute-done.a_ref, bf16[272,128]{1,0:T(8,128)(2,1)S(1)} %collective-permute-done.1.b_ref, ...), custom_call_target="tpu_custom_call", output_to_operand_aliasing={{}: (6, {})} | custom-call | flops 500000000 | bytes 3000000 | tf_op jit(solution)/shard_map/lower/pallas_call | solution.py:569
  55.0 5.6 %all-to-all-done.2 = bf16[128,4,128]{2,1,0:T(4,128)(2,1)S(1)} async-done(((bf16[128,4,128]{2,1,0:T(4,128)(2,1)}), bf16[128,4,128]{2,1,0:T(4,128)(2,1)S(1)}, u32[]{:S(2)}, u32[]{:S(2)}) %all-to-all-start.2) | async-done | bytes 131104 | tf_op jit(solution)/shard_map/all_to_all | solution.py:471
  60.6 0.8 %gradient.1 = f32[2,64,128]{2,1,0:T(8,128)} custom-call(bf16[512,128]{1,0:T(8,128)(2,1)S(1)} %bitcast.11, bf16[128,512]{1,0:T(8,128)(2,1)S(1)} %get-tuple-element.47.across_ref, f32[64,128]{1,0:T(8,128)S(1)} %get-tuple-element.48.adjoint_ref), custom_call_target="tpu_custom_call" | custom-call | flops 20000000 | bytes 400000 | tf_op jit(solution)/shard_map/gradient/pallas_call | solution.py:580
Async XLA Ops:
  2.6 13.4 %collective-permute-start = (bf16[272,128]{1,0:T(8,128)(2,1)S(1)}, bf16[272,128]{1,0:T(8,128)(2,1)S(1)}, u32[]{:S(2)}, u32[]{:S(2)}) collective-permute-start(bf16[272,128]{1,0:T(8,128)(2,1)S(1)} %get-tuple-element.27), channel_id=1, source_target_pairs={{0,8},{8,0},{16,24},{24,16},{32,40},{40,32},{48,56},{56,48},{64,72... | collective-permute-start | bytes 208904 | tf_op jit(solution)/shard_map/ppermute | solution.py:467
  5.1 10.9 %collective-permute-start.1 = (bf16[272,128]{1,0:T(8,128)(2,1)S(1)}, bf16[272,128]{1,0:T(8,128)(2,1)S(1)}, u32[]{:S(2)}, u32[]{:S(2)}) collective-permute-start(bf16[272,128]{1,0:T(8,128)(2,1)S(1)} %get-tuple-element.27), channel_id=1, source_target_pairs={{0,1},{120,121},{8,16},{16,8},{24,32},{32,24},{40,48},{48,40},{56,... | collective-permute-start | bytes 208904 | tf_op jit(solution)/shard_map/ppermute | solution.py:467
  6.1 19.9 %all-to-all-start = ((bf16[128,4,128]{2,1,0:T(4,128)(2,1)}), bf16[128,4,128]{2,1,0:T(4,128)(2,1)S(1)}, u32[]{:S(2)}, u32[]{:S(2)}) async-start(bf16[128,4,128]{2,1,0:T(4,128)(2,1)} %bitcast.2), calls=%async_computation | async-start | bytes 262144 | tf_op jit(solution)/shard_map/all_to_all | solution.py:471
  16.7 4.0 %collective-permute-start.2 = (bf16[144,128]{1,0:T(8,128)(2,1)S(1)}, bf16[144,128]{1,0:T(8,128)(2,1)S(1)}, u32[]{:S(2)}, u32[]{:S(2)}) collective-permute-start(bf16[144,128]{1,0:T(8,128)(2,1)S(1)} %get-tuple-element.33), channel_id=1, source_target_pairs={{0,1},{1,0},{2,3},{3,2},{4,5},{5,4},{6,7},{7,6},{8,9},{9,8},{10,11... | collective-permute-start | bytes 110600 | tf_op jit(solution)/shard_map/ppermute | solution.py:467
  17.8 3.7 %collective-permute-start.3 = (bf16[144,128]{1,0:T(8,128)(2,1)S(1)}, bf16[144,128]{1,0:T(8,128)(2,1)S(1)}, u32[]{:S(2)}, u32[]{:S(2)}) collective-permute-start(bf16[144,128]{1,0:T(8,128)(2,1)S(1)} %get-tuple-element.34), channel_id=1, source_target_pairs={{0,8},{7,15},{1,2},{2,1},{3,4},{4,3},{5,6},{6,5},{8,0},{15,7},{9,1... | collective-permute-start | bytes 110600 | tf_op jit(solution)/shard_map/ppermute | solution.py:467
  26.8 15.6 %all-to-all-start.1 = ((bf16[128,4,128]{2,1,0:T(4,128)(2,1)}), bf16[128,4,128]{2,1,0:T(4,128)(2,1)S(1)}, u32[]{:S(2)}, u32[]{:S(2)}) async-start(bf16[128,4,128]{2,1,0:T(4,128)(2,1)} %bitcast.4), calls=%async_computation.1 | async-start | bytes 262144 | tf_op jit(solution)/shard_map/all_to_all | solution.py:471
  46.4 14.3 %all-to-all-start.2 = ((bf16[128,4,128]{2,1,0:T(4,128)(2,1)}), bf16[128,4,128]{2,1,0:T(4,128)(2,1)S(1)}, u32[]{:S(2)}, u32[]{:S(2)}) async-start(bf16[128,4,128]{2,1,0:T(4,128)(2,1)} %bitcast.6), calls=%async_computation.2 | async-start | bytes 262144 | tf_op jit(solution)/shard_map/all_to_all | solution.py:471
